TPU v7x, 256 devices: a whole 4x4x8 slice. The times are simulated.
256 devices in a mesh: az: 16 (over y_lo, z), ax: 8 (over x, y_hi), rad: 2 (over core).
Axes of the slice: x: 4, y: 4 (y_hi: 2, y_lo: 2; y = y_hi * 2 + y_lo), z: 8, core: 2. Of those that a mesh axis runs over, the one named last changes fastest.
Arguments:
- source: float32 [3, 128, 32, 4096], P(None, 'ax', 'rad', 'az'), may hold values from -24 to 24
- region: int32 [128, 32, 4096], P('ax', 'rad', 'az'), may hold values from 0 to 3, as said below
- skew_shift: int32 [128], P('ax'), may hold values from 0 to 4095
Outputs:
- solution: float32 [3, 128, 32, 4096], P(None, 'ax', 'rad', 'az')
- residual: float32 [3, 128, 32, 4096], P(None, 'ax', 'rad', 'az')
- harmonics: float32 [2, 128, 16, 256], P(None, ('ax', 'az'), 'rad')
Inputs may be any that keep to these rules, and one draw needn't show every extreme that they name: `region`: 0 air, 1 iron, 2 magnet, 3 copper; the radial rows 8 to 23 are air.
All inputs are finite; a program needn't handle non-finite values.
Results may differ from a plain program's by a relative error of at most 0.0003.
Values sent between devices are 32-bit elements; how exact they have to be, the bound alone decides.
No kernel may reach another device: no remote copies, remote signals or barrier semaphores. Data moves between devices by JAX's collectives and lax.ppermute only.
A program may use at most 64 MiB of HBM per device.

v0:
```python
import math

import jax
import jax.numpy as jnp
from jax import lax
from jax.sharding import PartitionSpec as P

NA = 4096
MH = 256
GAP = 16


cheb_center = 7.1
cheb_radius = 6.9
ratio_sigma = cheb_center / cheb_radius
rho_first = 1.0 / ratio_sigma
rho_second = 1.0 / (2.0 * ratio_sigma - rho_first)
keep_weight = rho_second * rho_first
fresh_weight = 2.0 * rho_second / cheb_radius


def extended(array, sides, width, wrap):
    for axis, dim in sides:
        size, length = (lax.axis_size(axis), array.shape[dim])
        up = [(i, (i + 1) % size) for i in range(size if wrap else size - 1)]
        down = [(j, i) for i, j in up]
        last = lax.slice_in_dim(array, length - width, length, axis=dim)
        first = lax.slice_in_dim(array, 0, width, axis=dim)
        before = lax.ppermute(last, axis, up)
        after = lax.ppermute(first, axis, down)
        array = jnp.concatenate([before, array, after], axis=dim)
    return array


def materials(region):
    reluct = jnp.where(region == 1, 0.05, jnp.where(region == 2, 0.95, 1.0)).astype(jnp.float32)
    mass_term = jnp.where(
        region == 0, 0.2, jnp.where(region == 1, 1.5, jnp.where(region == 2, 0.6, 2.0))
    ).astype(jnp.float32)
    return (reluct, mass_term)


def forward_diff(field, dim_index):
    length = field.shape[dim_index]
    result = lax.slice_in_dim(field, 1, length, axis=dim_index) - lax.slice_in_dim(
        field, 0, length - 1, axis=dim_index
    )
    for other_dim in range(3):
        if other_dim != dim_index:
            result = lax.slice_in_dim(result, 0, result.shape[other_dim] - 1, axis=other_dim)
    return result


def backward_diff(field, dim_index):
    length = field.shape[dim_index]
    result = lax.slice_in_dim(field, 1, length, axis=dim_index) - lax.slice_in_dim(
        field, 0, length - 1, axis=dim_index
    )
    for other_dim in range(3):
        if other_dim != dim_index:
            result = lax.slice_in_dim(result, 1, result.shape[other_dim], axis=other_dim)
    return result


def curl_with(differ, parts):
    return jnp.stack(
        [
            differ(parts[2], 1) - differ(parts[1], 2),
            differ(parts[0], 2) - differ(parts[2], 0),
            differ(parts[1], 0) - differ(parts[0], 1),
        ]
    )


def apply_operator(field, coeff_ext):
    reluct = coeff_ext[0][:-1, :-1, :-1]
    flux_all = curl_with(forward_diff, field)
    strength = reluct[None] * flux_all
    image = (
        curl_with(backward_diff, strength)
        + coeff_ext[1][None, 1:-1, 1:-1, 1:-1] * field[:, 1:-1, 1:-1, 1:-1]
    )
    return (image, flux_all[:, 1:, 1:, 1:])


def extend(field, width):
    wrapped = extended(field, (("az", 3),), width, True)
    return extended(wrapped, (("ax", 1), ("rad", 2)), width, False)


def dft_basis(count):
    positions = jnp.arange(count, dtype=jnp.int32)
    phase_turns = positions[:, None] * jnp.arange(MH, dtype=jnp.int32)[None, :] % NA
    angle = phase_turns.astype(jnp.float32) * (2.0 * math.pi / NA)
    return jnp.concatenate([jnp.cos(angle), jnp.sin(angle)], axis=1) * (1.0 / math.sqrt(NA))


def rotate_phase(coeffs, shifts):
    phase_turns = jnp.arange(MH, dtype=jnp.int32)[None, :] * shifts[:, None] % NA
    angle = phase_turns.astype(jnp.float32) * (2.0 * math.pi / NA)
    cosine = jnp.cos(angle)[:, None, :]
    sine = jnp.sin(angle)[:, None, :]
    cos_part = coeffs[..., :MH]
    sin_part = coeffs[..., MH:]
    return jnp.stack([cosine * cos_part + sine * sin_part, sine * cos_part - cosine * sin_part])


def on_device(source, region, skew_shift):
    depth_z, depth_r, depth_a = region.shape
    first_step = source / cheb_center
    reluct, mass_term = materials(region)
    coeff_ext = extend(jnp.stack([reluct, mass_term]), 1)
    first_ext = extend(first_step, 1)
    first_image, first_flux = apply_operator(first_ext, coeff_ext)
    resid_one = source - first_image
    second_step = keep_weight * first_step + fresh_weight * resid_one
    second_image, second_flux = apply_operator(extend(second_step, 1), coeff_ext)
    solution = first_step + second_step
    residual = resid_one - second_image
    flux = first_flux + second_flux
    half_gap = GAP // 2
    first_row = (1 - lax.axis_index("rad")) * (depth_r - half_gap)
    gap_band = lax.dynamic_slice_in_dim(flux, first_row, half_gap, axis=2)
    stress = 0.5 * (gap_band[1] * gap_band[1] - gap_band[2] * gap_band[2])
    rows_here = depth_z // lax.axis_size("az")
    local_shift = lax.dynamic_slice_in_dim(skew_shift, lax.axis_index("az") * rows_here, rows_here)
    block = lax.all_to_all(stress, "az", split_axis=0, concat_axis=2, tiled=True)
    slab_rows, item_count, circle_length = block.shape
    product = jnp.dot(
        block.reshape(slab_rows * item_count, circle_length),
        dft_basis(circle_length),
        precision=lax.Precision.HIGHEST,
        preferred_element_type=jnp.float32,
    )
    harmonics = rotate_phase(product.reshape(slab_rows, item_count, 2 * MH), local_shift)
    return (solution, residual, harmonics)


def solution(mesh):
    in_specs = (P(None, "ax", "rad", "az"), P("ax", "rad", "az"), P("ax"))
    out_specs = (
        P(None, "ax", "rad", "az"),
        P(None, "ax", "rad", "az"),
        P(None, ("ax", "az"), "rad", None),
    )
    return jax.shard_map(
        on_device, mesh=mesh, in_specs=in_specs, out_specs=out_specs, check_vma=False
    )
```

profile of v0, /device:TPU:5, one launch (start us, length us, event | category | flops | bytes accessed | tf_op | source)
XLA Modules:
  0.0 132.0 jit_solution(4955163214592274134)
XLA Ops:
  1.9 1.7 %collective-permute-start = (f32[2,16,16,1]{3,2,1,0:T(8,128)S(1)}, f32[2,16,16,1]{3,2,1,0:T(8,128)S(1)}, u32[]{:S(2)}, u32[]{:S(2)}) collective-permute-start(f32[2,16,16,1]{3,2,1,0:T(8,128)S(1)} %get-tuple-element.87), channel_id=1, source_target_pairs={{0,16},{16,32},{32,48},{48,64},{64,80},{80,96},{96,112},{112,128},... | collective-permute-start | bytes 6152 | tf_op jit(solution)/shard_map/ppermute | solution.py:29
  3.6 5.0 %collective-permute-start.1 = (f32[2,16,16,1]{3,2,1,0:T(8,128)S(1)}, f32[2,16,16,1]{3,2,1,0:T(8,128)S(1)}, u32[]{:S(2)}, u32[]{:S(2)}) collective-permute-start(f32[2,16,16,1]{3,2,1,0:T(8,128)S(1)} %get-tuple-element.88), channel_id=1, source_target_pairs={{16,0},{32,16},{48,32},{64,48},{80,64},{96,80},{112,96},{128,112},... | collective-permute-start | bytes 6152 | tf_op jit(solution)/shard_map/ppermute | solution.py:30
  9.4 3.6 %collective-permute-start.7 = (f32[3,16,16,1]{3,1,2,0:T(8,128)S(1)}, f32[3,16,16,1]{3,1,2,0:T(8,128)S(1)}, u32[]{:S(2)}, u32[]{:S(2)}) collective-permute-start(f32[3,16,16,1]{3,1,2,0:T(8,128)S(1)} %get-tuple-element.52), channel_id=1, source_target_pairs={{16,0},{32,16},{48,32},{64,48},{80,64},{96,80},{112,96},{128,112},... | collective-permute-start | bytes 9224 | tf_op jit(solution)/shard_map/ppermute | solution.py:30
  13.0 1.6 %collective-permute-done = f32[2,16,16,1]{3,2,1,0:T(8,128)S(1)} collective-permute-done((f32[2,16,16,1]{3,2,1,0:T(8,128)S(1)}, f32[2,16,16,1]{3,2,1,0:T(8,128)S(1)}, u32[]{:S(2)}, u32[]{:S(2)}) %collective-permute-start) | collective-permute-done | bytes 2080 | tf_op jit(solution)/shard_map/ppermute | solution.py:29
  14.7 4.5 %collective-permute-start.2 = (f32[2,1,16,258]{3,2,1,0:T(8,128)S(1)}, f32[2,1,16,258]{3,2,1,0:T(8,128)S(1)}, u32[]{:S(2)}, u32[]{:S(2)}) collective-permute-start(f32[2,1,16,258]{3,2,1,0:T(8,128)S(1)} %get-tuple-element.47), channel_id=1, source_target_pairs={{0,2},{2,4},{4,6},{6,8},{8,10},{10,12},{12,14},{1,3},{3,5},{5,7},{... | collective-permute-start | bytes 99080 | tf_op jit(solution)/shard_map/ppermute | solution.py:29
  19.2 3.2 %collective-permute-start.3 = (f32[2,1,16,258]{3,2,1,0:T(8,128)S(1)}, f32[2,1,16,258]{3,2,1,0:T(8,128)S(1)}, u32[]{:S(2)}, u32[]{:S(2)}) collective-permute-start(f32[2,1,16,258]{3,2,1,0:T(8,128)S(1)} %get-tuple-element.48), channel_id=1, source_target_pairs={{2,0},{4,2},{6,4},{8,6},{10,8},{12,10},{14,12},{3,1},{5,3},{7,5},{... | collective-permute-start | bytes 99080 | tf_op jit(solution)/shard_map/ppermute | solution.py:30
  23.5 5.4 %collective-permute-start.8 = (f32[3,1,16,258]{3,1,2,0:T(1,128)S(1)}, f32[3,1,16,258]{3,1,2,0:T(1,128)S(1)}, u32[]{:S(2)}, u32[]{:S(2)}) collective-permute-start(f32[3,1,16,258]{3,1,2,0:T(1,128)S(1)} %get-tuple-element.41), channel_id=1, source_target_pairs={{0,2},{2,4},{4,6},{6,8},{8,10},{10,12},{12,14},{1,3},{3,5},{5,7},{... | collective-permute-start | bytes 148616 | tf_op jit(solution)/shard_map/ppermute | solution.py:29
  28.9 2.3 %collective-permute-start.9 = (f32[3,1,16,258]{3,1,2,0:T(1,128)S(1)}, f32[3,1,16,258]{3,1,2,0:T(1,128)S(1)}, u32[]{:S(2)}, u32[]{:S(2)}) collective-permute-start(f32[3,1,16,258]{3,1,2,0:T(1,128)S(1)} %get-tuple-element.42), channel_id=1, source_target_pairs={{2,0},{4,2},{6,4},{8,6},{10,8},{12,10},{14,12},{3,1},{5,3},{7,5},{... | collective-permute-start | bytes 148616 | tf_op jit(solution)/shard_map/ppermute | solution.py:30
  32.9 4.5 %collective-permute-start.5 = (f32[2,18,1,258]{3,2,1,0:T(1,128)S(1)}, f32[2,18,1,258]{3,2,1,0:T(1,128)S(1)}, u32[]{:S(2)}, u32[]{:S(2)}) collective-permute-start(f32[2,18,1,258]{3,2,1,0:T(1,128)S(1)} %get-tuple-element.46), channel_id=1, source_target_pairs={{1,0},{3,2},{5,4},{7,6},{9,8},{11,10},{13,12},{15,14},{17,16},{19,... | collective-permute-start | bytes 111464 | tf_op jit(solution)/shard_map/ppermute | solution.py:30
  38.8 3.0 %collective-permute-start.11 = (f32[3,18,1,258]{3,1,2,0:T(8,128)S(1)}, f32[3,18,1,258]{3,1,2,0:T(8,128)S(1)}, u32[]{:S(2)}, u32[]{:S(2)}) collective-permute-start(f32[3,18,1,258]{3,1,2,0:T(8,128)S(1)} %get-tuple-element.38), channel_id=1, source_target_pairs={{1,0},{3,2},{5,4},{7,6},{9,8},{11,10},{13,12},{15,14},{17,16},{19,... | collective-permute-start | bytes 167192 | tf_op jit(solution)/shard_map/ppermute | solution.py:30
  48.8 1.5 %fusion.54 = (f32[3,16,16,256]{3,1,2,0:T(8,128)}, f32[3,16,16,256]{3,1,2,0:T(8,128)S(1)}) fusion(f32[3,16,16,256]{3,2,1,0:T(8,128)S(1)} %copy-done, f32[16,16,256]{2,0,1:T(8,128)S(1)} %copy.18, f32[1,16,16,256]{3,1,2,0:T(8,128)S(1)} %fusion.40, f32[1,16,16,256]{3,1,2,0:T(8,128)S(1)} %fusion.41, f32[1,16,16,256]{3,1,2,0:T(8,128)S(1)} %fusion.43), kind=kLoop, calls=%fused_computation.154 | loop fusion | flops 1966080 | bytes 3407872 | tf_op jit(solution)/shard_map/add | solution.py:118
  50.6 4.2 %collective-permute-start.13 = (f32[3,16,16,1]{3,1,2,0:T(8,128)S(1)}, f32[3,16,16,1]{3,1,2,0:T(8,128)S(1)}, u32[]{:S(2)}, u32[]{:S(2)}) collective-permute-start(f32[3,16,16,1]{3,1,2,0:T(8,128)S(1)} %get-tuple-element.50), channel_id=1, source_target_pairs={{16,0},{32,16},{48,32},{64,48},{80,64},{96,80},{112,96},{128,112},... | collective-permute-start | bytes 9224 | tf_op jit(solution)/shard_map/ppermute | solution.py:30
  54.8 8.8 %collective-permute-done.12 = f32[3,16,16,1]{3,1,2,0:T(8,128)S(1)} collective-permute-done((f32[3,16,16,1]{3,1,2,0:T(8,128)S(1)}, f32[3,16,16,1]{3,1,2,0:T(8,128)S(1)}, u32[]{:S(2)}, u32[]{:S(2)}) %collective-permute-start.12) | collective-permute-done | bytes 3104 | tf_op jit(solution)/shard_map/ppermute | solution.py:29
  64.8 4.0 %collective-permute-start.14 = (f32[3,1,16,258]{3,1,2,0:T(1,128)}, f32[3,1,16,258]{3,1,2,0:T(1,128)}, u32[]{:S(2)}, u32[]{:S(2)}) collective-permute-start(f32[3,1,16,258]{3,1,2,0:T(1,128)} %get-tuple-element.39), channel_id=1, source_target_pairs={{0,2},{2,4},{4,6},{6,8},{8,10},{10,12},{12,14},{1,3},{3,5},{5,7},{... | collective-permute-start | bytes 148616 | tf_op jit(solution)/shard_map/ppermute | solution.py:29
  68.8 3.7 %collective-permute-start.15 = (f32[3,1,16,258]{3,1,2,0:T(1,128)}, f32[3,1,16,258]{3,1,2,0:T(1,128)}, u32[]{:S(2)}, u32[]{:S(2)}) collective-permute-start(f32[3,1,16,258]{3,1,2,0:T(1,128)} %get-tuple-element.40), channel_id=1, source_target_pairs={{2,0},{4,2},{6,4},{8,6},{10,8},{12,10},{14,12},{3,1},{5,3},{7,5},{... | collective-permute-start | bytes 148616 | tf_op jit(solution)/shard_map/ppermute | solution.py:30
  72.6 17.6 %fusion.10 = (f32[4096,256]{1,0:T(8,128)}, f32[4096,256]{1,0:T(8,128)}) fusion(), kind=kLoop, calls=%fused_computation.14 | loop fusion | flops 14680064 | bytes 8388608 | tf_op jit(solution)/shard_map/sin | solution.py:95
  90.7 1.6 %pad_maximum_fusion.10 = (f32[3,18,1,258]{3,1,2,0:T(8,128)}, f32[3,18,1,258]{3,1,2,0:T(8,128)}) fusion(f32[3,1,16,258]{3,1,2,0:T(1,128)} %collective-permute-done.15, f32[3,1,16,258]{3,1,2,0:T(1,128)} %collective-permute-done.14, f32[3,16,16,1]{3,1,2,0:T(8,128)S(1)} %collective-permute-done.13, f32[3,16,16,256]{3,1,2,0:T(8,128)S(1)} %get-tuple-element.10, ...), kind=kLoop, calls=%fused_computation.119 | loop fusion | flops 111456 | bytes 1003104 | tf_op jit(solution)/shard_map/slice | solution.py:27
  93.6 4.3 %collective-permute-start.17 = (f32[3,18,1,258]{3,1,2,0:T(8,128)}, f32[3,18,1,258]{3,1,2,0:T(8,128)}, u32[]{:S(2)}, u32[]{:S(2)}) collective-permute-start(f32[3,18,1,258]{3,1,2,0:T(8,128)} %get-tuple-element.36), channel_id=1, source_target_pairs={{1,0},{3,2},{5,4},{7,6},{9,8},{11,10},{13,12},{15,14},{17,16},{19,... | collective-permute-start | bytes 167192 | tf_op jit(solution)/shard_map/ppermute | solution.py:30
  98.6 1.9 %copy.21 = f32[16,16,256]{2,0,1:T(8,128)} copy(f32[16,16,256]{2,1,0:T(8,128)} %get-tuple-element.53) | data formatting | bytes 524288 | tf_op jit(solution)/shard_map/slice | solution.py:81
  100.5 1.8 %slice.656 = f32[3,16,16,256]{3,1,2,0:T(8,128)S(1)} slice(f32[3,17,17,257]{3,1,2,0:T(8,128)} %get-tuple-element.21), slice={[0:3], [1:17], [1:17], [1:257]} | slice | bytes 1572864 | tf_op jit(solution)/shard_map/slice | solution.py:83
  103.6 1.8 %pad_maximum_fusion.1 = f32[3,18,18,258]{3,1,2,0:T(8,128)S(1)} fusion(f32[3,18,1,258]{3,1,2,0:T(8,128)} %collective-permute-done.17, f32[3,1,16,258]{3,1,2,0:T(1,128)} %collective-permute-done.15, f32[3,16,16,1]{3,1,2,0:T(8,128)S(1)} %collective-permute-done.13, f32[3,16,16,256]{3,1,2,0:T(8,128)S(1)} %get-tuple-element.10, ...), kind=kLoop, calls=%fused_computation.17 | loop fusion | flops 1504656 | bytes 2006208 | tf_op jit(solution)/shard_map/concatenate | solution.py:31
  111.4 5.6 %all-to-all-start = ((f32[16,8,256]{2,1,0:T(8,128)}), f32[16,8,256]{2,1,0:T(8,128)S(1)}, u32[]{:S(2)}, u32[]{:S(2)}) async-start(f32[16,8,256]{2,1,0:T(8,128)} %copy.22), calls=%async_computation | async-start | bytes 262144 | tf_op jit(solution)/shard_map/all_to_all | solution.py:127
  122.4 2.5 %all-to-all-done = f32[16,8,256]{2,1,0:T(8,128)S(1)} async-done(((f32[16,8,256]{2,1,0:T(8,128)}), f32[16,8,256]{2,1,0:T(8,128)S(1)}, u32[]{:S(2)}, u32[]{:S(2)}) %all-to-all-start) | async-done | bytes 131104 | tf_op jit(solution)/shard_map/all_to_all | solution.py:127
  124.8 6.5 %fusion.12 = f32[1,8,512]{2,1,0:T(8,128)S(1)} fusion(f32[8,4096]{1,0:T(8,128)S(1)} %bitcast.87, f32[4096,256]{1,0:T(8,128)} %get-tuple-element.97, f32[4096,256]{1,0:T(8,128)} %get-tuple-element.98), kind=kOutput, calls=%fused_computation.21 | convolution fusion | flops 205520896 | bytes 8536064 | tf_op jit(solution)/shard_map/dot_general | solution.py:129
  (109 shorter events, 30.3 us)
Async XLA Ops:
  0.6 8.0 %copy-start = (f32[3,16,16,256]{3,2,1,0:T(8,128)S(1)}, f32[3,16,16,256]{3,2,1,0:T(8,128)}, u32[]{:S(2)}) copy-start(f32[3,16,16,256]{3,2,1,0:T(8,128)} %param.3) | copy-start | bytes 2359300
  1.9 12.7 %collective-permute-start = (f32[2,16,16,1]{3,2,1,0:T(8,128)S(1)}, f32[2,16,16,1]{3,2,1,0:T(8,128)S(1)}, u32[]{:S(2)}, u32[]{:S(2)}) collective-permute-start(f32[2,16,16,1]{3,2,1,0:T(8,128)S(1)} %get-tuple-element.87), channel_id=1, source_target_pairs={{0,16},{16,32},{32,48},{48,64},{64,80},{80,96},{96,112},{112,128},... | collective-permute-start | bytes 6152 | tf_op jit(solution)/shard_map/ppermute | solution.py:29
  3.6 11.0 %collective-permute-start.1 = (f32[2,16,16,1]{3,2,1,0:T(8,128)S(1)}, f32[2,16,16,1]{3,2,1,0:T(8,128)S(1)}, u32[]{:S(2)}, u32[]{:S(2)}) collective-permute-start(f32[2,16,16,1]{3,2,1,0:T(8,128)S(1)} %get-tuple-element.88), channel_id=1, source_target_pairs={{16,0},{32,16},{48,32},{64,48},{80,64},{96,80},{112,96},{128,112},... | collective-permute-start | bytes 6152 | tf_op jit(solution)/shard_map/ppermute | solution.py:30
  9.3 13.7 %collective-permute-start.6 = (f32[3,16,16,1]{3,1,2,0:T(8,128)S(1)}, f32[3,16,16,1]{3,1,2,0:T(8,128)S(1)}, u32[]{:S(2)}, u32[]{:S(2)}) collective-permute-start(f32[3,16,16,1]{3,1,2,0:T(8,128)S(1)} %get-tuple-element.51), channel_id=1, source_target_pairs={{0,16},{16,32},{32,48},{48,64},{64,80},{80,96},{96,112},{112,128},... | collective-permute-start | bytes 9224 | tf_op jit(solution)/shard_map/ppermute | solution.py:29
  9.4 13.6 %collective-permute-start.7 = (f32[3,16,16,1]{3,1,2,0:T(8,128)S(1)}, f32[3,16,16,1]{3,1,2,0:T(8,128)S(1)}, u32[]{:S(2)}, u32[]{:S(2)}) collective-permute-start(f32[3,16,16,1]{3,1,2,0:T(8,128)S(1)} %get-tuple-element.52), channel_id=1, source_target_pairs={{16,0},{32,16},{48,32},{64,48},{80,64},{96,80},{112,96},{128,112},... | collective-permute-start | bytes 9224 | tf_op jit(solution)/shard_map/ppermute | solution.py:30
  14.7 16.5 %collective-permute-start.2 = (f32[2,1,16,258]{3,2,1,0:T(8,128)S(1)}, f32[2,1,16,258]{3,2,1,0:T(8,128)S(1)}, u32[]{:S(2)}, u32[]{:S(2)}) collective-permute-start(f32[2,1,16,258]{3,2,1,0:T(8,128)S(1)} %get-tuple-element.47), channel_id=1, source_target_pairs={{0,2},{2,4},{4,6},{6,8},{8,10},{10,12},{12,14},{1,3},{3,5},{5,7},{... | collective-permute-start | bytes 99080 | tf_op jit(solution)/shard_map/ppermute | solution.py:29
  19.2 12.0 %collective-permute-start.3 = (f32[2,1,16,258]{3,2,1,0:T(8,128)S(1)}, f32[2,1,16,258]{3,2,1,0:T(8,128)S(1)}, u32[]{:S(2)}, u32[]{:S(2)}) collective-permute-start(f32[2,1,16,258]{3,2,1,0:T(8,128)S(1)} %get-tuple-element.48), channel_id=1, source_target_pairs={{2,0},{4,2},{6,4},{8,6},{10,8},{12,10},{14,12},{3,1},{5,3},{7,5},{... | collective-permute-start | bytes 99080 | tf_op jit(solution)/shard_map/ppermute | solution.py:30
  23.5 13.9 %collective-permute-start.8 = (f32[3,1,16,258]{3,1,2,0:T(1,128)S(1)}, f32[3,1,16,258]{3,1,2,0:T(1,128)S(1)}, u32[]{:S(2)}, u32[]{:S(2)}) collective-permute-start(f32[3,1,16,258]{3,1,2,0:T(1,128)S(1)} %get-tuple-element.41), channel_id=1, source_target_pairs={{0,2},{2,4},{4,6},{6,8},{8,10},{10,12},{12,14},{1,3},{3,5},{5,7},{... | collective-permute-start | bytes 148616 | tf_op jit(solution)/shard_map/ppermute | solution.py:29
  28.9 8.5 %collective-permute-start.9 = (f32[3,1,16,258]{3,1,2,0:T(1,128)S(1)}, f32[3,1,16,258]{3,1,2,0:T(1,128)S(1)}, u32[]{:S(2)}, u32[]{:S(2)}) collective-permute-start(f32[3,1,16,258]{3,1,2,0:T(1,128)S(1)} %get-tuple-element.42), channel_id=1, source_target_pairs={{2,0},{4,2},{6,4},{8,6},{10,8},{12,10},{14,12},{3,1},{5,3},{7,5},{... | collective-permute-start | bytes 148616 | tf_op jit(solution)/shard_map/ppermute | solution.py:30
  31.6 10.3 %collective-permute-start.4 = (f32[2,18,1,258]{3,2,1,0:T(1,128)S(1)}, f32[2,18,1,258]{3,2,1,0:T(1,128)S(1)}, u32[]{:S(2)}, u32[]{:S(2)}) collective-permute-start(f32[2,18,1,258]{3,2,1,0:T(1,128)S(1)} %get-tuple-element.45), channel_id=1, source_target_pairs={{0,1},{2,3},{4,5},{6,7},{8,9},{10,11},{12,13},{14,15},{16,17},{18,... | collective-permute-start | bytes 111464 | tf_op jit(solution)/shard_map/ppermute | solution.py:29
  32.9 9.0 %collective-permute-start.5 = (f32[2,18,1,258]{3,2,1,0:T(1,128)S(1)}, f32[2,18,1,258]{3,2,1,0:T(1,128)S(1)}, u32[]{:S(2)}, u32[]{:S(2)}) collective-permute-start(f32[2,18,1,258]{3,2,1,0:T(1,128)S(1)} %get-tuple-element.46), channel_id=1, source_target_pairs={{1,0},{3,2},{5,4},{7,6},{9,8},{11,10},{13,12},{15,14},{17,16},{19,... | collective-permute-start | bytes 111464 | tf_op jit(solution)/shard_map/ppermute | solution.py:30
  37.5 6.1 %collective-permute-start.10 = (f32[3,18,1,258]{3,1,2,0:T(8,128)S(1)}, f32[3,18,1,258]{3,1,2,0:T(8,128)S(1)}, u32[]{:S(2)}, u32[]{:S(2)}) collective-permute-start(f32[3,18,1,258]{3,1,2,0:T(8,128)S(1)} %get-tuple-element.37), channel_id=1, source_target_pairs={{0,1},{2,3},{4,5},{6,7},{8,9},{10,11},{12,13},{14,15},{16,17},{18,... | collective-permute-start | bytes 167192 | tf_op jit(solution)/shard_map/ppermute | solution.py:29
  38.8 4.9 %collective-permute-start.11 = (f32[3,18,1,258]{3,1,2,0:T(8,128)S(1)}, f32[3,18,1,258]{3,1,2,0:T(8,128)S(1)}, u32[]{:S(2)}, u32[]{:S(2)}) collective-permute-start(f32[3,18,1,258]{3,1,2,0:T(8,128)S(1)} %get-tuple-element.38), channel_id=1, source_target_pairs={{1,0},{3,2},{5,4},{7,6},{9,8},{11,10},{13,12},{15,14},{17,16},{19,... | collective-permute-start | bytes 167192 | tf_op jit(solution)/shard_map/ppermute | solution.py:30
  50.5 13.1 %collective-permute-start.12 = (f32[3,16,16,1]{3,1,2,0:T(8,128)S(1)}, f32[3,16,16,1]{3,1,2,0:T(8,128)S(1)}, u32[]{:S(2)}, u32[]{:S(2)}) collective-permute-start(f32[3,16,16,1]{3,1,2,0:T(8,128)S(1)} %get-tuple-element.49), channel_id=1, source_target_pairs={{0,16},{16,32},{32,48},{48,64},{64,80},{80,96},{96,112},{112,128},... | collective-permute-start | bytes 9224 | tf_op jit(solution)/shard_map/ppermute | solution.py:29
  50.6 13.2 %collective-permute-start.13 = (f32[3,16,16,1]{3,1,2,0:T(8,128)S(1)}, f32[3,16,16,1]{3,1,2,0:T(8,128)S(1)}, u32[]{:S(2)}, u32[]{:S(2)}) collective-permute-start(f32[3,16,16,1]{3,1,2,0:T(8,128)S(1)} %get-tuple-element.50), channel_id=1, source_target_pairs={{16,0},{32,16},{48,32},{64,48},{80,64},{96,80},{112,96},{128,112},... | collective-permute-start | bytes 9224 | tf_op jit(solution)/shard_map/ppermute | solution.py:30
  64.8 25.9 %collective-permute-start.14 = (f32[3,1,16,258]{3,1,2,0:T(1,128)}, f32[3,1,16,258]{3,1,2,0:T(1,128)}, u32[]{:S(2)}, u32[]{:S(2)}) collective-permute-start(f32[3,1,16,258]{3,1,2,0:T(1,128)} %get-tuple-element.39), channel_id=1, source_target_pairs={{0,2},{2,4},{4,6},{6,8},{8,10},{10,12},{12,14},{1,3},{3,5},{5,7},{... | collective-permute-start | bytes 148616 | tf_op jit(solution)/shard_map/ppermute | solution.py:29
  68.8 21.3 %copy-start.11 = (s32[16]{0:T(128)S(1)}, s32[16]{0:T(128)}, u32[]{:S(2)}) copy-start(s32[16]{0:T(128)} %param.5) | copy-start | bytes 196
  68.8 21.9 %collective-permute-start.15 = (f32[3,1,16,258]{3,1,2,0:T(1,128)}, f32[3,1,16,258]{3,1,2,0:T(1,128)}, u32[]{:S(2)}, u32[]{:S(2)}) collective-permute-start(f32[3,1,16,258]{3,1,2,0:T(1,128)} %get-tuple-element.40), channel_id=1, source_target_pairs={{2,0},{4,2},{6,4},{8,6},{10,8},{12,10},{14,12},{3,1},{5,3},{7,5},{... | collective-permute-start | bytes 148616 | tf_op jit(solution)/shard_map/ppermute | solution.py:30
  92.3 11.3 %collective-permute-start.16 = (f32[3,18,1,258]{3,1,2,0:T(8,128)}, f32[3,18,1,258]{3,1,2,0:T(8,128)}, u32[]{:S(2)}, u32[]{:S(2)}) collective-permute-start(f32[3,18,1,258]{3,1,2,0:T(8,128)} %get-tuple-element.35), channel_id=1, source_target_pairs={{0,1},{2,3},{4,5},{6,7},{8,9},{10,11},{12,13},{14,15},{16,17},{18,... | collective-permute-start | bytes 167192 | tf_op jit(solution)/shard_map/ppermute | solution.py:29
  93.6 10.0 %collective-permute-start.17 = (f32[3,18,1,258]{3,1,2,0:T(8,128)}, f32[3,18,1,258]{3,1,2,0:T(8,128)}, u32[]{:S(2)}, u32[]{:S(2)}) collective-permute-start(f32[3,18,1,258]{3,1,2,0:T(8,128)} %get-tuple-element.36), channel_id=1, source_target_pairs={{1,0},{3,2},{5,4},{7,6},{9,8},{11,10},{13,12},{15,14},{17,16},{19,... | collective-permute-start | bytes 167192 | tf_op jit(solution)/shard_map/ppermute | solution.py:30
  98.6 3.7 %copy-start.1 = (f32[3,16,16,256]{3,1,2,0:T(8,128)S(1)}, f32[3,16,16,256]{3,1,2,0:T(8,128)}, u32[]{:S(2)}) copy-start(f32[3,16,16,256]{3,1,2,0:T(8,128)} %get-tuple-element.9) | copy-start | bytes 2359300
  111.4 13.4 %all-to-all-start = ((f32[16,8,256]{2,1,0:T(8,128)}), f32[16,8,256]{2,1,0:T(8,128)S(1)}, u32[]{:S(2)}, u32[]{:S(2)}) async-start(f32[16,8,256]{2,1,0:T(8,128)} %copy.22), calls=%async_computation | async-start | bytes 262144 | tf_op jit(solution)/shard_map/all_to_all | solution.py:127
  117.4 2.9 %copy-start.5 = (f32[1,16,16,256]{3,1,2,0:T(8,128)S(1)}, f32[1,16,16,256]{3,1,2,0:T(8,128)}, u32[]{:S(2)}) copy-start(f32[1,16,16,256]{3,1,2,0:T(8,128)} %copy-done.4) | copy-start | bytes 786436
  117.4 2.9 %copy-start.10 = (f32[16,16,256]{2,0,1:T(8,128)S(1)}, f32[16,16,256]{2,0,1:T(8,128)}, u32[]{:S(2)}) copy-start(f32[16,16,256]{2,0,1:T(8,128)} %copy.21) | copy-start | bytes 786436
  (7 other events, 11.6 us)
where the time goes:
time: 133 us; the launch traced here: 132 us
  starting transfers between devices  59.1 us (44%)
  other arithmetic  37.2 us (28%)
  local copies, waits for them, and re-layouts  14.3 us (11%)
  waiting for transfers between devices  13.7 us (10%)
  matrix products  6.54 us (5%)
    ppermute x9, starting transfers between devices, extended(): after = lax.ppermute(first, axis, down)  33.8 us
    ppermute x9, starting transfers between devices, extended(): before = lax.ppermute(last, axis, up)  19.6 us
    sin x1, other arithmetic, dft_basis(): jnp.sin(angle)  17.6 us
    ppermute x9, waiting for transfers between devices, extended(): before = lax.ppermute(last, axis, up)  11 us
    dot_general x1, matrix products, on_device(): jnp.dot(block.reshape(slab_rows * item_count, circle_length), dft_basis(c...  6.54 us
    all_to_all x1, starting transfers between devices, on_device(): lax.all_to_all(stress, 'az', split_axis=0, concat_axis=2, tiled=True)  5.61 us
    another operation x14, other arithmetic, curl_with(): jnp.stack([differ(parts[2], 1) - differ(parts[1], 2), differ(parts[0], 2)...  5.25 us
    slice x6, other arithmetic, extended(): last = lax.slice_in_dim(array, length - width, length, axis=dim)  3.77 us
  transfers between devices with their start and end apart: 19, of which 5 were waited for; matrix products, arithmetic and copies ran while one was open for 24% of the time, Pallas kernels for 0%

commit v1 on v0

v1 whole, which is shorter than its diff:
```python
import functools
import math

import jax
import jax.numpy as jnp
import numpy as np
from jax import lax
from jax.experimental import pallas as pl
from jax.experimental.pallas import tpu as pltpu
from jax.sharding import PartitionSpec as P

NA = 4096
MH = 256
F32 = jnp.float32

cheb_center = 7.1
cheb_radius = 6.9
ratio_sigma = cheb_center / cheb_radius
rho_first = 1.0 / ratio_sigma
rho_second = 1.0 / (2.0 * ratio_sigma - rho_first)
keep_weight = rho_second * rho_first
fresh_weight = 2.0 * rho_second / cheb_radius

FIRST = 1.0 / cheb_center
SECOND_SRC = keep_weight / cheb_center + fresh_weight
SECOND_A = fresh_weight / cheb_center
SUM_SRC = FIRST + SECOND_SRC

VMEM = pl.BlockSpec(memory_space=pltpu.VMEM)
SMEM = pl.BlockSpec(memory_space=pltpu.SMEM)


def materials(code):
    iron, magnet, outside = code == 1.0, code == 2.0, code < 0.0
    reluct = jnp.where(iron, 0.05, jnp.where(magnet, 0.95, jnp.where(outside, 0.0, 1.0)))
    mass = jnp.where(
        iron,
        1.5,
        jnp.where(magnet, 0.6, jnp.where(outside, 0.0, jnp.where(code == 0.0, 0.2, 2.0))),
    )
    return reluct.astype(F32), mass.astype(F32)


def roll(x, shift, axis):
    return pltpu.roll(x, shift % x.shape[axis], axis)


def from_partner(shape, core):
    sub = lax.broadcasted_iota(jnp.int32, shape, len(shape) - 2)
    return (jnp.where(sub < 4, 1, 0) + core) == 1


def curl(v0, v1, v2, v0a, v1a, v0r, v2r, v1n, v2n):
    return (
        (v2r - v2) - (v1a - v1),
        (v0a - v0) - (v2n - v2),
        (v1n - v1) - (v0r - v0),
    )


def stress_kernel(info, src, reg, sw1, up, dn, sw2, out, v, g, u, hs):
    core, lo, hi = info[0], info[1].astype(F32), info[2].astype(F32)
    gap = pl.ds(pl.multiple_of(8 * (1 - core), 8), 8)
    other = pl.ds(pl.multiple_of(8 * core, 8), 8)
    pick3 = from_partner((16, 8, 256), core)
    pick = from_partner((8, 256), core)
    for c in range(3):
        v[c, 2:18, 0:8, :] = src[c, :, gap, :]
        v[c, 2:18, 8:16, :] = jnp.where(pick3, sw1[c], src[c, :, other, :])
        v[c, 1, 0:8, :] = up[c, 1, gap, :] * lo
        v[c, 1, 8:16, :] = jnp.where(pick, sw2[2 * c + 1], up[c, 1, other, :]) * lo
        v[c, 18, 0:8, :] = dn[c, gap, :] * hi
        v[c, 18, 8:16, :] = jnp.where(pick, sw2[8 + c], dn[c, other, :]) * hi
        if c > 0:
            v[c, 19, 0:8, :] = dn[3 + c, gap, :] * hi
            v[c, 19, 8:16, :] = jnp.where(pick, sw2[11 + c], dn[3 + c, other, :]) * hi
    g[2:18, 0:8, :] = reg[:, gap, :].astype(F32)
    g[2:18, 8:16, :] = jnp.where(pick3, sw1[3], reg[:, other, :].astype(F32))
    g[1, 0:8, :] = (up[3, 1, gap, :] + 1.0) * lo - 1.0
    g[1, 8:16, :] = (jnp.where(pick, sw2[7], up[3, 1, other, :]) + 1.0) * lo - 1.0
    g[18, 0:8, :] = (dn[3, gap, :] + 1.0) * hi - 1.0
    g[18, 8:16, :] = (jnp.where(pick, sw2[11], dn[3, other, :]) + 1.0) * hi - 1.0

    lane = lax.broadcasted_iota(jnp.int32, (16, 256), 1)
    last_lane, first_lane = lane == 255, lane == 0

    def after(x):
        return jnp.where(last_lane, 0.0, roll(x, -1, 1))

    def before(x):
        return jnp.where(first_lane, 0.0, roll(x, 1, 1))

    def strength(i):
        v0, v1, v2 = v[0, i], v[1, i], v[2, i]
        reluct, mass = materials(g[i])
        c0, c1, c2 = curl(
            v0, v1, v2, after(v0), after(v1), roll(v0, -1, 0), roll(v2, -1, 0), v[1, i + 1], v[2, i + 1]
        )
        return (v0, v1, v2), (reluct * c0, reluct * c1, reluct * c2), mass

    _, (_, h1_first, h2_first), _ = strength(1)

    def first_pass(i, carry):
        h1_prev, h2_prev = carry
        (v0, v1, v2), (h0, h1, h2), mass = strength(i)
        a0 = (h2 - roll(h2, 1, 0)) - (h1 - before(h1)) + mass * v0
        a1 = (h0 - before(h0)) - (h2 - h2_prev) + mass * v1
        a2 = (h1 - h1_prev) - (h0 - roll(h0, 1, 0)) + mass * v2
        inside = jnp.where(i == 18, hi, 1.0)
        u[0, i - 2] = (SUM_SRC * v0 - SECOND_A * a0) * inside
        u[1, i - 2] = (SUM_SRC * v1 - SECOND_A * a1) * inside
        u[2, i - 2] = (SUM_SRC * v2 - SECOND_A * a2) * inside
        hs[0, i - 2] = h0[:, 128:]
        hs[1, i - 2] = h1[:, 128:]
        return (h1, h2)

    lax.fori_loop(2, 19, first_pass, (h1_first, h2_first))

    lane = lax.broadcasted_iota(jnp.int32, (8, 128), 1)
    group = ((lane + 4) & 127) >> 3
    at_last, at_first = lane == 127, lane == 0
    f = SECOND_A

    def second_pass(z, carry):
        u0, u1, u2 = u[0, z], u[1, z], u[2, z]
        flux1 = (after(u0) - u0) - (u[2, z + 1] - u2)
        flux2 = (u[1, z + 1] - u1) - (roll(u0, -1, 0) - u0)
        flux1, flux2 = flux1[:8], flux2[:8]
        out[z, :, 0:256] = 0.5 * (flux1 * flux1 - flux2 * flux2)
        f1l, f1r, f2l, f2r = flux1[:, :128], flux1[:, 128:], flux2[:, :128], flux2[:, 128:]
        h1 = hs[1, z]
        fh1 = f * h1[:8]
        curl_h = f * ((hs[0, z + 1] - hs[0, z]) + (roll(h1, -1, 0) - h1))[:8]
        rel, _ = materials(g[z + 2, :, 128:])
        rel_n, _ = materials(g[z + 3, :, 128:])
        rel_up = f * roll(rel, -1, 0)[:8]
        rel_dn = f * roll(rel, 1, 0)[:8]
        rel_n_dn = f * roll(rel_n, 1, 0)[:8]
        v0, v1 = v[0, z + 2, :, :128], v[1, z + 2, :, :128]
        v0_up = roll(v0, -1, 0)[:8]
        v1_dn = roll(v1, 1, 0)[:8]
        v0, v1 = v0[:8], v1[:8]
        v0_p, v0_m = v[0, z + 3, 0:8, :128], v[0, z + 1, 0:8, :128]
        v1_p = v[1, z + 3, :, :128]
        v1_p_dn = roll(v1_p, 1, 0)[:8]
        v1_p = v1_p[:8]
        inside = jnp.where(z == 15, hi, 1.0)
        r_a = u0[:8, :128] + f * ((v0_p + v0_m) - (3.0 + inside) * v0 + (v1_p - v1))
        r_b = f * ((v1_p - v1) + v0)
        r_c = f1l + f * v0
        r_d = f2l - r_b
        parts = (
            (0, jnp.where(at_first, roll(fh1, 1, 1), jnp.where(at_last, f1r - fh1, f1r))),
            (1, jnp.where(at_first, roll(curl_h, 1, 1), f2r)),
            (2, jnp.where(at_last, -rel_n_dn, 0.0)),
            (3, jnp.where(at_last, rel_dn, 0.0)),
            (4, jnp.where(at_first, roll(rel_up, 1, 1), jnp.where(at_last, -rel_up, 0.0))),
            (8, jnp.where(at_first, r_c, jnp.where(at_last, roll(r_a, -1, 1), roll(f * v0, -2, 1)))),
            (9, jnp.where(at_first, r_d, jnp.where(at_last, roll(r_b, -1, 1), 0.0))),
            (10, roll(v1_p_dn, -1, 1)),
            (11, roll(v1_dn, -1, 1)),
            (12, jnp.where(at_first, v0_up, roll(v0_up, -1, 1))),
        )
        extra = jnp.zeros((8, 128), F32)
        for k, part in parts:
            extra = jnp.where(group == k, roll(part, 8 * k, 1) if k else part, extra)
        out[z, :, 256:384] = extra
        return carry

    lax.fori_loop(0, 16, second_pass, 0)


def stress_call(info, src, reg, sw1, up, dn, sw2):
    return pl.pallas_call(
        stress_kernel,
        out_shape=jax.ShapeDtypeStruct((16, 8, 384), F32),
        in_specs=[SMEM] + [VMEM] * 6,
        out_specs=VMEM,
        scratch_shapes=[
            pltpu.VMEM((3, 20, 16, 256), F32),
            pltpu.VMEM((20, 16, 256), F32),
            pltpu.VMEM((3, 17, 16, 256), F32),
            pltpu.VMEM((2, 17, 16, 128), F32),
        ],
        compiler_params=pltpu.CompilerParams(vmem_limit_bytes=16 * 2**20),
        cost_estimate=pl.CostEstimate(flops=20_000_000, bytes_accessed=2_000_000, transcendentals=0),
        name="stress",
    )(info, src, reg, sw1, up, dn, sw2)


def rims_kernel(info, src, reg, sw1, up, dn, sw2, field, up_out, dn_out):
    core, lo, hi = info[0], info[1].astype(F32), info[2].astype(F32)
    pick3 = from_partner((16, 8, 256), core)
    pick = from_partner((8, 256), core)
    for c in range(4):
        empty = 0.0 if c < 3 else -1.0
        field[c, 2:18, 0:16, :] = src[c] if c < 3 else reg[...].astype(F32)
        field[c, 2:18, 16:24, :] = jnp.where(pick3, sw1[c], empty)

        def put(i, value, beside, valid):
            field[c, i, 0:16, :] = (value - empty) * valid + empty
            field[c, i, 16:24, :] = jnp.where(pick, (beside - empty) * valid + empty, empty)

        put(0, up[c, 0], sw2[2 * c], lo)
        put(1, up[c, 1], sw2[2 * c + 1], lo)
        put(18, dn[c], sw2[8 + c], hi)
        if c in (1, 2):
            put(19, dn[3 + c], sw2[11 + c], hi)
        else:
            field[c, 19] = jnp.full((24, 256), empty, F32)
    lane = lax.broadcasted_iota(jnp.int32, (24, 128), 1) >> 1
    for t in range(2):
        up_acc = jnp.zeros((24, 128), F32)
        dn_acc = jnp.zeros((24, 128), F32)
        for k in range(64):
            q = 64 * t + k
            if q >= 80:
                break
            c, i = q // 20, q % 20
            here = lane == k
            up_acc = jnp.where(here, roll(field[c, i, :, 128:], 2 * k + 2, 1), up_acc)
            dn_acc = jnp.where(here, roll(field[c, i, :, :128], 2 * k, 1), dn_acc)
        up_out[:, 128 * t : 128 * t + 128] = up_acc
        dn_out[:, 128 * t : 128 * t + 128] = dn_acc


def rims_call(info, src, reg, sw1, up, dn, sw2):
    return pl.pallas_call(
        rims_kernel,
        out_shape=[
            jax.ShapeDtypeStruct((4, 20, 24, 256), F32),
            jax.ShapeDtypeStruct((24, 256), F32),
            jax.ShapeDtypeStruct((24, 256), F32),
        ],
        in_specs=[SMEM] + [VMEM] * 6,
        out_specs=[VMEM] * 3,
        compiler_params=pltpu.CompilerParams(vmem_limit_bytes=16 * 2**20),
        cost_estimate=pl.CostEstimate(flops=2_000_000, bytes_accessed=4_000_000, transcendentals=0),
        name="rims",
    )(info, src, reg, sw1, up, dn, sw2)


def steps_kernel(field, left, right, sol, res, v, s):
    lane = lax.broadcasted_iota(jnp.int32, (24, 128), 1)
    for c in range(4):
        v[c, :, :, 0:256] = field[c]
        for i in range(20):
            q = 20 * c + i
            t, k = q // 64, q % 64
            tile = slice(128 * t, 128 * t + 128)
            v[c, i, :, 256:384] = jnp.where(
                lane < 64, roll(right[:, tile], -2 * k, 1), roll(left[:, tile], -2 * k - 2, 1)
            )

    def strength(w, i, reluct):
        v0, v1, v2 = w[0, i], w[1, i], w[2, i]
        c0, c1, c2 = curl(
            v0,
            v1,
            v2,
            roll(v0, -1, 1),
            roll(v1, -1, 1),
            roll(v0, -1, 0),
            roll(v2, -1, 0),
            w[1, i + 1],
            w[2, i + 1],
        )
        return (v0, v1, v2), (reluct * c0, reluct * c1, reluct * c2)

    def operator(w, i, code, h1_prev, h2_prev):
        reluct, mass = materials(code)
        (v0, v1, v2), (h0, h1, h2) = strength(w, i, reluct)
        a0 = (h2 - roll(h2, 1, 0)) - (h1 - roll(h1, 1, 1)) + mass * v0
        a1 = (h0 - roll(h0, 1, 1)) - (h2 - h2_prev) + mass * v1
        a2 = (h1 - h1_prev) - (h0 - roll(h0, 1, 0)) + mass * v2
        return (v0, v1, v2), (a0, a1, a2), (h1, h2), mass

    def step_plane(i, carry):
        vs, a, carry, mass = operator(v, i, v[3, i], *carry)
        inside = mass > 0.0
        for c in range(3):
            s[c, i] = jnp.where(inside, SECOND_SRC * vs[c] - SECOND_A * a[c], 0.0)
        return vs, a, carry

    _, (_, h1, h2) = strength(v, 0, materials(v[3, 0])[0])
    _, _, carry = step_plane(1, (h1, h2))

    def first_pass(i, carry):
        vs, a, carry = step_plane(i, carry)
        for c in range(3):
            own = vs[c][:16, :256]
            res[c, i - 2] = own - FIRST * a[c][:16, :256]
            sol[c, i - 2] = FIRST * own + s[c, i, 0:16, 0:256]
        return carry

    carry = lax.fori_loop(2, 18, first_pass, carry)
    step_plane(18, carry)

    _, (_, h1, h2) = strength(s, 1, materials(v[3, 1])[0])

    def second_pass(i, carry):
        _, a, carry, _ = operator(s, i, v[3, i], *carry)
        for c in range(3):
            res[c, i - 2] = res[c, i - 2] - a[c][:16, :256]
        return carry

    lax.fori_loop(2, 18, second_pass, (h1, h2))


def steps_call(field, left, right):
    return pl.pallas_call(
        steps_kernel,
        out_shape=[jax.ShapeDtypeStruct((3, 16, 16, 256), F32)] * 2,
        in_specs=[VMEM] * 3,
        out_specs=[VMEM] * 2,
        scratch_shapes=[
            pltpu.VMEM((4, 20, 24, 384), F32),
            pltpu.VMEM((3, 19, 24, 384), F32),
        ],
        compiler_params=pltpu.CompilerParams(vmem_limit_bytes=24 * 2**20),
        cost_estimate=pl.CostEstimate(flops=60_000_000, bytes_accessed=6_000_000, transcendentals=0),
        name="steps",
    )(field, left, right)


def harmonics_kernel(block, basis_hi, basis_lo, cosine, sine, out):
    lane = lax.broadcasted_iota(jnp.int32, (16, 8, 128), 2)
    seam = block[:, :, 256:384]
    right = roll(jnp.concatenate([seam[1:], seam[:1]], axis=0).reshape(128, 128), 64, 1)
    seam = seam.reshape(128, 128)
    total, product = seam + right, seam * right
    flux1 = total + roll(product, -16, 1) + roll(product, -24, 1)
    flux2 = roll(total, -8, 1) + roll(product, -32, 1)
    fixed = (0.5 * (flux1 * flux1 - flux2 * flux2)).reshape(16, 8, 128)
    moved = jnp.concatenate([fixed[15:], fixed[:15]], axis=0)
    low = jnp.where(lane == 0, moved, block[:, :, 0:128])
    high = jnp.where(lane >= 126, fixed, block[:, :, 128:256])
    x = jnp.concatenate([low.reshape(128, 128), high.reshape(128, 128)], axis=1)
    x_hi = x.astype(jnp.bfloat16)
    x_lo = (x - x_hi.astype(F32)).astype(jnp.bfloat16)

    def dot(a, b):
        return jnp.dot(a, b[...], preferred_element_type=F32)

    local = dot(x_hi, basis_hi) + (dot(x_hi, basis_lo) + dot(x_lo, basis_hi))
    local = local.reshape(16, 8, 2 * MH)
    real = jnp.zeros((8, MH), F32)
    imag = jnp.zeros((8, MH), F32)
    for j in range(16):
        c, s = cosine[j : j + 1, :], sine[j : j + 1, :]
        pc, ps = local[j, :, :MH], local[j, :, MH:]
        real = real + (pc * c - ps * s)
        imag = imag - (pc * s + ps * c)
    out[0, 0] = real
    out[1, 0] = imag


def harmonics_call(block, cosine, sine):
    turns = np.arange(256)[:, None] * np.arange(MH)[None, :] / NA
    angle = 2.0 * math.pi * turns
    basis = np.concatenate([np.cos(angle), np.sin(angle)], axis=1) / math.sqrt(NA)
    hi = basis.astype(jnp.bfloat16)
    lo = (basis - hi.astype(np.float64)).astype(jnp.bfloat16)
    return pl.pallas_call(
        harmonics_kernel,
        out_shape=jax.ShapeDtypeStruct((2, 1, 8, MH), F32),
        in_specs=[VMEM] * 5,
        out_specs=VMEM,
        compiler_params=pltpu.CompilerParams(vmem_limit_bytes=8 * 2**20),
        cost_estimate=pl.CostEstimate(flops=100_000_000, bytes_accessed=1_000_000, transcendentals=0),
        name="harmonics",
    )(block, jnp.asarray(hi), jnp.asarray(lo), cosine, sine)


def ring(axis, size, step):
    return functools.partial(
        lax.ppermute, axis_name=axis, perm=[(i, (i + step) % size) for i in range(size)]
    )


def on_device(source, region, skew_shift):
    n_az, n_ax = lax.axis_size("az"), lax.axis_size("ax")
    az, ax, rad = lax.axis_index("az"), lax.axis_index("ax"), lax.axis_index("rad")
    info = jnp.stack([rad, (ax > 0).astype(jnp.int32), (ax < n_ax - 1).astype(jnp.int32)])
    edge = region.astype(F32)
    up = jnp.concatenate([source[:, 14:16], edge[None, 14:16]], axis=0)
    dn = jnp.concatenate([source[:, 0], edge[None, 0], source[1:3, 1]], axis=0)
    up = ring("ax", n_ax, 1)(up)
    dn = ring("ax", n_ax, -1)(dn)
    swap = ring("rad", 2, 1)
    start = 8 * (1 - rad)
    sw1 = swap(
        jnp.concatenate(
            [
                lax.dynamic_slice_in_dim(source, start, 8, axis=2),
                lax.dynamic_slice_in_dim(edge, start, 8, axis=1)[None],
            ],
            axis=0,
        )
    )
    rim = jnp.concatenate([up.reshape(8, 16, 256), dn], axis=0)
    sw2 = swap(lax.dynamic_slice_in_dim(rim, start, 8, axis=1))
    stress = stress_call(info, source, region, sw1, up, dn, sw2)
    block = lax.all_to_all(stress, "az", split_axis=0, concat_axis=0, tiled=True)
    field, az_up, az_dn = rims_call(info, source, region, sw1, up, dn, sw2)
    left = ring("az", n_az, 1)(az_up)
    right = ring("az", n_az, -1)(az_dn)
    solution, residual = steps_call(field, left, right)
    shift = lax.dynamic_slice_in_dim(skew_shift, az, 1)
    offset = 256 * jnp.arange(16, dtype=jnp.int32) - shift
    turns = (offset[:, None] * jnp.arange(MH, dtype=jnp.int32)[None, :]) & (NA - 1)
    angle = turns.astype(F32) * (2.0 * math.pi / NA)
    harmonics = harmonics_call(block, jnp.cos(angle), jnp.sin(angle))
    return (solution, residual, harmonics)


def solution(mesh):
    in_specs = (P(None, "ax", "rad", "az"), P("ax", "rad", "az"), P("ax"))
    out_specs = (
        P(None, "ax", "rad", "az"),
        P(None, "ax", "rad", "az"),
        P(None, ("ax", "az"), "rad", None),
    )
    return jax.shard_map(
        on_device, mesh=mesh, in_specs=in_specs, out_specs=out_specs, check_vma=False
    )
```

time: 133 us -> 49.4 us (0.37)
  the two profiles are of different devices: /device:TPU:5 before, /device:TPU:8 now
where the time goes in v1:
time: 49.4 us; the launch traced here: 48.5 us
  starting transfers between devices  20.2 us (41%)
  Pallas kernels  16 us (32%)
  waiting for transfers between devices  7 us (14%)
  local copies, waits for them, and re-layouts  2.66 us (5%)
  other arithmetic  1.9 us (4%)
  between operations  0.79 us (2%)
    all_to_all x1, starting transfers between devices, on_device(): lax.all_to_all(stress, 'az', split_axis=0, concat_axis=0, tiled=True)  9.94 us
    pallas_call x1, Pallas kernels, steps_call(): pl.pallas_call(steps_kernel, out_shape=[jax.ShapeDtypeStruct((3, 16, 16,...  7.27 us
    pallas_call x1, Pallas kernels, stress_call(): pl.pallas_call(stress_kernel, out_shape=jax.ShapeDtypeStruct((16, 8, 384)...  6.55 us
    ppermute x1, waiting for transfers between devices, on_device(): dn = ring('ax', n_ax, -1)(dn)  3.98 us
    ppermute x1, starting transfers between devices, on_device(): dn = ring('ax', n_ax, -1)(dn)  3.42 us
    ppermute x1, starting transfers between devices, on_device(): right = ring('az', n_az, -1)(az_dn)  2.67 us
    ppermute x1, starting transfers between devices, on_device(): up = ring('ax', n_ax, 1)(up)  2.37 us
    ppermute x1, waiting for transfers between devices, on_device(): left = ring('az', n_az, 1)(az_up)  1.83 us
  transfers between devices with their start and end apart: 7, of which 3 were waited for; matrix products, arithmetic and copies ran while one was open for 5% of the time, Pallas kernels for 17%

profile of v1, /device:TPU:8, one launch (start us, length us, event | category | flops | bytes accessed | tf_op | source)
XLA Modules:
  0.0 48.5 jit_solution(16483909566769494848)
XLA Ops:
  0.6 0.0 copy-start.1
  0.7 1.0 %slice.15 = f32[3,2,16,256]{3,2,1,0:T(8,128)S(1)} slice(f32[3,16,16,256]{3,2,1,0:T(8,128)} %src.3), slice={[0:3], [14:16], [0:16], [0:256]} | slice | bytes 196608 | tf_op jit(solution)/shard_map/slice | solution.py:386
  1.6 1.0 %convert_element_type.8 = f32[16,16,256]{2,1,0:T(8,128)S(1)} convert(s32[16,16,256]{2,1,0:T(8,128)} %reg.3) | non-fusion elementwise | flops 65536 | bytes 524288 | tf_op jit(solution)/shard_map/convert_element_type | solution.py:385
  2.6 2.4 %collective-permute-start.1 = (f32[4,2,16,256]{3,2,1,0:T(8,128)S(1)}, f32[4,2,16,256]{3,2,1,0:T(8,128)S(1)}, u32[]{:S(2)}, u32[]{:S(2)}) collective-permute-start(f32[4,2,16,256]{3,2,1,0:T(8,128)S(1)} %pad_maximum_fusion.1), channel_id=1, source_target_pairs={{0,2},{2,4},{4,6},{6,8},{8,10},{10,12},{12,14},{14,0},{1,3},{3,5},... | collective-permute-start | bytes 393224 | tf_op jit(solution)/shard_map/ppermute | solution.py:388
  5.0 1.0 %constant_dynamic-slice_fusion = f32[3,16,8,256]{3,2,1,0:T(8,128)S(1)} fusion(f32[3,16,16,256]{3,2,1,0:T(8,128)} %src.3, s32[]{:T(128)S(6)} %select_n.8), kind=kLoop, calls=%fused_computation.13 | loop fusion | bytes 786436 | tf_op jit(solution)/shard_map/dynamic_slice | solution.py:395
  6.1 0.1 collective-permute-start
  6.3 3.4 %collective-permute-start.2 = (f32[6,16,256]{2,1,0:T(8,128)S(1)}, f32[6,16,256]{2,1,0:T(8,128)S(1)}, u32[]{:S(2)}, u32[]{:S(2)}) collective-permute-start(f32[6,16,256]{2,1,0:T(8,128)S(1)} %pad_maximum_fusion.2), channel_id=1, source_target_pairs={{0,14},{2,0},{4,2},{6,4},{8,6},{10,8},{12,10},{14,12},{1,15},{3,1}... | collective-permute-start | bytes 294920 | tf_op jit(solution)/shard_map/ppermute | solution.py:389
  9.7 4.0 %collective-permute-done.2.dn = f32[6,16,256]{2,1,0:T(8,128)S(1)} collective-permute-done((f32[6,16,256]{2,1,0:T(8,128)S(1)}, f32[6,16,256]{2,1,0:T(8,128)S(1)}, u32[]{:S(2)}, u32[]{:S(2)}) %collective-permute-start.2) | collective-permute-done | bytes 98336 | tf_op jit(solution)/shard_map/ppermute | solution.py:389
  13.7 0.2 collective-permute-start.3
  13.9 0.1 pad_add_fusion.info
  13.9 1.2 %collective-permute-done.3.sw2 = f32[14,8,256]{2,1,0:T(8,128)S(1)} collective-permute-done((f32[14,8,256]{2,1,0:T(8,128)S(1)}, f32[14,8,256]{2,1,0:T(8,128)S(1)}, u32[]{:S(2)}, u32[]{:S(2)}) %collective-permute-start.3) | collective-permute-done | bytes 114720 | tf_op jit(solution)/shard_map/ppermute | solution.py:402
  15.1 6.5 %stress.1 = f32[16,8,384]{2,1,0:T(8,128)} custom-call(s32[3]{0:T(128)S(1)} %pad_add_fusion.info, f32[3,16,16,256]{3,2,1,0:T(8,128)S(1)} %copy-done, s32[16,16,256]{2,1,0:T(8,128)S(1)} %copy-done.1, f32[4,16,8,256]{3,2,1,0:T(8,128)S(1)} %collective-permute-done.sw1, f32[4,2,16,256]{3,2,1,0:T(8,128)S(1)} %collective-permute-done.1.up, ...), custom_call_target="tpu_custom_call" | custom-call | flops 20000000 | bytes 2000000 | tf_op jit(solution)/shard_map/stress/pallas_call | solution.py:174
  21.7 9.9 %all-to-all-start = ((f32[16,8,384]{2,1,0:T(8,128)}), f32[16,8,384]{2,1,0:T(8,128)S(1)}, u32[]{:S(2)}, u32[]{:S(2)}) async-start(f32[16,8,384]{2,1,0:T(8,128)} %stress.1), calls=%async_computation | async-start | bytes 393216 | tf_op jit(solution)/shard_map/all_to_all | solution.py:404
  31.6 0.6 %dynamic_slice.15 = s32[1]{0:T(128)} dynamic-slice(s32[16]{0:T(128)S(1)} %copy-done.4, s32[]{:T(128)S(6)} %select_n.9), dynamic_slice_sizes={1} | dynamic-slice | bytes 12 | tf_op jit(solution)/shard_map/dynamic_slice | solution.py:409
  32.2 0.6 %multiply_subtract_fusion = s32[16]{0:T(128)S(1)} fusion(s32[]{:T(128)} %bitcast.8), kind=kLoop, calls=%fused_computation.15 | loop fusion | flops 32 | bytes 68 | tf_op jit(solution)/shard_map/sub | solution.py:410
  32.9 0.0 copy-start.2
  32.9 0.0 copy-start.3
  32.9 1.1 %rims.1 = (f32[4,20,24,256]{3,2,1,0:T(8,128)S(1)}, f32[24,256]{1,0:T(8,128)S(1)}, f32[24,256]{1,0:T(8,128)S(1)}) custom-call(s32[3]{0:T(128)S(1)} %pad_add_fusion.info, f32[3,16,16,256]{3,2,1,0:T(8,128)S(1)} %copy-done, s32[16,16,256]{2,1,0:T(8,128)S(1)} %copy-done.1, f32[4,16,8,256]{3,2,1,0:T(8,128)S(1)} %collective-permute-done.sw1, ...), custom_call_target="tpu_custom_call" | custom-call | flops 2000000 | bytes 4000000 | tf_op jit(solution)/shard_map/rims/pallas_call | solution.py:228
  34.0 1.5 %collective-permute-start.4 = (f32[24,256]{1,0:T(8,128)S(1)}, f32[24,256]{1,0:T(8,128)S(1)}, u32[]{:S(2)}, u32[]{:S(2)}) collective-permute-start(f32[24,256]{1,0:T(8,128)S(1)} %get-tuple-element.9), channel_id=1, source_target_pairs={{0,16},{16,32},{32,48},{48,64},{64,80},{80,96},{96,112},{112,128},... | collective-permute-start | bytes 73736 | tf_op jit(solution)/shard_map/ppermute | solution.py:406
  35.6 2.7 %collective-permute-start.5 = (f32[24,256]{1,0:T(8,128)S(1)}, f32[24,256]{1,0:T(8,128)S(1)}, u32[]{:S(2)}, u32[]{:S(2)}) collective-permute-start(f32[24,256]{1,0:T(8,128)S(1)} %get-tuple-element.10), channel_id=1, source_target_pairs={{0,240},{16,0},{32,16},{48,32},{64,48},{80,64},{96,80},{112,96},{1... | collective-permute-start | bytes 73736 | tf_op jit(solution)/shard_map/ppermute | solution.py:407
  38.2 0.1 fusion.1
  38.4 1.8 %collective-permute-done.4.left = f32[24,256]{1,0:T(8,128)S(1)} collective-permute-done((f32[24,256]{1,0:T(8,128)S(1)}, f32[24,256]{1,0:T(8,128)S(1)}, u32[]{:S(2)}, u32[]{:S(2)}) %collective-permute-start.4) | collective-permute-done | bytes 24608 | tf_op jit(solution)/shard_map/ppermute | solution.py:406
  40.2 7.3 %steps.1 = (f32[3,16,16,256]{3,2,1,0:T(8,128)}, f32[3,16,16,256]{3,2,1,0:T(8,128)}) custom-call(f32[4,20,24,256]{3,2,1,0:T(8,128)S(1)} %get-tuple-element.8.field, f32[24,256]{1,0:T(8,128)S(1)} %collective-permute-done.4.left, f32[24,256]{1,0:T(8,128)S(1)} %collective-permute-done.5.right), custom_call_target="tpu_custom_call" | custom-call | flops 60000000 | bytes 6000000 | tf_op jit(solution)/shard_map/steps/pallas_call | solution.py:311
  47.5 1.0 %harmonics.1 = f32[2,1,8,256]{3,2,1,0:T(8,128)} custom-call(f32[16,8,384]{2,1,0:T(8,128)S(1)} %all-to-all-done.block, bf16[256,512]{1,0:T(8,128)(2,1)S(1)} %copy-done.3, bf16[256,512]{1,0:T(8,128)(2,1)S(1)} %copy-done.2, f32[16,256]{1,0:T(8,128)S(1)} %get-tuple-element.14.cosine, f32[16,256]{1,0:T(8,128)S(1)} %get-tuple-element.13.sine), custom_call_target="tpu_custom_call" | custom-call | flops 100000000 | bytes 1000000 | tf_op jit(solution)/shard_map/harmonics/pallas_call | solution.py:364
  (20 shorter events, 0.1 us)
Async XLA Ops:
  0.6 5.6 %copy-start = (f32[3,16,16,256]{3,2,1,0:T(8,128)S(1)}, f32[3,16,16,256]{3,2,1,0:T(8,128)}, u32[]{:S(2)}) copy-start(f32[3,16,16,256]{3,2,1,0:T(8,128)} %src.3) | copy-start | bytes 2359300
  0.6 14.5 %copy-start.1 = (s32[16,16,256]{2,1,0:T(8,128)S(1)}, s32[16,16,256]{2,1,0:T(8,128)}, u32[]{:S(2)}) copy-start(s32[16,16,256]{2,1,0:T(8,128)} %reg.3) | copy-start | bytes 786436
  2.6 11.0 %collective-permute-start.1 = (f32[4,2,16,256]{3,2,1,0:T(8,128)S(1)}, f32[4,2,16,256]{3,2,1,0:T(8,128)S(1)}, u32[]{:S(2)}, u32[]{:S(2)}) collective-permute-start(f32[4,2,16,256]{3,2,1,0:T(8,128)S(1)} %pad_maximum_fusion.1), channel_id=1, source_target_pairs={{0,2},{2,4},{4,6},{6,8},{8,10},{10,12},{12,14},{14,0},{1,3},{3,5},... | collective-permute-start | bytes 393224 | tf_op jit(solution)/shard_map/ppermute | solution.py:388
  6.1 25.5 %copy-start.4 = (s32[16]{0:T(128)S(1)}, s32[16]{0:T(128)}, u32[]{:S(2)}) copy-start(s32[16]{0:T(128)} %param.7) | copy-start | bytes 196
  6.1 9.0 %collective-permute-start = (f32[4,16,8,256]{3,2,1,0:T(8,128)S(1)}, f32[4,16,8,256]{3,2,1,0:T(8,128)S(1)}, u32[]{:S(2)}, u32[]{:S(2)}) collective-permute-start(f32[4,16,8,256]{3,2,1,0:T(8,128)S(1)} %pad_maximum_fusion), channel_id=1, source_target_pairs={{0,1},{1,0},{2,3},{3,2},{4,5},{5,4},{6,7},{7,6},{8,9},{9,8},{10,11... | collective-permute-start | bytes 1572872 | tf_op jit(solution)/shard_map/ppermute | solution.py:392
  6.3 7.4 %collective-permute-start.2 = (f32[6,16,256]{2,1,0:T(8,128)S(1)}, f32[6,16,256]{2,1,0:T(8,128)S(1)}, u32[]{:S(2)}, u32[]{:S(2)}) collective-permute-start(f32[6,16,256]{2,1,0:T(8,128)S(1)} %pad_maximum_fusion.2), channel_id=1, source_target_pairs={{0,14},{2,0},{4,2},{6,4},{8,6},{10,8},{12,10},{14,12},{1,15},{3,1}... | collective-permute-start | bytes 294920 | tf_op jit(solution)/shard_map/ppermute | solution.py:389
  13.7 1.4 %collective-permute-start.3 = (f32[14,8,256]{2,1,0:T(8,128)S(1)}, f32[14,8,256]{2,1,0:T(8,128)S(1)}, u32[]{:S(2)}, u32[]{:S(2)}) collective-permute-start(f32[14,8,256]{2,1,0:T(8,128)S(1)} %fusion), channel_id=1, source_target_pairs={{0,1},{1,0},{2,3},{3,2},{4,5},{5,4},{6,7},{7,6},{8,9},{9,8},{10,11... | collective-permute-start | bytes 344072 | tf_op jit(solution)/shard_map/ppermute | solution.py:402
  21.7 25.8 %all-to-all-start = ((f32[16,8,384]{2,1,0:T(8,128)}), f32[16,8,384]{2,1,0:T(8,128)S(1)}, u32[]{:S(2)}, u32[]{:S(2)}) async-start(f32[16,8,384]{2,1,0:T(8,128)} %stress.1), calls=%async_computation | async-start | bytes 393216 | tf_op jit(solution)/shard_map/all_to_all | solution.py:404
  32.9 14.6 %copy-start.2 = (bf16[256,512]{1,0:T(8,128)(2,1)S(1)}, bf16[256,512]{1,0:T(8,128)(2,1)}, u32[]{:S(2)}) copy-start(bf16[256,512]{1,0:T(8,128)(2,1)} %constant.34.clone.basis_lo) | copy-start | bytes 786436
  32.9 14.6 %copy-start.3 = (bf16[256,512]{1,0:T(8,128)(2,1)S(1)}, bf16[256,512]{1,0:T(8,128)(2,1)}, u32[]{:S(2)}) copy-start(bf16[256,512]{1,0:T(8,128)(2,1)} %constant.33.clone.basis_hi) | copy-start | bytes 786436
  34.0 6.2 %collective-permute-start.4 = (f32[24,256]{1,0:T(8,128)S(1)}, f32[24,256]{1,0:T(8,128)S(1)}, u32[]{:S(2)}, u32[]{:S(2)}) collective-permute-start(f32[24,256]{1,0:T(8,128)S(1)} %get-tuple-element.9), channel_id=1, source_target_pairs={{0,16},{16,32},{32,48},{48,64},{64,80},{80,96},{96,112},{112,128},... | collective-permute-start | bytes 73736 | tf_op jit(solution)/shard_map/ppermute | solution.py:406
  35.6 4.7 %collective-permute-start.5 = (f32[24,256]{1,0:T(8,128)S(1)}, f32[24,256]{1,0:T(8,128)S(1)}, u32[]{:S(2)}, u32[]{:S(2)}) collective-permute-start(f32[24,256]{1,0:T(8,128)S(1)} %get-tuple-element.10), channel_id=1, source_target_pairs={{0,240},{16,0},{32,16},{48,32},{64,48},{80,64},{96,80},{112,96},{1... | collective-permute-start | bytes 73736 | tf_op jit(solution)/shard_map/ppermute | solution.py:407

commit v2 on v0

v2 whole, which is shorter than its diff:
```python
import functools
import math

import jax
import jax.numpy as jnp
import numpy as np
from jax import lax
from jax.experimental import pallas as pl
from jax.experimental.pallas import tpu as pltpu
from jax.sharding import PartitionSpec as P

NA = 4096
MH = 256
F32 = jnp.float32

cheb_center = 7.1
cheb_radius = 6.9
ratio_sigma = cheb_center / cheb_radius
rho_first = 1.0 / ratio_sigma
rho_second = 1.0 / (2.0 * ratio_sigma - rho_first)
keep_weight = rho_second * rho_first
fresh_weight = 2.0 * rho_second / cheb_radius

FIRST = 1.0 / cheb_center
SECOND_SRC = keep_weight / cheb_center + fresh_weight
SECOND_A = fresh_weight / cheb_center
SUM_SRC = FIRST + SECOND_SRC

VMEM = pl.BlockSpec(memory_space=pltpu.VMEM)
SMEM = pl.BlockSpec(memory_space=pltpu.SMEM)
HBM = pl.BlockSpec(memory_space=pltpu.HBM)

UNROLL = 2
SEND_KIB = 54784


def materials(code):
    iron, magnet, outside = code == 1.0, code == 2.0, code < 0.0
    reluct = jnp.where(iron, 0.05, jnp.where(magnet, 0.95, jnp.where(outside, 0.0, 1.0)))
    mass = jnp.where(
        iron,
        1.5,
        jnp.where(magnet, 0.6, jnp.where(outside, 0.0, jnp.where(code == 0.0, 0.2, 2.0))),
    )
    return reluct.astype(F32), mass.astype(F32)


def roll(x, shift, axis):
    return pltpu.roll(x, shift % x.shape[axis], axis)


def from_partner(shape, core):
    sub = lax.broadcasted_iota(jnp.int32, shape, len(shape) - 2)
    return (sub >= 6 * core) & (sub < 6 * core + 2)


class Kept:
    planes = 48
    of_field, of_step, of_res = (0, 1, 13, 14, 15), (1, 2, 13, 14), (1, 14)

    def field(self, c, z):
        return 5 * c + self.of_field.index(z)

    def step(self, c, z):
        return 20 + 4 * c + self.of_step.index(z)

    def res(self, c, z):
        return (32 + 2 * c + self.of_res.index(z), slice(0, 16))

    def strips(self, c, side):
        return (38 + c, slice(None), slice(128 * side, 128 * side + 128))

    def stress(self, z):
        return (42 + z // 3, slice(8 * (z % 3), 8 * (z % 3) + 8))


class Rim:
    planes = 12 + 6 + 4 + 1

    def step(self, c, z):
        return 4 * c + (-1, 0, 15, 16).index(z)

    def res(self, c, z):
        return (12 + 2 * c + (0, 15).index(z), slice(0, 16))

    def strips(self, c, side):
        return (18 + c, slice(None), slice(128 * side, 128 * side + 128))

    code = 22


KEPT, RIM = Kept(), Rim()


def gap_tile(x, core):
    return jnp.where(core == 1, x[0:8], x[8:16])


def loop(first, last, body, unroll):
    rounds = (last - first) // unroll

    def several(t, carry):
        for k in range(unroll):
            body(first + t * unroll + k)
        return carry

    lax.fori_loop(0, rounds, several, 0)
    for k in range(first + rounds * unroll, last):
        body(k)


def curl(v0, v1, v2, v0a, v1a, v0r, v2r, v1n, v2n):
    return (
        (v2r - v2) - (v1a - v1),
        (v0a - v0) - (v2n - v2),
        (v1n - v1) - (v0r - v0),
    )


def strength(v0, v1, v2, v1n, v2n, reluct):
    c0, c1, c2 = curl(
        v0, v1, v2, roll(v0, -1, 1), roll(v1, -1, 1), roll(v0, -1, 0), roll(v2, -1, 0), v1n, v2n
    )
    return reluct * c0, reluct * c1, reluct * c2


def image(v, h, h1p, h2p, mass):
    h0, h1, h2 = h
    return (
        (h2 - roll(h2, 1, 0)) - (h1 - roll(h1, 1, 1)) + mass * v[0],
        (h0 - roll(h0, 1, 1)) - (h2 - h2p) + mass * v[1],
        (h1 - h1p) - (h0 - roll(h0, 1, 0)) + mass * v[2],
    )


def second_of(v, a, mass):
    return [jnp.where(mass > 0.0, SECOND_SRC * v[c] - SECOND_A * a[c], 0.0) for c in range(3)]


def fluxes(u0, u1, u2, u1n, u2n):
    return (roll(u0, -1, 1) - u0) - (u2n - u2), (u1n - u1) - (roll(u0, -1, 0) - u0)


def stress_of(u0, u1, u2, u1n, u2n, core):
    flux1, flux2 = fluxes(u0, u1, u2, u1n, u2n)
    flux1, flux2 = gap_tile(flux1, core), gap_tile(flux2, core)
    return 0.5 * (flux1 * flux1 - flux2 * flux2)


def pack_plane(rights, lefts, x, i, lane):
    here = (lane >= 6 * i) & (lane < 6 * i + 6)
    right = jnp.where(here, roll(x[:, 128:], 6 * i + 4, 1), rights)
    left = jnp.where(here, roll(x[:, :128], 6 * i + 2, 1), lefts)
    return right, left


def send_kernel(src, reg, up, dn, rows, sems):
    pairs = [
        (reg.at[14:16], rows.at[0:2]),
        (reg.at[0], rows.at[2]),
        (src.at[1, 1], dn.at[4]),
        (src.at[2, 1], dn.at[5]),
    ]
    for c in range(3):
        pairs.append((src.at[c, 14:16], up.at[2 * c : 2 * c + 2]))
        pairs.append((src.at[c, 0], dn.at[c]))
    copies = [pltpu.make_async_copy(x, y, sems.at[n]) for n, (x, y) in enumerate(pairs)]
    for copy in copies:
        copy.start()
    for copy in copies:
        copy.wait()
    up[6:8] = rows[0:2].astype(F32)
    dn[3] = rows[2].astype(F32)


def send_call(src, reg):
    shapes = [(8, 16, 256), (6, 16, 256)]
    return pl.pallas_call(
        send_kernel,
        out_shape=[jax.ShapeDtypeStruct(shape, F32) for shape in shapes],
        in_specs=[HBM, HBM],
        out_specs=[VMEM] * 2,
        scratch_shapes=[pltpu.VMEM((3, 16, 256), jnp.int32), pltpu.SemaphoreType.DMA((10,))],
        compiler_params=pltpu.CompilerParams(vmem_limit_bytes=SEND_KIB * 2**10),
        name="send",
    )(src, reg)


def beside_kernel(src, reg, _, sw):
    core = lax.axis_index("rad")
    tile = pl.ds(pl.multiple_of(8 * (1 - core), 8), 8)
    sub = lax.broadcasted_iota(jnp.int32, (16, 8, 256), 1) >> 1
    packed = jnp.zeros((16, 8, 256), F32)
    for c in range(4):
        rows = src[c, :, tile, :] if c < 3 else reg[:, tile, :].astype(F32)
        first = pltpu.roll(rows, 2 * c, 1) if c else rows
        last = pltpu.roll(rows, (2 * c + 2) % 8, 1) if c < 3 else rows
        packed = jnp.where(sub == c, jnp.where(core == 1, first, last), packed)
    sw[...] = packed


def call(kernel, name, outs, scratch, limit, in_specs, out_specs):
    return pl.pallas_call(
        kernel,
        out_shape=[jax.ShapeDtypeStruct(shape, F32) for shape in outs],
        in_specs=in_specs,
        out_specs=out_specs,
        scratch_shapes=[pltpu.VMEM(x, F32) if isinstance(x, tuple) else x for x in scratch],
        compiler_params=pltpu.CompilerParams(vmem_limit_bytes=limit * 2**20),
        cost_estimate=pl.CostEstimate(flops=10_000_000, bytes_accessed=2_000_000, transcendentals=0),
        name=name,
    )


def inner_kernel(src, reg, sw, kept, flag, sol_out, res_out, field, s, hh, sol, res, ids, sems):
    flag[...] = jnp.zeros(flag.shape, F32)
    core = lax.axis_index("rad")
    pick = from_partner((8, 256), core)
    lane = lax.broadcasted_iota(jnp.int32, (24, 128), 1)
    copies = [pltpu.make_async_copy(src.at[c], field.at[c, :, 0:16, :], sems.at[c]) for c in range(3)]
    copies.append(pltpu.make_async_copy(reg, ids, sems.at[3]))
    for copy in copies:
        copy.start()
    for copy in copies:
        copy.wait()

    def assemble(z):
        for c in range(4):
            first = roll(sw[z], -2 * c, 0) if c else sw[z]
            last = roll(sw[z], 6 - 2 * c, 0) if c < 3 else sw[z]
            rows = jnp.where(core == 1, last, first)
            field[c, z, 16:24, :] = jnp.where(pick, rows, 0.0 if c < 3 else -1.0)
        field[3, z, 0:16, :] = ids[z].astype(F32)

    loop(0, 16, assemble, 4)

    def vec(z):
        return [field[c, z] for c in range(3)]

    def first_h(z):
        reluct, _ = materials(field[3, z])
        h = strength(*vec(z), field[1, z + 1], field[2, z + 1], reluct)
        for c in range(3):
            hh[c, z] = h[c]

    loop(0, 15, first_h, UNROLL)

    def first_a(z):
        v = vec(z)
        _, mass = materials(field[3, z])
        a = image(v, [hh[c, z] for c in range(3)], hh[1, z - 1], hh[2, z - 1], mass)
        step = second_of(v, a, mass)
        for c in range(3):
            s[c, z] = step[c]
            res[c, z] = (v[c] - FIRST * a[c])[:16]
            sol[c, z] = (FIRST * v[c] + step[c])[:16]

    loop(1, 15, first_a, UNROLL)

    copies = [pltpu.make_async_copy(sol, sol_out, sems.at[0])]
    copies[0].start()

    def stress_plane(z):
        u0, u1, u2 = [FIRST * field[c, z] + s[c, z] for c in range(3)]
        u1n, u2n = [FIRST * field[c, z + 1] + s[c, z + 1] for c in (1, 2)]
        kept[KEPT.stress(z)] = stress_of(u0, u1, u2, u1n, u2n, core)

    for z in range(1, 14):
        stress_plane(z)

    def second_h(z):
        reluct, _ = materials(field[3, z])
        h = strength(s[0, z], s[1, z], s[2, z], s[1, z + 1], s[2, z + 1], reluct)
        for c in range(3):
            hh[c, z] = h[c]

    loop(1, 14, second_h, UNROLL)

    def second_a(z):
        _, mass = materials(field[3, z])
        v = [s[c, z] for c in range(3)]
        a = image(v, [hh[c, z] for c in range(3)], hh[1, z - 1], hh[2, z - 1], mass)
        for c in range(3):
            res[c, z] = res[c, z] - a[c][:16]

    loop(2, 14, second_a, UNROLL)
    copies.append(pltpu.make_async_copy(res, res_out, sems.at[1]))
    copies[1].start()
    for c in range(3):
        for z in KEPT.of_step:
            kept[KEPT.step(c, z)] = s[c, z]
        for z in KEPT.of_res:
            kept[KEPT.res(c, z)] = res[c, z]
    for c in range(4):
        for z in KEPT.of_field:
            kept[KEPT.field(c, z)] = field[c, z]

    for c in range(4):
        right = left = jnp.full((24, 128), 0.0 if c < 3 else -1.0, F32)
        for z in range(16):
            right, left = pack_plane(right, left, field[c, z], z + 2, lane)
        kept[KEPT.strips(c, 0)] = right
        kept[KEPT.strips(c, 1)] = left

    for copy in copies:
        copy.wait()


def rim_kernel(kept, up, dn, sw2, _, hbm, rim, az_up, az_dn, w, out, sem):
    core, ax = lax.axis_index("rad"), lax.axis_index("ax")
    lo = jnp.where(ax > 0, 1.0, 0.0)
    hi = jnp.where(ax < lax.axis_size("ax") - 1, 1.0, 0.0)
    pick = from_partner((8, 256), core)
    for c in range(4):
        empty = 0.0 if c < 3 else -1.0

        def put(i, value, beside, valid):
            w[c, i, 0:16, :] = (value - empty) * valid + empty
            w[c, i, 16:24, :] = jnp.where(pick, (beside - empty) * valid + empty, empty)

        put(0, up[2 * c], sw2[2 * c], lo)
        put(1, up[2 * c + 1], sw2[2 * c + 1], lo)
        put(6, dn[c], sw2[8 + c], hi)
        if c in (1, 2):
            put(7, dn[3 + c], sw2[11 + c], hi)
        else:
            w[c, 7] = jnp.full((24, 256), empty, F32)
        w[c, 2] = kept[KEPT.field(c, 0)]
        w[c, 3] = kept[KEPT.field(c, 1)]
        w[c, 4] = kept[KEPT.field(c, 14)]
        w[c, 5] = kept[KEPT.field(c, 15)]

    def vec(i):
        return [w[c, i] for c in range(3)]

    def h_of(i, reluct):
        return strength(*vec(i), w[1, i + 1], w[2, i + 1], reluct)

    def rims(i, zs):
        _, h1, h2 = h_of(i, materials(w[3, i])[0])
        steps = []
        for n in range(2):
            reluct, mass = materials(w[3, i + 1 + n])
            h = h_of(i + 1 + n, reluct)
            v = vec(i + 1 + n)
            a = image(v, h, h1, h2, mass)
            h1, h2 = h[1], h[2]
            step = second_of(v, a, mass)
            for c in range(3):
                rim[RIM.step(c, zs[n])] = step[c]
                if zs[n] in (0, 15):
                    rim[RIM.res(c, zs[n])] = (v[c] - FIRST * a[c])[:16]
            steps.append([FIRST * v[c] + step[c] for c in range(3)])
        return steps

    rim[RIM.code] = w[3, 1]
    _, u_first = rims(0, (-1, 0))
    u_last, u_after = rims(4, (15, 16))
    u_one = [FIRST * w[c, 3] + kept[KEPT.step(c, 1)] for c in range(3)]
    u_14 = [FIRST * w[c, 4] + kept[KEPT.step(c, 14)] for c in range(3)]
    for z in range(1, 14):
        out[z, :, 0:256] = kept[KEPT.stress(z)]
    out[0, :, 0:256] = stress_of(*u_first, u_one[1], u_one[2], core)
    out[14, :, 0:256] = stress_of(*u_14, u_last[1], u_last[2], core)
    out[15, :, 0:256] = stress_of(*u_last, u_after[1], u_after[2], core)

    lane = lax.broadcasted_iota(jnp.int32, (24, 128), 1)
    plane = (lane * 43) >> 8
    k = lane - 6 * plane
    right, left = [], []
    for c in range(4):
        r, l = kept[KEPT.strips(c, 0)], kept[KEPT.strips(c, 1)]
        for i, n in ((0, 0), (1, 1), (18, 6), (19, 7)):
            r, l = pack_plane(r, l, w[c, n], i, lane)
        empty = 0.0 if c < 3 else -1.0
        r = jnp.where(k < 4, r, empty)
        l = jnp.where(k > 1, l, empty)
        rim[RIM.strips(c, 0)] = r
        rim[RIM.strips(c, 1)] = l
        right.append(r)
        left.append(l)
    for msg, x in ((az_up, right), (az_dn, left)):
        msg[0] = jnp.where(
            k < 2, roll(x[2], -2, 1), jnp.where(k < 4, x[0], roll(x[1], 2, 1))
        )
        msg[1] = x[3]

    f = SECOND_A

    def partial(x):
        reluct, mass = materials(x[3])
        v = x[:3]
        h = strength(*v, roll(v[1], -6, 1), roll(v[2], -6, 1), reluct)
        a = image(v, h, roll(h[1], 6, 1), roll(h[2], 6, 1), mass)
        step = second_of(v, a, mass)
        u = [FIRST * v[c] + step[c] for c in range(3)]
        return reluct, h, u, fluxes(*u, roll(u[1], -6, 1), roll(u[2], -6, 1))

    reluct, (h0, h1, _), _, (flux1, flux2) = partial(right)
    fh1 = f * h1
    rest = f * ((roll(h0, -6, 1) - h0) + (roll(h1, -1, 0) - h1))
    rel_up, rel_dn = f * roll(reluct, -1, 0), f * roll(reluct, 1, 0)
    a_part = jnp.where(
        k < 2,
        roll(jnp.where(k == 3, flux1 - fh1, flux1), -2, 1),
        jnp.where(k == 2, roll(fh1, -1, 1), jnp.where(k < 5, roll(flux2, 1, 1), roll(rest, 2, 1))),
    )
    x_part = jnp.where(
        k == 1,
        -roll(rel_dn, -8, 1),
        jnp.where(k == 4, -roll(rel_up, 1, 1), jnp.where(k == 5, roll(rel_up, 2, 1), 0.0)),
    )
    z_part = jnp.where(k == 1, roll(rel_dn, -2, 1), 0.0)

    _, _, u, (flux1, flux2) = partial(left)
    v0, v1 = left[0], left[1]
    v1n = roll(v1, -6, 1)
    v1_dn = roll(v1, 1, 0)
    v0_up = roll(v0, -1, 0)
    inside = jnp.where(plane == 17, hi, 1.0)
    r_a = u[0] + f * ((roll(v0, -6, 1) + roll(v0, 6, 1)) - (3.0 + inside) * v0 + (v1n - v1))
    r_b = f * ((v1n - v1) + v0)
    b_part = jnp.where(
        k == 0,
        roll(f * v0, -2, 1),
        jnp.where(
            k == 1,
            roll(r_a, -1, 1),
            jnp.where(
                k == 2,
                flux1 + f * v0,
                jnp.where(k == 4, roll(r_b, 2, 1), jnp.where(k == 5, roll(flux2 - r_b, 3, 1), 0.0)),
            ),
        ),
    )
    y_part = jnp.where(
        k == 1, roll(v1_dn, -7, 1), jnp.where(k == 4, roll(v0_up, 2, 1), roll(v0_up, 3, 1))
    )
    w_part = roll(v1_dn, -1, 1)

    lane = lax.broadcasted_iota(jnp.int32, (8, 128), 1)
    group = lane >> 3
    parts = [
        (n, gap_tile(x, core))
        for n, x in ((0, a_part), (1, x_part), (2, z_part), (8, b_part), (9, y_part), (10, w_part))
    ]
    for z in range(16):
        extra = jnp.zeros((8, 128), F32)
        for n, part in parts:
            extra = jnp.where(group == n, roll(part, 8 * n - 6 * (z + 2), 1), extra)
        out[z, :, 256:384] = extra
    copy = pltpu.make_async_copy(out, hbm, sem.at[0])
    copy.start()
    copy.wait()


def edge_kernel(skew, kept, rim, sol_in, res_in, sol, out, table):
    offset = 256 * lax.broadcasted_iota(jnp.int32, (16, MH), 0) - skew[lax.axis_index("az")]
    turns = (offset * lax.broadcasted_iota(jnp.int32, (16, MH), 1)) & (NA - 1)
    angle = turns.astype(F32) * (2.0 * math.pi / NA)
    table[0] = jnp.cos(angle)
    table[1] = jnp.sin(angle)

    def step(z, c):
        return rim[RIM.step(c, z)] if z in (-1, 0, 15, 16) else kept[KEPT.step(c, z)]

    def materials_of(z):
        return materials(rim[RIM.code] if z < 0 else kept[KEPT.field(3, z)])

    def h_of(z):
        return strength(
            step(z, 0), step(z, 1), step(z, 2), step(z + 1, 1), step(z + 1, 2), materials_of(z)[0]
        )

    for z in (0, 14):
        _, h1, h2 = h_of(z - 1)
        for n in range(2):
            h = h_of(z + n)
            a = image([step(z + n, c) for c in range(3)], h, h1, h2, materials_of(z + n)[1])
            h1, h2 = h[1], h[2]
            for c in range(3):
                x = z + n
                before = rim[RIM.res(c, x)] if x in (0, 15) else kept[KEPT.res(c, x)]
                out[c, x] = before - a[c][:16]
    for c in range(3):
        out[c, 2:14] = res_in[c, 2:14]
        sol[c, 1:15] = sol_in[c, 1:15]
        for z in (0, 15):
            sol[c, z] = FIRST * kept[KEPT.field(c, z)][:16] + rim[RIM.step(c, z)][:16]


def seam_kernel(rim, sol_in, res_in, from_left, from_right, sol, res, a_sol, a_res, sems):
    lane = lax.broadcasted_iota(jnp.int32, (24, 128), 1)
    plane = (lane * 43) >> 8
    k = lane - 6 * plane

    def full(x, msg, halo, shifts):
        return [
            jnp.where(halo, roll(msg[t], shift, 1) if shift else msg[t], x[c])
            for c, (t, shift) in enumerate(zip((0, 0, 0, 1), shifts))
        ]

    def solve(x):
        reluct, mass = materials(x[3])
        v = x[:3]
        h = strength(*v, roll(v[1], -6, 1), roll(v[2], -6, 1), reluct)
        a = image(v, h, roll(h[1], 6, 1), roll(h[2], 6, 1), mass)
        step = second_of(v, a, mass)
        h = strength(*step, roll(step[1], -6, 1), roll(step[2], -6, 1), reluct)
        a2 = image(step, h, roll(h[1], 6, 1), roll(h[2], 6, 1), mass)
        return (
            [(FIRST * v[c] + step[c])[:16] for c in range(3)],
            [(v[c] - FIRST * a[c] - a2[c])[:16] for c in range(3)],
        )

    right = solve(full([rim[RIM.strips(c, 0)] for c in range(4)], from_right, k > 3, (2, 0, 4, 2)))
    left = solve(full([rim[RIM.strips(c, 1)] for c in range(4)], from_left, k < 2, (-2, -4, 0, -2)))
    lane = lax.broadcasted_iota(jnp.int32, (16, 128), 1)
    copies = []
    for z in range(16):
        i = z + 2
        for n, buf in ((0, a_sol), (1, a_res)):
            for c in range(3):
                x = (sol_in, res_in)[n][c, z]
                buf[z // 4, c, z % 4, :, 0:128] = jnp.where(
                    lane < 2, roll(left[n][c], -(6 * i + 2), 1), x[:, :128]
                )
                buf[z // 4, c, z % 4, :, 128:256] = jnp.where(
                    lane >= 126, roll(right[n][c], 124 - 6 * i, 1), x[:, 128:]
                )
        if z % 4 == 3:
            t = z // 4
            for n, (buf, dst) in enumerate(((a_sol, sol), (a_res, res))):
                copy = pltpu.make_async_copy(
                    buf.at[t], dst.at[:, pl.ds(4 * t, 4)], sems.at[n, t]
                )
                copy.start()
                copies.append(copy)
    for copy in copies:
        copy.wait()


def seam_call(*args):
    out = jax.ShapeDtypeStruct((3, 16, 16, 256), F32)
    return pl.pallas_call(
        seam_kernel,
        out_shape=[out, out],
        in_specs=[VMEM] * len(args),
        out_specs=[HBM] * 2,
        scratch_shapes=[
            pltpu.VMEM((4, 3, 4, 16, 256), F32),
            pltpu.VMEM((4, 3, 4, 16, 256), F32),
            pltpu.SemaphoreType.DMA((2, 4)),
        ],
        compiler_params=pltpu.CompilerParams(vmem_limit_bytes=12 * 2**20),
        cost_estimate=pl.CostEstimate(flops=4_000_000, bytes_accessed=4_000_000, transcendentals=0),
        name="seams",
    )(*args)


def harmonics_kernel(block, basis_hi, basis_lo, table, out):
    lane = lax.broadcasted_iota(jnp.int32, (16, 8, 128), 2)
    seam = block[:, :, 256:384]
    right = roll(jnp.concatenate([seam[1:], seam[:1]], axis=0).reshape(128, 128), 64, 1)
    seam = seam.reshape(128, 128)
    product = seam * right
    flux = seam + right + roll(product, -8, 1) + roll(product, -16, 1)
    square = 0.5 * (flux * flux)
    fixed = roll(square - roll(square, -3, 1), -2, 1).reshape(16, 8, 128)
    moved = jnp.concatenate([fixed[15:], fixed[:15]], axis=0)
    low = jnp.where(lane == 0, moved, block[:, :, 0:128])
    high = jnp.where(lane >= 126, fixed, block[:, :, 128:256])
    x = jnp.concatenate([low.reshape(128, 128), high.reshape(128, 128)], axis=1)
    x_hi = x.astype(jnp.bfloat16)
    x_lo = (x - x_hi.astype(F32)).astype(jnp.bfloat16)

    def dot(a, b):
        return jnp.dot(a, b[...], preferred_element_type=F32)

    local = dot(x_hi, basis_hi) + (dot(x_hi, basis_lo) + dot(x_lo, basis_hi))
    local = local.reshape(16, 8, 2 * MH)
    real = jnp.zeros((8, MH), F32)
    imag = jnp.zeros((8, MH), F32)
    for j in range(16):
        c, s = table[0, j : j + 1, :], table[1, j : j + 1, :]
        pc, ps = local[j, :, :MH], local[j, :, MH:]
        real = real + (pc * c - ps * s)
        imag = imag - (pc * s + ps * c)
    out[0, 0] = real
    out[1, 0] = imag


def harmonics_call(block, table):
    turns = np.arange(256)[:, None] * np.arange(MH)[None, :] / NA
    angle = 2.0 * math.pi * turns
    basis = np.concatenate([np.cos(angle), np.sin(angle)], axis=1) / math.sqrt(NA)
    hi = basis.astype(jnp.bfloat16)
    lo = (basis - hi.astype(np.float64)).astype(jnp.bfloat16)
    return pl.pallas_call(
        harmonics_kernel,
        out_shape=jax.ShapeDtypeStruct((2, 1, 8, MH), F32),
        in_specs=[VMEM] * 4,
        out_specs=VMEM,
        compiler_params=pltpu.CompilerParams(vmem_limit_bytes=8 * 2**20),
        cost_estimate=pl.CostEstimate(flops=100_000_000, bytes_accessed=1_000_000, transcendentals=0),
        name="harmonics",
    )(block, jnp.asarray(hi), jnp.asarray(lo), table)


def ring(axis, size, step):
    return functools.partial(
        lax.ppermute, axis_name=axis, perm=[(i, (i + step) % size) for i in range(size)]
    )


def on_device(source, region, skew_shift):
    n_az, n_ax = lax.axis_size("az"), lax.axis_size("ax")
    rad = lax.axis_index("rad")
    up, dn = send_call(source, region)
    (sw,) = call(
        beside_kernel, "beside", [(16, 8, 256)], [], 4, [VMEM, VMEM, pl.BlockSpec(memory_space=pl.ANY)], [VMEM]
    )(source, region, up)
    up = ring("ax", n_ax, 1)(up)
    dn = ring("ax", n_ax, -1)(dn)
    swap = ring("rad", 2, 1)
    sw = swap(sw)
    block, tall = (3, 16, 16, 256), (16, 24, 256)
    kept, flag, sol, res = call(
        inner_kernel,
        "inner",
        [(Kept.planes, 24, 256), (8, 128), block, block],
        [
            (4, *tall),
            (3, *tall),
            (3, *tall),
            block,
            block,
            pltpu.VMEM((16, 16, 256), jnp.int32),
            pltpu.SemaphoreType.DMA((4,)),
        ],
        16,
        [HBM, HBM, VMEM],
        [VMEM, VMEM, HBM, HBM],
    )(source, region, sw)
    start, flag = lax.optimization_barrier((8 * (1 - rad), flag))
    sw2 = swap(lax.dynamic_slice_in_dim(jnp.concatenate([up, dn], axis=0), start, 8, axis=1))
    stress, rim, az_up, az_dn = call(
        rim_kernel,
        "rim",
        [(16, 8, 384), (Rim.planes, 24, 256), (2, 24, 128), (2, 24, 128)],
        [(4, 8, 24, 256), (16, 8, 384), pltpu.SemaphoreType.DMA((1,))],
        8,
        [VMEM] * 4 + [pl.BlockSpec(memory_space=pl.ANY)],
        [HBM, VMEM, VMEM, VMEM],
    )(kept, up, dn, sw2, flag)
    circle = lax.all_to_all(stress, "az", split_axis=0, concat_axis=0, tiled=True)
    from_left = ring("az", n_az, 1)(az_up)
    from_right = ring("az", n_az, -1)(az_dn)
    sol, res, table = call(
        edge_kernel, "edge", [block, block, (2, 16, MH)], [], 8, [SMEM] + [VMEM] * 4, [VMEM] * 3
    )(skew_shift, kept, rim, sol, res)
    solution, residual = seam_call(rim, sol, res, from_left, from_right)
    harmonics = harmonics_call(circle, table)
    return (solution, residual, harmonics)


def solution(mesh):
    in_specs = (P(None, "ax", "rad", "az"), P("ax", "rad", "az"), P("ax"))
    out_specs = (
        P(None, "ax", "rad", "az"),
        P(None, "ax", "rad", "az"),
        P(None, ("ax", "az"), "rad", None),
    )
    return jax.shard_map(
        on_device, mesh=mesh, in_specs=in_specs, out_specs=out_specs, check_vma=False
    )
```

time: 133 us -> 38 us (0.29)
  the two profiles are of different devices: /device:TPU:5 before, /device:TPU:8 now
where the time goes in v2:
time: 38 us; the launch traced here: 37.8 us
  starting transfers between devices  20 us (53%)
  Pallas kernels  10.9 us (29%)
  waiting for transfers between devices  4 us (11%)
  local copies, waits for them, and re-layouts  2.03 us (5%)
  between operations  0.77 us (2%)
    all_to_all x1, starting transfers between devices, on_device(): lax.all_to_all(stress, 'az', split_axis=0, concat_axis=0, tiled=True)  9.96 us
    pallas_call x1, Pallas kernels, on_device(): call(inner_kernel, 'inner', [(Kept.planes, 24, 256), (8, 128), block, blo...  3.68 us
    ppermute x1, starting transfers between devices, on_device(): dn = ring('ax', n_ax, -1)(dn)  3.35 us
    ppermute x1, starting transfers between devices, on_device(): from_right = ring('az', n_az, -1)(az_dn)  2.67 us
    ppermute x1, starting transfers between devices, on_device(): up = ring('ax', n_ax, 1)(up)  2.37 us
    unnamed x14, local copies, waits for them, and re-layouts  2.03 us
    pallas_call x1, Pallas kernels, on_device(): call(rim_kernel, 'rim', [(16, 8, 384), (Rim.planes, 24, 256), (2, 24, 128...  1.77 us
    pallas_call x1, Pallas kernels, seam_call(): pl.pallas_call(seam_kernel, out_shape=[out, out], in_specs=[VMEM] * len(a...  1.7 us
  transfers between devices with their start and end apart: 7, of which 3 were waited for; matrix products, arithmetic and copies ran while one was open for 0% of the time, Pallas kernels for 16%

profile of v2, /device:TPU:8, one launch (start us, length us, event | category | flops | bytes accessed | tf_op | source)
XLA Modules:
  0.0 37.8 jit_solution(4862304899119868181)
XLA Ops:
  0.6 1.7 %send.1 = (f32[8,16,256]{2,1,0:T(8,128)S(1)}, f32[6,16,256]{2,1,0:T(8,128)}) custom-call(f32[3,16,16,256]{3,2,1,0:T(8,128)} %src.5, s32[16,16,256]{2,1,0:T(8,128)} %reg.5), custom_call_target="tpu_custom_call" | custom-call | tf_op jit(solution)/shard_map/send/pallas_call | solution.py:178
  2.4 0.1 beside.1
  2.5 0.1 collective-permute-start
  2.6 2.4 %collective-permute-start.1 = (f32[8,16,256]{2,1,0:T(8,128)S(1)}, f32[8,16,256]{2,1,0:T(8,128)S(1)}, u32[]{:S(2)}, u32[]{:S(2)}) collective-permute-start(f32[8,16,256]{2,1,0:T(8,128)S(1)} %get-tuple-element.20._), channel_id=1, source_target_pairs={{0,2},{2,4},{4,6},{6,8},{8,10},{10,12},{12,14},{14,0},{1,3},{3,5},... | collective-permute-start | bytes 393224 | tf_op jit(solution)/shard_map/ppermute | solution.py:623
  4.9 3.3 %collective-permute-start.2 = (f32[6,16,256]{2,1,0:T(8,128)}, f32[6,16,256]{2,1,0:T(8,128)S(1)}, u32[]{:S(2)}, u32[]{:S(2)}) collective-permute-start(f32[6,16,256]{2,1,0:T(8,128)} %get-tuple-element.22), channel_id=1, source_target_pairs={{0,14},{2,0},{4,2},{6,4},{8,6},{10,8},{12,10},{14,12},{1,15},{3,1}... | collective-permute-start | bytes 294920 | tf_op jit(solution)/shard_map/ppermute | solution.py:624
  8.3 3.7 %inner.1 = (f32[48,24,256]{2,1,0:T(8,128)S(1)}, f32[8,128]{1,0:T(8,128)S(1)}, f32[3,16,16,256]{3,2,1,0:T(8,128)S(1)}, f32[3,16,16,256]{3,2,1,0:T(8,128)S(1)}) custom-call(f32[3,16,16,256]{3,2,1,0:T(8,128)S(1)} %copy-done, s32[16,16,256]{2,1,0:T(8,128)S(1)} %copy-done.1, f32[16,8,256]{2,1,0:T(8,128)S(1)} %collective-permute-done.sw), custom_call_target="tpu_custom_call" | custom-call | flops 10000000 | bytes 2000000 | tf_op jit(solution)/shard_map/inner/pallas_call | solution.py:628
  12.0 0.0 copy-start.2
  12.0 0.9 %copy-done.2 = f32[3,16,16,256]{3,2,1,0:T(8,128)} copy-done((f32[3,16,16,256]{3,2,1,0:T(8,128)}, f32[3,16,16,256]{3,2,1,0:T(8,128)S(1)}, u32[]{:S(2)}) %copy-start.2) | copy-done | bytes 786456
  12.8 1.3 %collective-permute-done.2.dn = f32[6,16,256]{2,1,0:T(8,128)S(1)} collective-permute-done((f32[6,16,256]{2,1,0:T(8,128)}, f32[6,16,256]{2,1,0:T(8,128)S(1)}, u32[]{:S(2)}, u32[]{:S(2)}) %collective-permute-start.2) | collective-permute-done | bytes 98336 | tf_op jit(solution)/shard_map/ppermute | solution.py:624
  14.2 0.0 collective-permute-done.1.up
  14.2 0.1 collective-permute-start.3
  14.4 1.3 %collective-permute-done.3.sw2 = f32[14,8,256]{2,1,0:T(8,128)S(1)} collective-permute-done((f32[14,8,256]{2,1,0:T(8,128)S(1)}, f32[14,8,256]{2,1,0:T(8,128)S(1)}, u32[]{:S(2)}, u32[]{:S(2)}) %collective-permute-start.3) | collective-permute-done | bytes 114720 | tf_op jit(solution)/shard_map/ppermute | solution.py:646
  15.6 1.8 %rim.1 = (f32[16,8,384]{2,1,0:T(8,128)}, f32[23,24,256]{2,1,0:T(8,128)S(1)}, f32[2,24,128]{2,1,0:T(8,128)S(1)}, f32[2,24,128]{2,1,0:T(8,128)S(1)}) custom-call(f32[48,24,256]{2,1,0:T(8,128)S(1)} %get-tuple-element.21.kept, f32[8,16,256]{2,1,0:T(8,128)S(1)} %collective-permute-done.1.up, f32[6,16,256]{2,1,0:T(8,128)S(1)} %collective-permute-done.2.dn, ...), custom_call_target="tpu_custom_call" | custom-call | flops 10000000 | bytes 2000000 | tf_op jit(solution)/shard_map/rim/pallas_call | solution.py:647
  17.4 10.0 %all-to-all-start = ((f32[16,8,384]{2,1,0:T(8,128)}), f32[16,8,384]{2,1,0:T(8,128)S(1)}, u32[]{:S(2)}, u32[]{:S(2)}) async-start(f32[16,8,384]{2,1,0:T(8,128)} %get-tuple-element.35), calls=%async_computation | async-start | bytes 393216 | tf_op jit(solution)/shard_map/all_to_all | solution.py:656
  27.4 1.5 %collective-permute-start.4 = (f32[2,24,128]{2,1,0:T(8,128)S(1)}, f32[2,24,128]{2,1,0:T(8,128)S(1)}, u32[]{:S(2)}, u32[]{:S(2)}) collective-permute-start(f32[2,24,128]{2,1,0:T(8,128)S(1)} %get-tuple-element.31), channel_id=1, source_target_pairs={{0,16},{16,32},{32,48},{48,64},{64,80},{80,96},{96,112},{112,128},... | collective-permute-start | bytes 73736 | tf_op jit(solution)/shard_map/ppermute | solution.py:657
  28.8 2.7 %collective-permute-start.5 = (f32[2,24,128]{2,1,0:T(8,128)S(1)}, f32[2,24,128]{2,1,0:T(8,128)S(1)}, u32[]{:S(2)}, u32[]{:S(2)}) collective-permute-start(f32[2,24,128]{2,1,0:T(8,128)S(1)} %get-tuple-element.32), channel_id=1, source_target_pairs={{0,240},{16,0},{32,16},{48,32},{64,48},{80,64},{96,80},{112,96},{1... | collective-permute-start | bytes 73736 | tf_op jit(solution)/shard_map/ppermute | solution.py:658
  31.5 1.1 %copy-done.3 = f32[3,16,16,256]{3,2,1,0:T(8,128)S(1)} copy-done((f32[3,16,16,256]{3,2,1,0:T(8,128)S(1)}, f32[3,16,16,256]{3,2,1,0:T(8,128)}, u32[]{:S(2)}) %copy-start.3) | copy-done | bytes 786456
  32.7 0.8 %edge.1 = (f32[3,16,16,256]{3,2,1,0:T(8,128)S(1)}, f32[3,16,16,256]{3,2,1,0:T(8,128)S(1)}, f32[2,16,256]{2,1,0:T(8,128)S(1)}) custom-call(s32[16]{0:T(128)S(1)} %copy-done.6, f32[48,24,256]{2,1,0:T(8,128)S(1)} %get-tuple-element.21.kept, f32[23,24,256]{2,1,0:T(8,128)S(1)} %get-tuple-element.26.rim, f32[3,16,16,256]{3,2,1,0:T(8,128)S(1)} %get-tuple-element.27.sol_in, ...), custom_call_target="tpu_custom_call" | custom-call | flops 10000000 | bytes 2000000 | tf_op jit(solution)/shard_map/edge/pallas_call | solution.py:659
  33.5 0.0 copy-start.4
  33.5 0.0 copy-start.5
  33.5 1.4 %collective-permute-done.4.from_left = f32[2,24,128]{2,1,0:T(8,128)S(1)} collective-permute-done((f32[2,24,128]{2,1,0:T(8,128)S(1)}, f32[2,24,128]{2,1,0:T(8,128)S(1)}, u32[]{:S(2)}, u32[]{:S(2)}) %collective-permute-start.4) | collective-permute-done | bytes 24608 | tf_op jit(solution)/shard_map/ppermute | solution.py:657
  34.9 1.7 %seams.1 = (f32[3,16,16,256]{3,2,1,0:T(8,128)}, f32[3,16,16,256]{3,2,1,0:T(8,128)}) custom-call(f32[23,24,256]{2,1,0:T(8,128)S(1)} %get-tuple-element.26.rim, f32[3,16,16,256]{3,2,1,0:T(8,128)S(1)} %get-tuple-element.29.sol_in, f32[3,16,16,256]{3,2,1,0:T(8,128)S(1)} %get-tuple-element.30.res_in, f32[2,24,128]{2,1,0:T(8,128)S(1)} %collective-permute-done.4.from_left, ...), custom_call_target="tpu_custom_call" | custom-call | flops 4000000 | bytes 4000000 | tf_op jit(solution)/shard_map/seams/pallas_call | solution.py:545
  36.6 0.0 all-to-all-done.block
  36.6 1.1 %harmonics.1 = f32[2,1,8,256]{3,2,1,0:T(8,128)} custom-call(f32[16,8,384]{2,1,0:T(8,128)S(1)} %all-to-all-done.block, bf16[256,512]{1,0:T(8,128)(2,1)S(1)} %copy-done.5, bf16[256,512]{1,0:T(8,128)(2,1)S(1)} %copy-done.4, f32[2,16,256]{2,1,0:T(8,128)S(1)} %get-tuple-element.36.table), custom_call_target="tpu_custom_call" | custom-call | flops 100000000 | bytes 1000000 | tf_op jit(solution)/shard_map/harmonics/pallas_call | solution.py:599
  (12 shorter events, 0.1 us)
Async XLA Ops:
  0.6 1.7 %copy-start.1 = (s32[16,16,256]{2,1,0:T(8,128)S(1)}, s32[16,16,256]{2,1,0:T(8,128)}, u32[]{:S(2)}) copy-start(s32[16,16,256]{2,1,0:T(8,128)} %reg.5) | copy-start | bytes 786436
  0.6 1.7 %copy-start = (f32[3,16,16,256]{3,2,1,0:T(8,128)S(1)}, f32[3,16,16,256]{3,2,1,0:T(8,128)}, u32[]{:S(2)}) copy-start(f32[3,16,16,256]{3,2,1,0:T(8,128)} %src.5) | copy-start | bytes 2359300
  2.5 5.8 %collective-permute-start = (f32[16,8,256]{2,1,0:T(8,128)S(1)}, f32[16,8,256]{2,1,0:T(8,128)S(1)}, u32[]{:S(2)}, u32[]{:S(2)}) collective-permute-start(f32[16,8,256]{2,1,0:T(8,128)S(1)} %beside.1), channel_id=1, source_target_pairs={{0,1},{1,0},{2,3},{3,2},{4,5},{5,4},{6,7},{7,6},{8,9},{9,8},{10,11... | collective-permute-start | bytes 393224 | tf_op jit(solution)/shard_map/ppermute | solution.py:626
  2.6 11.6 %collective-permute-start.1 = (f32[8,16,256]{2,1,0:T(8,128)S(1)}, f32[8,16,256]{2,1,0:T(8,128)S(1)}, u32[]{:S(2)}, u32[]{:S(2)}) collective-permute-start(f32[8,16,256]{2,1,0:T(8,128)S(1)} %get-tuple-element.20._), channel_id=1, source_target_pairs={{0,2},{2,4},{4,6},{6,8},{8,10},{10,12},{12,14},{14,0},{1,3},{3,5},... | collective-permute-start | bytes 393224 | tf_op jit(solution)/shard_map/ppermute | solution.py:623
  4.9 9.3 %collective-permute-start.2 = (f32[6,16,256]{2,1,0:T(8,128)}, f32[6,16,256]{2,1,0:T(8,128)S(1)}, u32[]{:S(2)}, u32[]{:S(2)}) collective-permute-start(f32[6,16,256]{2,1,0:T(8,128)} %get-tuple-element.22), channel_id=1, source_target_pairs={{0,14},{2,0},{4,2},{6,4},{8,6},{10,8},{12,10},{14,12},{1,15},{3,1}... | collective-permute-start | bytes 294920 | tf_op jit(solution)/shard_map/ppermute | solution.py:624
  12.0 0.9 %copy-start.2 = (f32[3,16,16,256]{3,2,1,0:T(8,128)}, f32[3,16,16,256]{3,2,1,0:T(8,128)S(1)}, u32[]{:S(2)}) copy-start(f32[3,16,16,256]{3,2,1,0:T(8,128)S(1)} %get-tuple-element.28.res_in) | copy-start | bytes 2359300
  12.8 18.7 %copy-start.6 = (s32[16]{0:T(128)S(1)}, s32[16]{0:T(128)}, u32[]{:S(2)}) copy-start(s32[16]{0:T(128)} %skew.1) | copy-start | bytes 196
  14.2 1.4 %collective-permute-start.3 = (f32[14,8,256]{2,1,0:T(8,128)S(1)}, f32[14,8,256]{2,1,0:T(8,128)S(1)}, u32[]{:S(2)}, u32[]{:S(2)}) collective-permute-start(f32[14,8,256]{2,1,0:T(8,128)S(1)} %fusion), channel_id=1, source_target_pairs={{0,1},{1,0},{2,3},{3,2},{4,5},{5,4},{6,7},{7,6},{8,9},{9,8},{10,11... | collective-permute-start | bytes 344072 | tf_op jit(solution)/shard_map/ppermute | solution.py:646
  17.4 19.2 %all-to-all-start = ((f32[16,8,384]{2,1,0:T(8,128)}), f32[16,8,384]{2,1,0:T(8,128)S(1)}, u32[]{:S(2)}, u32[]{:S(2)}) async-start(f32[16,8,384]{2,1,0:T(8,128)} %get-tuple-element.35), calls=%async_computation | async-start | bytes 393216 | tf_op jit(solution)/shard_map/all_to_all | solution.py:656
  27.4 7.5 %collective-permute-start.4 = (f32[2,24,128]{2,1,0:T(8,128)S(1)}, f32[2,24,128]{2,1,0:T(8,128)S(1)}, u32[]{:S(2)}, u32[]{:S(2)}) collective-permute-start(f32[2,24,128]{2,1,0:T(8,128)S(1)} %get-tuple-element.31), channel_id=1, source_target_pairs={{0,16},{16,32},{32,48},{48,64},{64,80},{80,96},{96,112},{112,128},... | collective-permute-start | bytes 73736 | tf_op jit(solution)/shard_map/ppermute | solution.py:657
  28.8 6.0 %collective-permute-start.5 = (f32[2,24,128]{2,1,0:T(8,128)S(1)}, f32[2,24,128]{2,1,0:T(8,128)S(1)}, u32[]{:S(2)}, u32[]{:S(2)}) collective-permute-start(f32[2,24,128]{2,1,0:T(8,128)S(1)} %get-tuple-element.32), channel_id=1, source_target_pairs={{0,240},{16,0},{32,16},{48,32},{64,48},{80,64},{96,80},{112,96},{1... | collective-permute-start | bytes 73736 | tf_op jit(solution)/shard_map/ppermute | solution.py:658
  31.5 1.1 %copy-start.3 = (f32[3,16,16,256]{3,2,1,0:T(8,128)S(1)}, f32[3,16,16,256]{3,2,1,0:T(8,128)}, u32[]{:S(2)}) copy-start(f32[3,16,16,256]{3,2,1,0:T(8,128)} %copy-done.2) | copy-start | bytes 2359300
  33.5 3.1 %copy-start.4 = (bf16[256,512]{1,0:T(8,128)(2,1)S(1)}, bf16[256,512]{1,0:T(8,128)(2,1)}, u32[]{:S(2)}) copy-start(bf16[256,512]{1,0:T(8,128)(2,1)} %constant.17.clone.basis_lo) | copy-start | bytes 786436
  33.5 3.1 %copy-start.5 = (bf16[256,512]{1,0:T(8,128)(2,1)S(1)}, bf16[256,512]{1,0:T(8,128)(2,1)}, u32[]{:S(2)}) copy-start(bf16[256,512]{1,0:T(8,128)(2,1)} %constant.16.clone.basis_hi) | copy-start | bytes 786436

commit v3 on v2

--- a/solution.py
+++ b/solution.py
@@ -31,7 +31,7 @@
 HBM = pl.BlockSpec(memory_space=pltpu.HBM)
 
 UNROLL = 2
-SEND_KIB = 54784
+SEND_KIB = 54656
 
 
 def materials(code):
@@ -154,55 +154,73 @@
     return right, left
 
 
-def send_kernel(src, reg, up, dn, rows, sems):
-    pairs = [
+def send_kernel(src, reg, up, dn, sw, rows, ids, tiles, sems):
+    core = lax.axis_index("rad")
+    tile = pl.ds(pl.multiple_of(8 * (1 - core), 8), 8)
+    pairs = [(reg.at[:, tile, :], ids)]
+    for c in range(3):
+        pairs.append((src.at[c, :, tile, :], tiles.at[c]))
+    later = [
         (reg.at[14:16], rows.at[0:2]),
         (reg.at[0], rows.at[2]),
         (src.at[1, 1], dn.at[4]),
         (src.at[2, 1], dn.at[5]),
     ]
     for c in range(3):
-        pairs.append((src.at[c, 14:16], up.at[2 * c : 2 * c + 2]))
-        pairs.append((src.at[c, 0], dn.at[c]))
-    copies = [pltpu.make_async_copy(x, y, sems.at[n]) for n, (x, y) in enumerate(pairs)]
+        later.append((src.at[c, 14:16], up.at[2 * c : 2 * c + 2]))
+        later.append((src.at[c, 0], dn.at[c]))
+    copies = [
+        pltpu.make_async_copy(x, y, sems.at[n]) for n, (x, y) in enumerate(pairs + later)
+    ]
     for copy in copies:
         copy.start()
-    for copy in copies:
+    for copy in copies[:4]:
+        copy.wait()
+    sub = lax.broadcasted_iota(jnp.int32, (16, 8, 256), 1) >> 1
+    packed = jnp.zeros((16, 8, 256), F32)
+    for c in range(4):
+        x = tiles[c] if c < 3 else ids[...].astype(F32)
+        first = pltpu.roll(x, 2 * c, 1) if c else x
+        last = pltpu.roll(x, (2 * c + 2) % 8, 1) if c < 3 else x
+        packed = jnp.where(sub == c, jnp.where(core == 1, first, last), packed)
+    sw[...] = packed
+    for copy in copies[4:]:
         copy.wait()
     up[6:8] = rows[0:2].astype(F32)
     dn[3] = rows[2].astype(F32)
 
 
 def send_call(src, reg):
-    shapes = [(8, 16, 256), (6, 16, 256)]
+    shapes = [(8, 16, 256), (6, 16, 256), (16, 8, 256)]
     return pl.pallas_call(
         send_kernel,
         out_shape=[jax.ShapeDtypeStruct(shape, F32) for shape in shapes],
         in_specs=[HBM, HBM],
-        out_specs=[VMEM] * 2,
-        scratch_shapes=[pltpu.VMEM((3, 16, 256), jnp.int32), pltpu.SemaphoreType.DMA((10,))],
+        out_specs=[VMEM] * 3,
+        scratch_shapes=[
+            pltpu.VMEM((3, 16, 256), jnp.int32),
+            pltpu.VMEM((16, 8, 256), jnp.int32),
+            pltpu.VMEM((3, 16, 8, 256), F32),
+            pltpu.SemaphoreType.DMA((14,)),
+        ],
         compiler_params=pltpu.CompilerParams(vmem_limit_bytes=SEND_KIB * 2**10),
         name="send",
     )(src, reg)
 
 
-def beside_kernel(src, reg, _, sw):
-    core = lax.axis_index("rad")
-    tile = pl.ds(pl.multiple_of(8 * (1 - core), 8), 8)
-    sub = lax.broadcasted_iota(jnp.int32, (16, 8, 256), 1) >> 1
-    packed = jnp.zeros((16, 8, 256), F32)
-    for c in range(4):
-        rows = src[c, :, tile, :] if c < 3 else reg[:, tile, :].astype(F32)
-        first = pltpu.roll(rows, 2 * c, 1) if c else rows
-        last = pltpu.roll(rows, (2 * c + 2) % 8, 1) if c < 3 else rows
-        packed = jnp.where(sub == c, jnp.where(core == 1, first, last), packed)
-    sw[...] = packed
+def partner_rows(packed, c, core):
+    first = roll(packed, -2 * c, 0) if c else packed
+    last = roll(packed, 6 - 2 * c, 0) if c < 3 else packed
+    return jnp.where(core == 1, last, first)
 
 
 def call(kernel, name, outs, scratch, limit, in_specs, out_specs):
     return pl.pallas_call(
         kernel,
-        out_shape=[jax.ShapeDtypeStruct(shape, F32) for shape in outs],
+        out_shape=[
+            pltpu.HBM(shape, F32) if spec is HBM else jax.ShapeDtypeStruct(shape, F32)
+            for shape, spec in zip(outs, out_specs)
+        ],
         in_specs=in_specs,
         out_specs=out_specs,
         scratch_shapes=[pltpu.VMEM(x, F32) if isinstance(x, tuple) else x for x in scratch],
@@ -212,8 +230,7 @@
     )
 
 
-def inner_kernel(src, reg, sw, kept, flag, sol_out, res_out, field, s, hh, sol, res, ids, sems):
-    flag[...] = jnp.zeros(flag.shape, F32)
+def inner_kernel(src, reg, sw, kept, sol_out, res_out, field, s, hh, sol, res, ids, sems):
     core = lax.axis_index("rad")
     pick = from_partner((8, 256), core)
     lane = lax.broadcasted_iota(jnp.int32, (24, 128), 1)
@@ -226,9 +243,7 @@
 
     def assemble(z):
         for c in range(4):
-            first = roll(sw[z], -2 * c, 0) if c else sw[z]
-            last = roll(sw[z], 6 - 2 * c, 0) if c < 3 else sw[z]
-            rows = jnp.where(core == 1, last, first)
+            rows = partner_rows(sw[z], c, core)
             field[c, z, 16:24, :] = jnp.where(pick, rows, 0.0 if c < 3 else -1.0)
         field[3, z, 0:16, :] = ids[z].astype(F32)
 
@@ -306,7 +321,7 @@
         copy.wait()
 
 
-def rim_kernel(kept, up, dn, sw2, _, hbm, rim, az_up, az_dn, w, out, sem):
+def rim_kernel(kept, up, dn, hbm, az_up, az_dn, rim, w, out, up_msg, dn_msg, sem):
     core, ax = lax.axis_index("rad"), lax.axis_index("ax")
     lo = jnp.where(ax > 0, 1.0, 0.0)
     hi = jnp.where(ax < lax.axis_size("ax") - 1, 1.0, 0.0)
@@ -318,11 +333,11 @@
             w[c, i, 0:16, :] = (value - empty) * valid + empty
             w[c, i, 16:24, :] = jnp.where(pick, (beside - empty) * valid + empty, empty)
 
-        put(0, up[2 * c], sw2[2 * c], lo)
-        put(1, up[2 * c + 1], sw2[2 * c + 1], lo)
-        put(6, dn[c], sw2[8 + c], hi)
+        put(0, up[2 * c], partner_rows(up[8, 0:8], c, core), lo)
+        put(1, up[2 * c + 1], partner_rows(up[8, 8:16], c, core), lo)
+        put(6, dn[c], partner_rows(dn[6, 0:8], c, core), hi)
         if c in (1, 2):
-            put(7, dn[3 + c], sw2[11 + c], hi)
+            put(7, dn[3 + c], partner_rows(dn[6, 8:16], c, core), hi)
         else:
             w[c, 7] = jnp.full((24, 256), empty, F32)
         w[c, 2] = kept[KEPT.field(c, 0)]
@@ -363,6 +378,9 @@
     out[0, :, 0:256] = stress_of(*u_first, u_one[1], u_one[2], core)
     out[14, :, 0:256] = stress_of(*u_14, u_last[1], u_last[2], core)
     out[15, :, 0:256] = stress_of(*u_last, u_after[1], u_after[2], core)
+    main, last = [slice(0, 256), slice(256, 384)]
+    copies = [pltpu.make_async_copy(out.at[:, :, main], hbm.at[:, :, main], sem.at[0])]
+    copies[0].start()
 
     lane = lax.broadcasted_iota(jnp.int32, (24, 128), 1)
     plane = (lane * 43) >> 8
@@ -379,11 +397,15 @@
         rim[RIM.strips(c, 1)] = l
         right.append(r)
         left.append(l)
-    for msg, x in ((az_up, right), (az_dn, left)):
+    for msg, x in ((up_msg, right), (dn_msg, left)):
         msg[0] = jnp.where(
             k < 2, roll(x[2], -2, 1), jnp.where(k < 4, x[0], roll(x[1], 2, 1))
         )
         msg[1] = x[3]
+    copies.append(pltpu.make_async_copy(up_msg, az_up, sem.at[1]))
+    copies.append(pltpu.make_async_copy(dn_msg, az_dn, sem.at[2]))
+    copies[1].start()
+    copies[2].start()
 
     f = SECOND_A
 
@@ -439,19 +461,20 @@
     w_part = roll(v1_dn, -1, 1)
 
     lane = lax.broadcasted_iota(jnp.int32, (8, 128), 1)
-    group = lane >> 3
     parts = [
-        (n, gap_tile(x, core))
-        for n, x in ((0, a_part), (1, x_part), (2, z_part), (8, b_part), (9, y_part), (10, w_part))
+        roll(gap_tile(x, core), 6 * n, 1) if n else gap_tile(x, core)
+        for n, x in enumerate((a_part, x_part, z_part, b_part, y_part, w_part))
     ]
     for z in range(16):
-        extra = jnp.zeros((8, 128), F32)
-        for n, part in parts:
-            extra = jnp.where(group == n, roll(part, 8 * n - 6 * (z + 2), 1), extra)
+        part = (((lane - 6 * (z + 2)) & 127) * 43) >> 8
+        extra = parts[5]
+        for n in range(5):
+            extra = jnp.where(part == n, parts[n], extra)
         out[z, :, 256:384] = extra
-    copy = pltpu.make_async_copy(out, hbm, sem.at[0])
-    copy.start()
-    copy.wait()
+    copies.append(pltpu.make_async_copy(out.at[:, :, last], hbm.at[:, :, last], sem.at[3]))
+    copies[3].start()
+    for copy in copies:
+        copy.wait()
 
 
 def edge_kernel(skew, kept, rim, sol_in, res_in, sol, out, table):
@@ -515,6 +538,10 @@
 
     right = solve(full([rim[RIM.strips(c, 0)] for c in range(4)], from_right, k > 3, (2, 0, 4, 2)))
     left = solve(full([rim[RIM.strips(c, 1)] for c in range(4)], from_left, k < 2, (-2, -4, 0, -2)))
+    k = k[:16]
+    merged = [
+        [jnp.where(k < 4, right[n][c], roll(left[n][c], 2, 1)) for c in range(3)] for n in range(2)
+    ]
     lane = lax.broadcasted_iota(jnp.int32, (16, 128), 1)
     copies = []
     for z in range(16):
@@ -522,12 +549,9 @@
         for n, buf in ((0, a_sol), (1, a_res)):
             for c in range(3):
                 x = (sol_in, res_in)[n][c, z]
-                buf[z // 4, c, z % 4, :, 0:128] = jnp.where(
-                    lane < 2, roll(left[n][c], -(6 * i + 2), 1), x[:, :128]
-                )
-                buf[z // 4, c, z % 4, :, 128:256] = jnp.where(
-                    lane >= 126, roll(right[n][c], 124 - 6 * i, 1), x[:, 128:]
-                )
+                edge = roll(merged[n][c], 124 - 6 * i, 1)
+                buf[z // 4, c, z % 4, :, 0:128] = jnp.where(lane < 2, edge, x[:, :128])
+                buf[z // 4, c, z % 4, :, 128:256] = jnp.where(lane >= 126, edge, x[:, 128:])
         if z % 4 == 3:
             t = z // 4
             for n, (buf, dst) in enumerate(((a_sol, sol), (a_res, res))):
@@ -561,10 +585,12 @@
 def harmonics_kernel(block, basis_hi, basis_lo, table, out):
     lane = lax.broadcasted_iota(jnp.int32, (16, 8, 128), 2)
     seam = block[:, :, 256:384]
-    right = roll(jnp.concatenate([seam[1:], seam[:1]], axis=0).reshape(128, 128), 64, 1)
-    seam = seam.reshape(128, 128)
+    right = jnp.concatenate([seam[1:], seam[:1]], axis=0).reshape(128, 128)
+    first = 6 * (lax.axis_index("az") + 2)
+    right = pltpu.roll(right, lax.rem(256 - first - 18, 128), 1)
+    seam = pltpu.roll(seam.reshape(128, 128), lax.rem(256 - first, 128), 1)
     product = seam * right
-    flux = seam + right + roll(product, -8, 1) + roll(product, -16, 1)
+    flux = seam + right + roll(product, -6, 1) + roll(product, -12, 1)
     square = 0.5 * (flux * flux)
     fixed = roll(square - roll(square, -3, 1), -2, 1).reshape(16, 8, 128)
     moved = jnp.concatenate([fixed[15:], fixed[:15]], axis=0)
@@ -577,7 +603,8 @@
     def dot(a, b):
         return jnp.dot(a, b[...], preferred_element_type=F32)
 
-    local = dot(x_hi, basis_hi) + (dot(x_hi, basis_lo) + dot(x_lo, basis_hi))
+    both = dot(jnp.concatenate([x_hi, x_lo], axis=0), basis_hi)
+    local = both[:128] + (both[128:] + dot(x_hi, basis_lo))
     local = local.reshape(16, 8, 2 * MH)
     real = jnp.zeros((8, MH), F32)
     imag = jnp.zeros((8, MH), F32)
@@ -615,20 +642,15 @@
 
 def on_device(source, region, skew_shift):
     n_az, n_ax = lax.axis_size("az"), lax.axis_size("ax")
-    rad = lax.axis_index("rad")
-    up, dn = send_call(source, region)
-    (sw,) = call(
-        beside_kernel, "beside", [(16, 8, 256)], [], 4, [VMEM, VMEM, pl.BlockSpec(memory_space=pl.ANY)], [VMEM]
-    )(source, region, up)
-    up = ring("ax", n_ax, 1)(up)
-    dn = ring("ax", n_ax, -1)(dn)
-    swap = ring("rad", 2, 1)
-    sw = swap(sw)
+    up, dn, sw = send_call(source, region)
+    sw = ring("rad", 2, 1)(sw)
+    up = ring("ax", n_ax, 1)(jnp.concatenate([up, sw[14:16].reshape(1, 16, 256)], axis=0))
+    dn = ring("ax", n_ax, -1)(jnp.concatenate([dn, sw[0:2].reshape(1, 16, 256)], axis=0))
     block, tall = (3, 16, 16, 256), (16, 24, 256)
-    kept, flag, sol, res = call(
+    kept, sol, res = call(
         inner_kernel,
         "inner",
-        [(Kept.planes, 24, 256), (8, 128), block, block],
+        [(Kept.planes, 24, 256), block, block],
         [
             (4, *tall),
             (3, *tall),
@@ -640,19 +662,23 @@
         ],
         16,
         [HBM, HBM, VMEM],
-        [VMEM, VMEM, HBM, HBM],
+        [VMEM, HBM, HBM],
     )(source, region, sw)
-    start, flag = lax.optimization_barrier((8 * (1 - rad), flag))
-    sw2 = swap(lax.dynamic_slice_in_dim(jnp.concatenate([up, dn], axis=0), start, 8, axis=1))
-    stress, rim, az_up, az_dn = call(
+    stress, az_up, az_dn, rim = call(
         rim_kernel,
         "rim",
-        [(16, 8, 384), (Rim.planes, 24, 256), (2, 24, 128), (2, 24, 128)],
-        [(4, 8, 24, 256), (16, 8, 384), pltpu.SemaphoreType.DMA((1,))],
+        [(16, 8, 384), (2, 24, 128), (2, 24, 128), (Rim.planes, 24, 256)],
+        [
+            (4, 8, 24, 256),
+            (16, 8, 384),
+            (2, 24, 128),
+            (2, 24, 128),
+            pltpu.SemaphoreType.DMA((4,)),
+        ],
         8,
-        [VMEM] * 4 + [pl.BlockSpec(memory_space=pl.ANY)],
-        [HBM, VMEM, VMEM, VMEM],
-    )(kept, up, dn, sw2, flag)
+        [VMEM] * 3,
+        [HBM, HBM, HBM, VMEM],
+    )(kept, up, dn)
     circle = lax.all_to_all(stress, "az", split_axis=0, concat_axis=0, tiled=True)
     from_left = ring("az", n_az, 1)(az_up)
     from_right = ring("az", n_az, -1)(az_dn)

time: 38 us -> 37.4 us (0.984)
  local copies, waits for them, and re-layouts: 2.03 us -> 0.04 us
  waiting for transfers between devices: 4 us -> 5.49 us
    unnamed x14, local copies, waits for them, and re-layouts: 2.03 us -> 0.04 us
    ppermute x1, waiting for transfers between devices: 1.37 us -> 2.3 us  [on_device(): from_left = ring('az', n_az, 1)(az_up)]
    ppermute x4 -> x3, waiting for transfers between devices: 2.63 us -> 3.19 us  [the longest x1 1.85 us: on_device(): ring('ax', n_ax, -1)]
    pallas_call x3 -> x2, Pallas kernels: 5.53 us -> 5.75 us  [the longest x1 4.34 us: on_device(): call(inner_kernel, 'inner', [(Kept.planes, 24, 256), block, block], [(4,...]
    ppermute x4 -> x3, starting transfers between devices: 5.94 us -> 5.89 us  [the longest x1 3.42 us: on_device(): ring('ax', n_ax, -1)]
  transfers between devices with their start and end apart: 7 -> 6, of which waited for: 3 -> 3; matrix products, arithmetic and copies ran while one was open for 0% -> 0% of each run, Pallas kernels for 16% -> 19%
where the time goes in v3:
time: 37.4 us; the launch traced here: 37.2 us
  starting transfers between devices  20 us (53%)
  Pallas kernels  10.9 us (29%)
  waiting for transfers between devices  5.49 us (15%)
  between operations  0.77 us (2%)
    all_to_all x1, starting transfers between devices, on_device(): lax.all_to_all(stress, 'az', split_axis=0, concat_axis=0, tiled=True)  9.96 us
    pallas_call x1, Pallas kernels, on_device(): call(inner_kernel, 'inner', [(Kept.planes, 24, 256), block, block], [(4,...  4.34 us
    ppermute x1, starting transfers between devices, on_device(): ring('ax', n_ax, -1)  3.42 us
    ppermute x1, starting transfers between devices, on_device(): from_right = ring('az', n_az, -1)(az_dn)  2.67 us
    ppermute x1, starting transfers between devices, on_device(): ring('ax', n_ax, 1)  2.37 us
    ppermute x1, waiting for transfers between devices, on_device(): from_left = ring('az', n_az, 1)(az_up)  2.3 us
    ppermute x1, waiting for transfers between devices, on_device(): ring('ax', n_ax, -1)  1.85 us
    pallas_call x1, Pallas kernels, seam_call(): pl.pallas_call(seam_kernel, out_shape=[out, out], in_specs=[VMEM] * len(a...  1.81 us
  transfers between devices with their start and end apart: 6, of which 3 were waited for; matrix products, arithmetic and copies ran while one was open for 0% of the time, Pallas kernels for 19%

profile of v3, /device:TPU:8, one launch (start us, length us, event | category | flops | bytes accessed | tf_op | source)
XLA Modules:
  0.0 37.2 jit_solution(3488913907884472873)
XLA Ops:
  0.6 0.0 copy-start.1
  0.6 1.4 %send.1 = (f32[8,16,256]{2,1,0:T(8,128)S(1)}, f32[6,16,256]{2,1,0:T(8,128)S(1)}, f32[16,8,256]{2,1,0:T(8,128)S(1)}) custom-call(f32[3,16,16,256]{3,2,1,0:T(8,128)} %src.3, s32[16,16,256]{2,1,0:T(8,128)} %reg.3), custom_call_target="tpu_custom_call" | custom-call | tf_op jit(solution)/shard_map/send/pallas_call | solution.py:195
  2.1 0.1 collective-permute-start
  2.2 1.3 %collective-permute-done.sw = f32[16,8,256]{2,1,0:T(8,128)S(1)} collective-permute-done((f32[16,8,256]{2,1,0:T(8,128)S(1)}, f32[16,8,256]{2,1,0:T(8,128)S(1)}, u32[]{:S(2)}, u32[]{:S(2)}) %collective-permute-start) | collective-permute-done | bytes 131104 | tf_op jit(solution)/shard_map/ppermute | solution.py:646
  3.5 2.4 %collective-permute-start.1 = (f32[9,16,256]{2,1,0:T(8,128)S(1)}, f32[9,16,256]{2,1,0:T(8,128)S(1)}, u32[]{:S(2)}, u32[]{:S(2)}) collective-permute-start(f32[9,16,256]{2,1,0:T(8,128)S(1)} %pad_maximum_fusion), channel_id=1, source_target_pairs={{0,2},{2,4},{4,6},{6,8},{8,10},{10,12},{12,14},{14,0},{1,3},{3,5},... | collective-permute-start | bytes 442376 | tf_op jit(solution)/shard_map/ppermute | solution.py:647
  5.9 3.4 %collective-permute-start.2 = (f32[7,16,256]{2,1,0:T(8,128)S(1)}, f32[7,16,256]{2,1,0:T(8,128)S(1)}, u32[]{:S(2)}, u32[]{:S(2)}) collective-permute-start(f32[7,16,256]{2,1,0:T(8,128)S(1)} %pad_maximum_fusion.1), channel_id=1, source_target_pairs={{0,14},{2,0},{4,2},{6,4},{8,6},{10,8},{12,10},{14,12},{1,15},{3,1}... | collective-permute-start | bytes 344072 | tf_op jit(solution)/shard_map/ppermute | solution.py:648
  9.3 4.3 %inner.1 = (f32[48,24,256]{2,1,0:T(8,128)S(1)}, f32[3,16,16,256]{3,2,1,0:T(8,128)}, f32[3,16,16,256]{3,2,1,0:T(8,128)}) custom-call(f32[3,16,16,256]{3,2,1,0:T(8,128)S(1)} %copy-done, s32[16,16,256]{2,1,0:T(8,128)S(1)} %copy-done.1, f32[16,8,256]{2,1,0:T(8,128)S(1)} %collective-permute-done.sw), custom_call_target="tpu_custom_call" | custom-call | flops 10000000 | bytes 2000000 | tf_op jit(solution)/shard_map/inner/pallas_call | solution.py:650
  13.7 0.0 copy-start.2
  13.7 0.0 copy-start.3
  13.7 0.0 copy-start.6
  13.7 1.9 %collective-permute-done.2.dn = f32[7,16,256]{2,1,0:T(8,128)S(1)} collective-permute-done((f32[7,16,256]{2,1,0:T(8,128)S(1)}, f32[7,16,256]{2,1,0:T(8,128)S(1)}, u32[]{:S(2)}, u32[]{:S(2)}) %collective-permute-start.2) | collective-permute-done | bytes 114720 | tf_op jit(solution)/shard_map/ppermute | solution.py:648
  15.6 0.0 collective-permute-done.1.up
  15.6 1.4 %rim.1 = (f32[16,8,384]{2,1,0:T(8,128)}, f32[2,24,128]{2,1,0:T(8,128)}, f32[2,24,128]{2,1,0:T(8,128)}, f32[23,24,256]{2,1,0:T(8,128)S(1)}) custom-call(f32[48,24,256]{2,1,0:T(8,128)S(1)} %get-tuple-element.19.kept, f32[9,16,256]{2,1,0:T(8,128)S(1)} %collective-permute-done.1.up, f32[7,16,256]{2,1,0:T(8,128)S(1)} %collective-permute-done.2.dn), custom_call_target="tpu_custom_call" | custom-call | flops 10000000 | bytes 2000000 | tf_op jit(solution)/shard_map/rim/pallas_call | solution.py:667
  17.0 10.0 %all-to-all-start = ((f32[16,8,384]{2,1,0:T(8,128)}), f32[16,8,384]{2,1,0:T(8,128)S(1)}, u32[]{:S(2)}, u32[]{:S(2)}) async-start(f32[16,8,384]{2,1,0:T(8,128)} %get-tuple-element.31), calls=%async_computation | async-start | bytes 393216 | tf_op jit(solution)/shard_map/all_to_all | solution.py:682
  26.9 1.5 %collective-permute-start.3 = (f32[2,24,128]{2,1,0:T(8,128)}, f32[2,24,128]{2,1,0:T(8,128)S(1)}, u32[]{:S(2)}, u32[]{:S(2)}) collective-permute-start(f32[2,24,128]{2,1,0:T(8,128)} %get-tuple-element.27), channel_id=1, source_target_pairs={{0,16},{16,32},{32,48},{48,64},{64,80},{80,96},{96,112},{112,128},... | collective-permute-start | bytes 73736 | tf_op jit(solution)/shard_map/ppermute | solution.py:683
  28.4 2.7 %collective-permute-start.4 = (f32[2,24,128]{2,1,0:T(8,128)}, f32[2,24,128]{2,1,0:T(8,128)S(1)}, u32[]{:S(2)}, u32[]{:S(2)}) collective-permute-start(f32[2,24,128]{2,1,0:T(8,128)} %get-tuple-element.28), channel_id=1, source_target_pairs={{0,240},{16,0},{32,16},{48,32},{64,48},{80,64},{96,80},{112,96},{1... | collective-permute-start | bytes 73736 | tf_op jit(solution)/shard_map/ppermute | solution.py:684
  31.1 0.8 %edge.1 = (f32[3,16,16,256]{3,2,1,0:T(8,128)S(1)}, f32[3,16,16,256]{3,2,1,0:T(8,128)S(1)}, f32[2,16,256]{2,1,0:T(8,128)S(1)}) custom-call(s32[16]{0:T(128)S(1)} %copy-done.6, f32[48,24,256]{2,1,0:T(8,128)S(1)} %get-tuple-element.19.kept, f32[23,24,256]{2,1,0:T(8,128)S(1)} %get-tuple-element.22.rim, f32[3,16,16,256]{3,2,1,0:T(8,128)S(1)} %copy-done.2, ...), custom_call_target="tpu_custom_call" | custom-call | flops 10000000 | bytes 2000000 | tf_op jit(solution)/shard_map/edge/pallas_call | solution.py:685
  31.9 0.0 copy-start.4
  31.9 0.0 copy-start.5
  31.9 2.3 %collective-permute-done.3.from_left = f32[2,24,128]{2,1,0:T(8,128)S(1)} collective-permute-done((f32[2,24,128]{2,1,0:T(8,128)}, f32[2,24,128]{2,1,0:T(8,128)S(1)}, u32[]{:S(2)}, u32[]{:S(2)}) %collective-permute-start.3) | collective-permute-done | bytes 24608 | tf_op jit(solution)/shard_map/ppermute | solution.py:683
  34.2 0.0 collective-permute-done.4.from_right
  34.3 1.8 %seams.1 = (f32[3,16,16,256]{3,2,1,0:T(8,128)}, f32[3,16,16,256]{3,2,1,0:T(8,128)}) custom-call(f32[23,24,256]{2,1,0:T(8,128)S(1)} %get-tuple-element.22.rim, f32[3,16,16,256]{3,2,1,0:T(8,128)S(1)} %get-tuple-element.25.sol_in, f32[3,16,16,256]{3,2,1,0:T(8,128)S(1)} %get-tuple-element.26.res_in, f32[2,24,128]{2,1,0:T(8,128)S(1)} %collective-permute-done.3.from_left, ...), custom_call_target="tpu_custom_call" | custom-call | flops 4000000 | bytes 4000000 | tf_op jit(solution)/shard_map/seams/pallas_call | solution.py:569
  36.1 0.0 all-to-all-done.block
  36.1 1.1 %harmonics.1 = f32[2,1,8,256]{3,2,1,0:T(8,128)} custom-call(f32[16,8,384]{2,1,0:T(8,128)S(1)} %all-to-all-done.block, bf16[256,512]{1,0:T(8,128)(2,1)S(1)} %copy-done.5, bf16[256,512]{1,0:T(8,128)(2,1)S(1)} %copy-done.4, f32[2,16,256]{2,1,0:T(8,128)S(1)} %get-tuple-element.32.table), custom_call_target="tpu_custom_call" | custom-call | flops 100000000 | bytes 1000000 | tf_op jit(solution)/shard_map/harmonics/pallas_call | solution.py:626
  (11 shorter events, 0.0 us)
Async XLA Ops:
  0.6 8.7 %copy-start.1 = (s32[16,16,256]{2,1,0:T(8,128)S(1)}, s32[16,16,256]{2,1,0:T(8,128)}, u32[]{:S(2)}) copy-start(s32[16,16,256]{2,1,0:T(8,128)} %reg.3) | copy-start | bytes 786436
  0.6 8.7 %copy-start = (f32[3,16,16,256]{3,2,1,0:T(8,128)S(1)}, f32[3,16,16,256]{3,2,1,0:T(8,128)}, u32[]{:S(2)}) copy-start(f32[3,16,16,256]{3,2,1,0:T(8,128)} %src.3) | copy-start | bytes 2359300
  2.1 1.4 %collective-permute-start = (f32[16,8,256]{2,1,0:T(8,128)S(1)}, f32[16,8,256]{2,1,0:T(8,128)S(1)}, u32[]{:S(2)}, u32[]{:S(2)}) collective-permute-start(f32[16,8,256]{2,1,0:T(8,128)S(1)} %get-tuple-element.18), channel_id=1, source_target_pairs={{0,1},{1,0},{2,3},{3,2},{4,5},{5,4},{6,7},{7,6},{8,9},{9,8},{10,11... | collective-permute-start | bytes 393224 | tf_op jit(solution)/shard_map/ppermute | solution.py:646
  3.5 12.0 %collective-permute-start.1 = (f32[9,16,256]{2,1,0:T(8,128)S(1)}, f32[9,16,256]{2,1,0:T(8,128)S(1)}, u32[]{:S(2)}, u32[]{:S(2)}) collective-permute-start(f32[9,16,256]{2,1,0:T(8,128)S(1)} %pad_maximum_fusion), channel_id=1, source_target_pairs={{0,2},{2,4},{4,6},{6,8},{8,10},{10,12},{12,14},{14,0},{1,3},{3,5},... | collective-permute-start | bytes 442376 | tf_op jit(solution)/shard_map/ppermute | solution.py:647
  5.9 9.7 %collective-permute-start.2 = (f32[7,16,256]{2,1,0:T(8,128)S(1)}, f32[7,16,256]{2,1,0:T(8,128)S(1)}, u32[]{:S(2)}, u32[]{:S(2)}) collective-permute-start(f32[7,16,256]{2,1,0:T(8,128)S(1)} %pad_maximum_fusion.1), channel_id=1, source_target_pairs={{0,14},{2,0},{4,2},{6,4},{8,6},{10,8},{12,10},{14,12},{1,15},{3,1}... | collective-permute-start | bytes 344072 | tf_op jit(solution)/shard_map/ppermute | solution.py:648
  13.7 17.4 %copy-start.2 = (f32[3,16,16,256]{3,2,1,0:T(8,128)S(1)}, f32[3,16,16,256]{3,2,1,0:T(8,128)}, u32[]{:S(2)}) copy-start(f32[3,16,16,256]{3,2,1,0:T(8,128)} %get-tuple-element.23.sol_in) | copy-start | bytes 2359300
  13.7 17.4 %copy-start.3 = (f32[3,16,16,256]{3,2,1,0:T(8,128)S(1)}, f32[3,16,16,256]{3,2,1,0:T(8,128)}, u32[]{:S(2)}) copy-start(f32[3,16,16,256]{3,2,1,0:T(8,128)} %get-tuple-element.24.res_in) | copy-start | bytes 2359300
  13.7 17.4 %copy-start.6 = (s32[16]{0:T(128)S(1)}, s32[16]{0:T(128)}, u32[]{:S(2)}) copy-start(s32[16]{0:T(128)} %skew.1) | copy-start | bytes 196
  17.0 19.1 %all-to-all-start = ((f32[16,8,384]{2,1,0:T(8,128)}), f32[16,8,384]{2,1,0:T(8,128)S(1)}, u32[]{:S(2)}, u32[]{:S(2)}) async-start(f32[16,8,384]{2,1,0:T(8,128)} %get-tuple-element.31), calls=%async_computation | async-start | bytes 393216 | tf_op jit(solution)/shard_map/all_to_all | solution.py:682
  26.9 7.3 %collective-permute-start.3 = (f32[2,24,128]{2,1,0:T(8,128)}, f32[2,24,128]{2,1,0:T(8,128)S(1)}, u32[]{:S(2)}, u32[]{:S(2)}) collective-permute-start(f32[2,24,128]{2,1,0:T(8,128)} %get-tuple-element.27), channel_id=1, source_target_pairs={{0,16},{16,32},{32,48},{48,64},{64,80},{80,96},{96,112},{112,128},... | collective-permute-start | bytes 73736 | tf_op jit(solution)/shard_map/ppermute | solution.py:683
  28.4 5.8 %collective-permute-start.4 = (f32[2,24,128]{2,1,0:T(8,128)}, f32[2,24,128]{2,1,0:T(8,128)S(1)}, u32[]{:S(2)}, u32[]{:S(2)}) collective-permute-start(f32[2,24,128]{2,1,0:T(8,128)} %get-tuple-element.28), channel_id=1, source_target_pairs={{0,240},{16,0},{32,16},{48,32},{64,48},{80,64},{96,80},{112,96},{1... | collective-permute-start | bytes 73736 | tf_op jit(solution)/shard_map/ppermute | solution.py:684
  31.9 4.2 %copy-start.4 = (bf16[256,512]{1,0:T(8,128)(2,1)S(1)}, bf16[256,512]{1,0:T(8,128)(2,1)}, u32[]{:S(2)}) copy-start(bf16[256,512]{1,0:T(8,128)(2,1)} %constant.5.clone.basis_lo) | copy-start | bytes 786436
  31.9 4.2 %copy-start.5 = (bf16[256,512]{1,0:T(8,128)(2,1)S(1)}, bf16[256,512]{1,0:T(8,128)(2,1)}, u32[]{:S(2)}) copy-start(bf16[256,512]{1,0:T(8,128)(2,1)} %constant.4.clone.basis_hi) | copy-start | bytes 786436

commit v4 on v3

--- a/solution.py
+++ b/solution.py
@@ -55,7 +55,7 @@
 
 
 class Kept:
-    planes = 48
+    planes = 53
     of_field, of_step, of_res = (0, 1, 13, 14, 15), (1, 2, 13, 14), (1, 14)
 
     def field(self, c, z):
@@ -73,20 +73,24 @@
     def stress(self, z):
         return (42 + z // 3, slice(8 * (z % 3), 8 * (z % 3) + 8))
 
+    def strength(self, c, z):
+        return 48 + c if z == 0 else 50 + c
+
 
 class Rim:
-    planes = 12 + 6 + 4 + 1
+    planes = 9 + 6 + 4 + 8
 
     def step(self, c, z):
-        return 4 * c + (-1, 0, 15, 16).index(z)
+        return 3 * c + (0, 15, 16).index(z)
 
     def res(self, c, z):
-        return (12 + 2 * c + (0, 15).index(z), slice(0, 16))
+        return (9 + 2 * c + (0, 15).index(z), slice(0, 16))
 
     def strips(self, c, side):
-        return (18 + c, slice(None), slice(128 * side, 128 * side + 128))
-
-    code = 22
+        return (15 + c, slice(None), slice(128 * side, 128 * side + 128))
+
+    def field(self, c, z):
+        return 19 + 2 * c + (-2, -1).index(z)
 
 
 KEPT, RIM = Kept(), Rim()
@@ -230,7 +234,8 @@
     )
 
 
-def inner_kernel(src, reg, sw, kept, sol_out, res_out, field, s, hh, sol, res, ids, sems):
+def inner_kernel(src, reg, sw, kept, flag, sol_out, res_out, field, s, hh, sol, res, ids, sems):
+    flag[...] = jnp.zeros((8, 128), F32)
     core = lax.axis_index("rad")
     pick = from_partner((8, 256), core)
     lane = lax.broadcasted_iota(jnp.int32, (24, 128), 1)
@@ -306,6 +311,9 @@
             kept[KEPT.step(c, z)] = s[c, z]
         for z in KEPT.of_res:
             kept[KEPT.res(c, z)] = res[c, z]
+        kept[KEPT.strength(c, 0)] = hh[c, 0]
+        if c > 0:
+            kept[KEPT.strength(c, 14)] = hh[c, 14]
     for c in range(4):
         for z in KEPT.of_field:
             kept[KEPT.field(c, z)] = field[c, z]
@@ -321,7 +329,7 @@
         copy.wait()
 
 
-def rim_kernel(kept, up, dn, hbm, az_up, az_dn, rim, w, out, up_msg, dn_msg, sem):
+def rim_kernel(kept, up, sw, dn, _, hbm, az_up, az_dn, rim, w, out, up_msg, dn_msg, sem):
     core, ax = lax.axis_index("rad"), lax.axis_index("ax")
     lo = jnp.where(ax > 0, 1.0, 0.0)
     hi = jnp.where(ax < lax.axis_size("ax") - 1, 1.0, 0.0)
@@ -333,13 +341,15 @@
             w[c, i, 0:16, :] = (value - empty) * valid + empty
             w[c, i, 16:24, :] = jnp.where(pick, (beside - empty) * valid + empty, empty)
 
-        put(0, up[2 * c], partner_rows(up[8, 0:8], c, core), lo)
-        put(1, up[2 * c + 1], partner_rows(up[8, 8:16], c, core), lo)
+        put(0, up[2 * c], sw[2 * c], lo)
+        put(1, up[2 * c + 1], sw[2 * c + 1], lo)
         put(6, dn[c], partner_rows(dn[6, 0:8], c, core), hi)
         if c in (1, 2):
             put(7, dn[3 + c], partner_rows(dn[6, 8:16], c, core), hi)
         else:
             w[c, 7] = jnp.full((24, 256), empty, F32)
+        for z in (-2, -1):
+            rim[RIM.field(c, z)] = w[c, z + 2]
         w[c, 2] = kept[KEPT.field(c, 0)]
         w[c, 3] = kept[KEPT.field(c, 1)]
         w[c, 4] = kept[KEPT.field(c, 14)]
@@ -351,26 +361,23 @@
     def h_of(i, reluct):
         return strength(*vec(i), w[1, i + 1], w[2, i + 1], reluct)
 
-    def rims(i, zs):
-        _, h1, h2 = h_of(i, materials(w[3, i])[0])
-        steps = []
-        for n in range(2):
-            reluct, mass = materials(w[3, i + 1 + n])
-            h = h_of(i + 1 + n, reluct)
-            v = vec(i + 1 + n)
-            a = image(v, h, h1, h2, mass)
-            h1, h2 = h[1], h[2]
-            step = second_of(v, a, mass)
-            for c in range(3):
-                rim[RIM.step(c, zs[n])] = step[c]
-                if zs[n] in (0, 15):
-                    rim[RIM.res(c, zs[n])] = (v[c] - FIRST * a[c])[:16]
-            steps.append([FIRST * v[c] + step[c] for c in range(3)])
-        return steps
-
-    rim[RIM.code] = w[3, 1]
-    _, u_first = rims(0, (-1, 0))
-    u_last, u_after = rims(4, (15, 16))
+    def step_of(i, z, h, h1p, h2p):
+        v, mass = vec(i), materials(w[3, i])[1]
+        a = image(v, h, h1p, h2p, mass)
+        step = second_of(v, a, mass)
+        for c in range(3):
+            rim[RIM.step(c, z)] = step[c]
+            if z < 16:
+                rim[RIM.res(c, z)] = (v[c] - FIRST * a[c])[:16]
+        return [FIRST * v[c] + step[c] for c in range(3)]
+
+    h_before = h_of(1, materials(w[3, 1])[0])
+    h_last = h_of(5, materials(w[3, 5])[0])
+    h_after = h_of(6, materials(w[3, 6])[0])
+    h_zero = [kept[KEPT.strength(c, 0)] for c in range(3)]
+    u_first = step_of(2, 0, h_zero, h_before[1], h_before[2])
+    u_last = step_of(5, 15, h_last, kept[KEPT.strength(1, 14)], kept[KEPT.strength(2, 14)])
+    u_after = step_of(6, 16, h_after, h_last[1], h_last[2])
     u_one = [FIRST * w[c, 3] + kept[KEPT.step(c, 1)] for c in range(3)]
     u_14 = [FIRST * w[c, 4] + kept[KEPT.step(c, 14)] for c in range(3)]
     for z in range(1, 14):
@@ -484,11 +491,20 @@
     table[0] = jnp.cos(angle)
     table[1] = jnp.sin(angle)
 
+    v2, v1 = [[rim[RIM.field(c, z)] for c in range(4)] for z in (-2, -1)]
+    v0 = [kept[KEPT.field(c, 0)] for c in range(3)]
+    rim_code = materials(v1[3])
+    _, h1, h2 = strength(*v2[:3], v1[1], v1[2], materials(v2[3])[0])
+    h = strength(*v1[:3], v0[1], v0[2], rim_code[0])
+    before_first = second_of(v1, image(v1, h, h1, h2, rim_code[1]), rim_code[1])
+
     def step(z, c):
-        return rim[RIM.step(c, z)] if z in (-1, 0, 15, 16) else kept[KEPT.step(c, z)]
+        if z < 0:
+            return before_first[c]
+        return rim[RIM.step(c, z)] if z in (0, 15, 16) else kept[KEPT.step(c, z)]
 
     def materials_of(z):
-        return materials(rim[RIM.code] if z < 0 else kept[KEPT.field(3, z)])
+        return rim_code if z < 0 else materials(kept[KEPT.field(3, z)])
 
     def h_of(z):
         return strength(
@@ -550,13 +566,13 @@
             for c in range(3):
                 x = (sol_in, res_in)[n][c, z]
                 edge = roll(merged[n][c], 124 - 6 * i, 1)
-                buf[z // 4, c, z % 4, :, 0:128] = jnp.where(lane < 2, edge, x[:, :128])
-                buf[z // 4, c, z % 4, :, 128:256] = jnp.where(lane >= 126, edge, x[:, 128:])
-        if z % 4 == 3:
-            t = z // 4
+                buf[z // 8, c, z % 8, :, 0:128] = jnp.where(lane < 2, edge, x[:, :128])
+                buf[z // 8, c, z % 8, :, 128:256] = jnp.where(lane >= 126, edge, x[:, 128:])
+        if z % 8 == 7:
+            t = z // 8
             for n, (buf, dst) in enumerate(((a_sol, sol), (a_res, res))):
                 copy = pltpu.make_async_copy(
-                    buf.at[t], dst.at[:, pl.ds(4 * t, 4)], sems.at[n, t]
+                    buf.at[t], dst.at[:, pl.ds(8 * t, 8)], sems.at[n, t]
                 )
                 copy.start()
                 copies.append(copy)
@@ -572,9 +588,9 @@
         in_specs=[VMEM] * len(args),
         out_specs=[HBM] * 2,
         scratch_shapes=[
-            pltpu.VMEM((4, 3, 4, 16, 256), F32),
-            pltpu.VMEM((4, 3, 4, 16, 256), F32),
-            pltpu.SemaphoreType.DMA((2, 4)),
+            pltpu.VMEM((2, 3, 8, 16, 256), F32),
+            pltpu.VMEM((2, 3, 8, 16, 256), F32),
+            pltpu.SemaphoreType.DMA((2, 2)),
         ],
         compiler_params=pltpu.CompilerParams(vmem_limit_bytes=12 * 2**20),
         cost_estimate=pl.CostEstimate(flops=4_000_000, bytes_accessed=4_000_000, transcendentals=0),
@@ -643,14 +659,15 @@
 def on_device(source, region, skew_shift):
     n_az, n_ax = lax.axis_size("az"), lax.axis_size("ax")
     up, dn, sw = send_call(source, region)
-    sw = ring("rad", 2, 1)(sw)
-    up = ring("ax", n_ax, 1)(jnp.concatenate([up, sw[14:16].reshape(1, 16, 256)], axis=0))
+    swap = ring("rad", 2, 1)
+    sw = swap(sw)
+    up = ring("ax", n_ax, 1)(up)
     dn = ring("ax", n_ax, -1)(jnp.concatenate([dn, sw[0:2].reshape(1, 16, 256)], axis=0))
     block, tall = (3, 16, 16, 256), (16, 24, 256)
-    kept, sol, res = call(
+    kept, flag, sol, res = call(
         inner_kernel,
         "inner",
-        [(Kept.planes, 24, 256), block, block],
+        [(Kept.planes, 24, 256), (8, 128), block, block],
         [
             (4, *tall),
             (3, *tall),
@@ -662,8 +679,10 @@
         ],
         16,
         [HBM, HBM, VMEM],
-        [VMEM, HBM, HBM],
+        [VMEM, VMEM, HBM, HBM],
     )(source, region, sw)
+    start, flag = lax.optimization_barrier((8 * (1 - lax.axis_index("rad")), flag))
+    sw_up = swap(lax.dynamic_slice_in_dim(up, start, 8, axis=1))
     stress, az_up, az_dn, rim = call(
         rim_kernel,
         "rim",
@@ -676,9 +695,9 @@
             pltpu.SemaphoreType.DMA((4,)),
         ],
         8,
-        [VMEM] * 3,
+        [VMEM] * 4 + [pl.BlockSpec(memory_space=pl.ANY)],
         [HBM, HBM, HBM, VMEM],
-    )(kept, up, dn)
+    )(kept, up, sw_up, dn, flag)
     circle = lax.all_to_all(stress, "az", split_axis=0, concat_axis=0, tiled=True)
     from_left = ring("az", n_az, 1)(az_up)
     from_right = ring("az", n_az, -1)(az_dn)

time: 37.4 us -> 35.9 us (0.960)
  waiting for transfers between devices: 5.49 us -> 2.74 us
  local copies, waits for them, and re-layouts: 0.04 us -> 1.19 us
    ppermute x1, waiting for transfers between devices: 1.85 us -> 0.31 us  [on_device(): ring('ax', n_ax, -1)]
    unnamed x14, local copies, waits for them, and re-layouts: 0.04 us -> 1.17 us
    ppermute x1, waiting for transfers between devices: 2.3 us -> 1.18 us  [on_device(): from_left = ring('az', n_az, 1)(az_up)]
    ppermute x2 -> x3, starting transfers between devices: 2.46 us -> 2.56 us  [the longest x1 2.37 us: on_device(): up = ring('ax', n_ax, 1)(up)]
    ppermute x2 -> x3, waiting for transfers between devices: 1.34 us -> 1.25 us  [the longest x1 1.24 us: on_device(): sw_up = swap(lax.dynamic_slice_in_dim(up, start, 8, axis=1))]
  transfers between devices with their start and end apart: 6 -> 7, of which waited for: 3 -> 3; matrix products, arithmetic and copies ran while one was open for 0% -> 0% of each run, Pallas kernels for 19% -> 20%
where the time goes in v4:
time: 35.9 us; the launch traced here: 35.7 us
  starting transfers between devices  20.2 us (56%)
  Pallas kernels  10.8 us (30%)
  waiting for transfers between devices  2.74 us (8%)
  local copies, waits for them, and re-layouts  1.19 us (3%)
  between operations  0.78 us (2%)
    all_to_all x1, starting transfers between devices, on_device(): lax.all_to_all(stress, 'az', split_axis=0, concat_axis=0, tiled=True)  9.96 us
    pallas_call x1, Pallas kernels, on_device(): call(inner_kernel, 'inner', [(Kept.planes, 24, 256), (8, 128), block, blo...  4.34 us
    ppermute x1, starting transfers between devices, on_device(): ring('ax', n_ax, -1)  3.53 us
    ppermute x1, starting transfers between devices, on_device(): from_right = ring('az', n_az, -1)(az_dn)  2.67 us
    ppermute x1, starting transfers between devices, on_device(): up = ring('ax', n_ax, 1)(up)  2.37 us
    pallas_call x1, Pallas kernels, seam_call(): pl.pallas_call(seam_kernel, out_shape=[out, out], in_specs=[VMEM] * len(a...  1.73 us
    ppermute x1, starting transfers between devices, on_device(): from_left = ring('az', n_az, 1)(az_up)  1.46 us
    pallas_call x1, Pallas kernels, send_call(): pl.pallas_call(send_kernel, out_shape=[jax.ShapeDtypeStruct(shape, F32) f...  1.4 us
  transfers between devices with their start and end apart: 7, of which 3 were waited for; matrix products, arithmetic and copies ran while one was open for 0% of the time, Pallas kernels for 20%

profile of v4, /device:TPU:8, one launch (start us, length us, event | category | flops | bytes accessed | tf_op | source)
XLA Modules:
  0.0 35.7 jit_solution(556612726495076658)
XLA Ops:
  0.6 1.4 %send.1 = (f32[8,16,256]{2,1,0:T(8,128)S(1)}, f32[6,16,256]{2,1,0:T(8,128)S(1)}, f32[16,8,256]{2,1,0:T(8,128)S(1)}) custom-call(f32[3,16,16,256]{3,2,1,0:T(8,128)} %src.3, s32[16,16,256]{2,1,0:T(8,128)} %reg.3), custom_call_target="tpu_custom_call" | custom-call | tf_op jit(solution)/shard_map/send/pallas_call | solution.py:199
  2.1 0.1 collective-permute-start
  2.2 2.4 %collective-permute-start.1 = (f32[8,16,256]{2,1,0:T(8,128)S(1)}, f32[8,16,256]{2,1,0:T(8,128)S(1)}, u32[]{:S(2)}, u32[]{:S(2)}) collective-permute-start(f32[8,16,256]{2,1,0:T(8,128)S(1)} %get-tuple-element.23), channel_id=1, source_target_pairs={{0,2},{2,4},{4,6},{6,8},{8,10},{10,12},{12,14},{14,0},{1,3},{3,5},... | collective-permute-start | bytes 393224 | tf_op jit(solution)/shard_map/ppermute | solution.py:664
  4.5 0.0 collective-permute-done.sw
  4.5 3.5 %collective-permute-start.3 = (f32[7,16,256]{2,1,0:T(8,128)S(1)}, f32[7,16,256]{2,1,0:T(8,128)S(1)}, u32[]{:S(2)}, u32[]{:S(2)}) collective-permute-start(f32[7,16,256]{2,1,0:T(8,128)S(1)} %pad_maximum_fusion), channel_id=1, source_target_pairs={{0,14},{2,0},{4,2},{6,4},{8,6},{10,8},{12,10},{14,12},{1,15},{3,1}... | collective-permute-start | bytes 344072 | tf_op jit(solution)/shard_map/ppermute | solution.py:665
  8.1 4.3 %inner.1 = (f32[53,24,256]{2,1,0:T(8,128)S(1)}, f32[8,128]{1,0:T(8,128)S(1)}, f32[3,16,16,256]{3,2,1,0:T(8,128)}, f32[3,16,16,256]{3,2,1,0:T(8,128)}) custom-call(f32[3,16,16,256]{3,2,1,0:T(8,128)S(1)} %copy-done, s32[16,16,256]{2,1,0:T(8,128)S(1)} %copy-done.1, f32[16,8,256]{2,1,0:T(8,128)S(1)} %collective-permute-done.sw), custom_call_target="tpu_custom_call" | custom-call | flops 10000000 | bytes 2000000 | tf_op jit(solution)/shard_map/inner/pallas_call | solution.py:667
  12.4 0.0 copy-start.2
  12.4 0.0 copy-start.6
  12.4 0.0 collective-permute-done.1.up
  12.5 0.1 collective-permute-start.2
  12.6 1.2 %collective-permute-done.2.sw = f32[8,8,256]{2,1,0:T(8,128)S(1)} collective-permute-done((f32[8,8,256]{2,1,0:T(8,128)S(1)}, f32[8,8,256]{2,1,0:T(8,128)S(1)}, u32[]{:S(2)}, u32[]{:S(2)}) %collective-permute-start.2) | collective-permute-done | bytes 65568 | tf_op jit(solution)/shard_map/ppermute | solution.py:685
  13.8 0.3 collective-permute-done.3.dn
  14.1 1.3 %rim.1 = (f32[16,8,384]{2,1,0:T(8,128)}, f32[2,24,128]{2,1,0:T(8,128)}, f32[2,24,128]{2,1,0:T(8,128)}, f32[27,24,256]{2,1,0:T(8,128)S(1)}) custom-call(f32[53,24,256]{2,1,0:T(8,128)S(1)} %get-tuple-element.22.kept, f32[8,16,256]{2,1,0:T(8,128)S(1)} %collective-permute-done.1.up, f32[8,8,256]{2,1,0:T(8,128)S(1)} %collective-permute-done.2.sw, ...), custom_call_target="tpu_custom_call" | custom-call | flops 10000000 | bytes 2000000 | tf_op jit(solution)/shard_map/rim/pallas_call | solution.py:686
  15.4 10.0 %all-to-all-start = ((f32[16,8,384]{2,1,0:T(8,128)}), f32[16,8,384]{2,1,0:T(8,128)S(1)}, u32[]{:S(2)}, u32[]{:S(2)}) async-start(f32[16,8,384]{2,1,0:T(8,128)} %get-tuple-element.37), calls=%async_computation | async-start | bytes 393216 | tf_op jit(solution)/shard_map/all_to_all | solution.py:701
  25.4 1.5 %collective-permute-start.4 = (f32[2,24,128]{2,1,0:T(8,128)}, f32[2,24,128]{2,1,0:T(8,128)S(1)}, u32[]{:S(2)}, u32[]{:S(2)}) collective-permute-start(f32[2,24,128]{2,1,0:T(8,128)} %get-tuple-element.33), channel_id=1, source_target_pairs={{0,16},{16,32},{32,48},{48,64},{64,80},{80,96},{96,112},{112,128},... | collective-permute-start | bytes 73736 | tf_op jit(solution)/shard_map/ppermute | solution.py:702
  26.9 2.7 %collective-permute-start.5 = (f32[2,24,128]{2,1,0:T(8,128)}, f32[2,24,128]{2,1,0:T(8,128)S(1)}, u32[]{:S(2)}, u32[]{:S(2)}) collective-permute-start(f32[2,24,128]{2,1,0:T(8,128)} %get-tuple-element.34), channel_id=1, source_target_pairs={{0,240},{16,0},{32,16},{48,32},{64,48},{80,64},{96,80},{112,96},{1... | collective-permute-start | bytes 73736 | tf_op jit(solution)/shard_map/ppermute | solution.py:703
  29.5 1.1 %copy-done.3 = f32[3,16,16,256]{3,2,1,0:T(8,128)S(1)} copy-done((f32[3,16,16,256]{3,2,1,0:T(8,128)S(1)}, f32[3,16,16,256]{3,2,1,0:T(8,128)}, u32[]{:S(2)}) %copy-start.3) | copy-done | bytes 786456
  30.7 0.9 %edge.1 = (f32[3,16,16,256]{3,2,1,0:T(8,128)S(1)}, f32[3,16,16,256]{3,2,1,0:T(8,128)S(1)}, f32[2,16,256]{2,1,0:T(8,128)S(1)}) custom-call(s32[16]{0:T(128)S(1)} %copy-done.6, f32[53,24,256]{2,1,0:T(8,128)S(1)} %get-tuple-element.22.kept, f32[27,24,256]{2,1,0:T(8,128)S(1)} %get-tuple-element.28.rim, f32[3,16,16,256]{3,2,1,0:T(8,128)S(1)} %copy-done.2, ...), custom_call_target="tpu_custom_call" | custom-call | flops 10000000 | bytes 2000000 | tf_op jit(solution)/shard_map/edge/pallas_call | solution.py:704
  31.6 0.0 copy-start.4
  31.6 0.0 copy-start.5
  31.6 1.2 %collective-permute-done.4.from_left = f32[2,24,128]{2,1,0:T(8,128)S(1)} collective-permute-done((f32[2,24,128]{2,1,0:T(8,128)}, f32[2,24,128]{2,1,0:T(8,128)S(1)}, u32[]{:S(2)}, u32[]{:S(2)}) %collective-permute-start.4) | collective-permute-done | bytes 24608 | tf_op jit(solution)/shard_map/ppermute | solution.py:702
  32.8 0.0 collective-permute-done.5.from_right
  32.8 1.7 %seams.1 = (f32[3,16,16,256]{3,2,1,0:T(8,128)}, f32[3,16,16,256]{3,2,1,0:T(8,128)}) custom-call(f32[27,24,256]{2,1,0:T(8,128)S(1)} %get-tuple-element.28.rim, f32[3,16,16,256]{3,2,1,0:T(8,128)S(1)} %get-tuple-element.31.sol_in, f32[3,16,16,256]{3,2,1,0:T(8,128)S(1)} %get-tuple-element.32.res_in, f32[2,24,128]{2,1,0:T(8,128)S(1)} %collective-permute-done.4.from_left, ...), custom_call_target="tpu_custom_call" | custom-call | flops 4000000 | bytes 4000000 | tf_op jit(solution)/shard_map/seams/pallas_call | solution.py:585
  34.6 1.1 %harmonics.1 = f32[2,1,8,256]{3,2,1,0:T(8,128)} custom-call(f32[16,8,384]{2,1,0:T(8,128)S(1)} %all-to-all-done.block, bf16[256,512]{1,0:T(8,128)(2,1)S(1)} %copy-done.5, bf16[256,512]{1,0:T(8,128)(2,1)S(1)} %copy-done.4, f32[2,16,256]{2,1,0:T(8,128)S(1)} %get-tuple-element.38.table), custom_call_target="tpu_custom_call" | custom-call | flops 100000000 | bytes 1000000 | tf_op jit(solution)/shard_map/harmonics/pallas_call | solution.py:642
  (13 shorter events, 0.1 us)
Async XLA Ops:
  0.6 7.4 %copy-start.1 = (s32[16,16,256]{2,1,0:T(8,128)S(1)}, s32[16,16,256]{2,1,0:T(8,128)}, u32[]{:S(2)}) copy-start(s32[16,16,256]{2,1,0:T(8,128)} %reg.3) | copy-start | bytes 786436
  0.6 7.4 %copy-start = (f32[3,16,16,256]{3,2,1,0:T(8,128)S(1)}, f32[3,16,16,256]{3,2,1,0:T(8,128)}, u32[]{:S(2)}) copy-start(f32[3,16,16,256]{3,2,1,0:T(8,128)} %src.3) | copy-start | bytes 2359300
  2.1 2.5 %collective-permute-start = (f32[16,8,256]{2,1,0:T(8,128)S(1)}, f32[16,8,256]{2,1,0:T(8,128)S(1)}, u32[]{:S(2)}, u32[]{:S(2)}) collective-permute-start(f32[16,8,256]{2,1,0:T(8,128)S(1)} %get-tuple-element.21), channel_id=1, source_target_pairs={{0,1},{1,0},{2,3},{3,2},{4,5},{5,4},{6,7},{7,6},{8,9},{9,8},{10,11... | collective-permute-start | bytes 393224 | tf_op jit(solution)/shard_map/ppermute | solution.py:663
  2.2 10.3 %collective-permute-start.1 = (f32[8,16,256]{2,1,0:T(8,128)S(1)}, f32[8,16,256]{2,1,0:T(8,128)S(1)}, u32[]{:S(2)}, u32[]{:S(2)}) collective-permute-start(f32[8,16,256]{2,1,0:T(8,128)S(1)} %get-tuple-element.23), channel_id=1, source_target_pairs={{0,2},{2,4},{4,6},{6,8},{8,10},{10,12},{12,14},{14,0},{1,3},{3,5},... | collective-permute-start | bytes 393224 | tf_op jit(solution)/shard_map/ppermute | solution.py:664
  4.5 9.6 %collective-permute-start.3 = (f32[7,16,256]{2,1,0:T(8,128)S(1)}, f32[7,16,256]{2,1,0:T(8,128)S(1)}, u32[]{:S(2)}, u32[]{:S(2)}) collective-permute-start(f32[7,16,256]{2,1,0:T(8,128)S(1)} %pad_maximum_fusion), channel_id=1, source_target_pairs={{0,14},{2,0},{4,2},{6,4},{8,6},{10,8},{12,10},{14,12},{1,15},{3,1}... | collective-permute-start | bytes 344072 | tf_op jit(solution)/shard_map/ppermute | solution.py:665
  12.4 17.1 %copy-start.2 = (f32[3,16,16,256]{3,2,1,0:T(8,128)S(1)}, f32[3,16,16,256]{3,2,1,0:T(8,128)}, u32[]{:S(2)}) copy-start(f32[3,16,16,256]{3,2,1,0:T(8,128)} %get-tuple-element.29.sol_in) | copy-start | bytes 2359300
  12.4 17.1 %copy-start.6 = (s32[16]{0:T(128)S(1)}, s32[16]{0:T(128)}, u32[]{:S(2)}) copy-start(s32[16]{0:T(128)} %skew.1) | copy-start | bytes 196
  12.5 1.3 %collective-permute-start.2 = (f32[8,8,256]{2,1,0:T(8,128)S(1)}, f32[8,8,256]{2,1,0:T(8,128)S(1)}, u32[]{:S(2)}, u32[]{:S(2)}) collective-permute-start(f32[8,8,256]{2,1,0:T(8,128)S(1)} %constant_dynamic-slice_fusion), channel_id=1, source_target_pairs={{0,1},{1,0},{2,3},{3,2},{4,5},{5,4},{6,7},{7,6},{8,9},{9,8},{10,11... | collective-permute-start | bytes 196616 | tf_op jit(solution)/shard_map/ppermute | solution.py:685
  15.4 19.1 %all-to-all-start = ((f32[16,8,384]{2,1,0:T(8,128)}), f32[16,8,384]{2,1,0:T(8,128)S(1)}, u32[]{:S(2)}, u32[]{:S(2)}) async-start(f32[16,8,384]{2,1,0:T(8,128)} %get-tuple-element.37), calls=%async_computation | async-start | bytes 393216 | tf_op jit(solution)/shard_map/all_to_all | solution.py:701
  25.4 7.4 %collective-permute-start.4 = (f32[2,24,128]{2,1,0:T(8,128)}, f32[2,24,128]{2,1,0:T(8,128)S(1)}, u32[]{:S(2)}, u32[]{:S(2)}) collective-permute-start(f32[2,24,128]{2,1,0:T(8,128)} %get-tuple-element.33), channel_id=1, source_target_pairs={{0,16},{16,32},{32,48},{48,64},{64,80},{80,96},{96,112},{112,128},... | collective-permute-start | bytes 73736 | tf_op jit(solution)/shard_map/ppermute | solution.py:702
  26.9 5.9 %collective-permute-start.5 = (f32[2,24,128]{2,1,0:T(8,128)}, f32[2,24,128]{2,1,0:T(8,128)S(1)}, u32[]{:S(2)}, u32[]{:S(2)}) collective-permute-start(f32[2,24,128]{2,1,0:T(8,128)} %get-tuple-element.34), channel_id=1, source_target_pairs={{0,240},{16,0},{32,16},{48,32},{64,48},{80,64},{96,80},{112,96},{1... | collective-permute-start | bytes 73736 | tf_op jit(solution)/shard_map/ppermute | solution.py:703
  29.5 1.1 %copy-start.3 = (f32[3,16,16,256]{3,2,1,0:T(8,128)S(1)}, f32[3,16,16,256]{3,2,1,0:T(8,128)}, u32[]{:S(2)}) copy-start(f32[3,16,16,256]{3,2,1,0:T(8,128)} %get-tuple-element.30.res_in) | copy-start | bytes 2359300
  31.6 3.0 %copy-start.4 = (bf16[256,512]{1,0:T(8,128)(2,1)S(1)}, bf16[256,512]{1,0:T(8,128)(2,1)}, u32[]{:S(2)}) copy-start(bf16[256,512]{1,0:T(8,128)(2,1)} %constant.17.clone.basis_lo) | copy-start | bytes 786436
  31.6 3.0 %copy-start.5 = (bf16[256,512]{1,0:T(8,128)(2,1)S(1)}, bf16[256,512]{1,0:T(8,128)(2,1)}, u32[]{:S(2)}) copy-start(bf16[256,512]{1,0:T(8,128)(2,1)} %constant.16.clone.basis_hi) | copy-start | bytes 786436

commit v5 on v4

--- a/solution.py
+++ b/solution.py
@@ -184,9 +184,7 @@
     packed = jnp.zeros((16, 8, 256), F32)
     for c in range(4):
         x = tiles[c] if c < 3 else ids[...].astype(F32)
-        first = pltpu.roll(x, 2 * c, 1) if c else x
-        last = pltpu.roll(x, (2 * c + 2) % 8, 1) if c < 3 else x
-        packed = jnp.where(sub == c, jnp.where(core == 1, first, last), packed)
+        packed = jnp.where(sub == c, pltpu.roll(x, (2 * c + 2 - 2 * core) & 7, 1), packed)
     sw[...] = packed
     for copy in copies[4:]:
         copy.wait()
@@ -539,43 +537,38 @@
             for c, (t, shift) in enumerate(zip((0, 0, 0, 1), shifts))
         ]
 
-    def solve(x):
+    right = full([rim[RIM.strips(c, 0)] for c in range(4)], from_right, k > 3, (2, 0, 4, 2))
+    left = full([rim[RIM.strips(c, 1)] for c in range(4)], from_left, k < 2, (-2, -4, 0, -2))
+    copies = []
+
+    def operator(v, reluct, mass):
+        h = strength(*v, roll(v[1], -6, 1), roll(v[2], -6, 1), reluct)
+        return image(v, h, roll(h[1], 6, 1), roll(h[2], 6, 1), mass)
+
+    def send(n, buf, dst, inner, rights, lefts):
+        lane = lax.broadcasted_iota(jnp.int32, (16, 128), 1)
+        for c in range(3):
+            merged = jnp.where(k[:16] < 4, rights[c][:16], roll(lefts[c][:16], 2, 1))
+            for z in range(16):
+                edge = roll(merged, 124 - 6 * (z + 2), 1)
+                buf[c, z, :, 0:128] = jnp.where(lane < 2, edge, inner[c, z, :, 0:128])
+                buf[c, z, :, 128:256] = jnp.where(lane >= 126, edge, inner[c, z, :, 128:256])
+            copies.append(pltpu.make_async_copy(buf.at[c], dst.at[c], sems.at[n, c]))
+            copies[-1].start()
+
+    sides = []
+    for x in (right, left):
         reluct, mass = materials(x[3])
-        v = x[:3]
-        h = strength(*v, roll(v[1], -6, 1), roll(v[2], -6, 1), reluct)
-        a = image(v, h, roll(h[1], 6, 1), roll(h[2], 6, 1), mass)
-        step = second_of(v, a, mass)
-        h = strength(*step, roll(step[1], -6, 1), roll(step[2], -6, 1), reluct)
-        a2 = image(step, h, roll(h[1], 6, 1), roll(h[2], 6, 1), mass)
-        return (
-            [(FIRST * v[c] + step[c])[:16] for c in range(3)],
-            [(v[c] - FIRST * a[c] - a2[c])[:16] for c in range(3)],
-        )
-
-    right = solve(full([rim[RIM.strips(c, 0)] for c in range(4)], from_right, k > 3, (2, 0, 4, 2)))
-    left = solve(full([rim[RIM.strips(c, 1)] for c in range(4)], from_left, k < 2, (-2, -4, 0, -2)))
-    k = k[:16]
-    merged = [
-        [jnp.where(k < 4, right[n][c], roll(left[n][c], 2, 1)) for c in range(3)] for n in range(2)
-    ]
-    lane = lax.broadcasted_iota(jnp.int32, (16, 128), 1)
-    copies = []
-    for z in range(16):
-        i = z + 2
-        for n, buf in ((0, a_sol), (1, a_res)):
-            for c in range(3):
-                x = (sol_in, res_in)[n][c, z]
-                edge = roll(merged[n][c], 124 - 6 * i, 1)
-                buf[z // 8, c, z % 8, :, 0:128] = jnp.where(lane < 2, edge, x[:, :128])
-                buf[z // 8, c, z % 8, :, 128:256] = jnp.where(lane >= 126, edge, x[:, 128:])
-        if z % 8 == 7:
-            t = z // 8
-            for n, (buf, dst) in enumerate(((a_sol, sol), (a_res, res))):
-                copy = pltpu.make_async_copy(
-                    buf.at[t], dst.at[:, pl.ds(8 * t, 8)], sems.at[n, t]
-                )
-                copy.start()
-                copies.append(copy)
+        a = operator(x[:3], reluct, mass)
+        sides.append((x[:3], reluct, mass, a, second_of(x, a, mass)))
+    send(
+        0, a_sol, sol, sol_in, *[[FIRST * v[c] + step[c] for c in range(3)] for v, _, _, _, step in sides]
+    )
+    rest = []
+    for v, reluct, mass, a, step in sides:
+        a2 = operator(step, reluct, mass)
+        rest.append([v[c] - FIRST * a[c] - a2[c] for c in range(3)])
+    send(1, a_res, res, res_in, *rest)
     for copy in copies:
         copy.wait()
 
@@ -588,9 +581,9 @@
         in_specs=[VMEM] * len(args),
         out_specs=[HBM] * 2,
         scratch_shapes=[
-            pltpu.VMEM((2, 3, 8, 16, 256), F32),
-            pltpu.VMEM((2, 3, 8, 16, 256), F32),
-            pltpu.SemaphoreType.DMA((2, 2)),
+            pltpu.VMEM((3, 16, 16, 256), F32),
+            pltpu.VMEM((3, 16, 16, 256), F32),
+            pltpu.SemaphoreType.DMA((2, 3)),
         ],
         compiler_params=pltpu.CompilerParams(vmem_limit_bytes=12 * 2**20),
         cost_estimate=pl.CostEstimate(flops=4_000_000, bytes_accessed=4_000_000, transcendentals=0),

time: 35.9 us -> 35.8 us (level)
  transfers between devices with their start and end apart: 7 -> 7, of which waited for: 3 -> 3; matrix products, arithmetic and copies ran while one was open for 0% -> 0% of each run, Pallas kernels for 20% -> 19%
where the time goes in v5:
time: 35.8 us; the launch traced here: 35.6 us
  starting transfers between devices  20.2 us (56%)
  Pallas kernels  10.7 us (30%)
  waiting for transfers between devices  2.74 us (8%)
  local copies, waits for them, and re-layouts  1.19 us (3%)
  between operations  0.78 us (2%)
    all_to_all x1, starting transfers between devices, on_device(): lax.all_to_all(stress, 'az', split_axis=0, concat_axis=0, tiled=True)  9.96 us
    pallas_call x1, Pallas kernels, on_device(): call(inner_kernel, 'inner', [(Kept.planes, 24, 256), (8, 128), block, blo...  4.34 us
    ppermute x1, starting transfers between devices, on_device(): ring('ax', n_ax, -1)  3.53 us
    ppermute x1, starting transfers between devices, on_device(): from_right = ring('az', n_az, -1)(az_dn)  2.67 us
    ppermute x1, starting transfers between devices, on_device(): up = ring('ax', n_ax, 1)(up)  2.37 us
    pallas_call x1, Pallas kernels, seam_call(): pl.pallas_call(seam_kernel, out_shape=[out, out], in_specs=[VMEM] * len(a...  1.6 us
    ppermute x1, starting transfers between devices, on_device(): from_left = ring('az', n_az, 1)(az_up)  1.46 us
    pallas_call x1, Pallas kernels, send_call(): pl.pallas_call(send_kernel, out_shape=[jax.ShapeDtypeStruct(shape, F32) f...  1.37 us
  transfers between devices with their start and end apart: 7, of which 3 were waited for; matrix products, arithmetic and copies ran while one was open for 0% of the time, Pallas kernels for 19%

profile of v5, /device:TPU:8, one launch (start us, length us, event | category | flops | bytes accessed | tf_op | source)
XLA Modules:
  0.0 35.6 jit_solution(14944005826628196764)
XLA Ops:
  0.6 1.4 %send.1 = (f32[8,16,256]{2,1,0:T(8,128)S(1)}, f32[6,16,256]{2,1,0:T(8,128)S(1)}, f32[16,8,256]{2,1,0:T(8,128)S(1)}) custom-call(f32[3,16,16,256]{3,2,1,0:T(8,128)} %src.3, s32[16,16,256]{2,1,0:T(8,128)} %reg.3), custom_call_target="tpu_custom_call" | custom-call | tf_op jit(solution)/shard_map/send/pallas_call | solution.py:197
  2.0 0.1 collective-permute-start
  2.1 2.4 %collective-permute-start.1 = (f32[8,16,256]{2,1,0:T(8,128)S(1)}, f32[8,16,256]{2,1,0:T(8,128)S(1)}, u32[]{:S(2)}, u32[]{:S(2)}) collective-permute-start(f32[8,16,256]{2,1,0:T(8,128)S(1)} %get-tuple-element.23), channel_id=1, source_target_pairs={{0,2},{2,4},{4,6},{6,8},{8,10},{10,12},{12,14},{14,0},{1,3},{3,5},... | collective-permute-start | bytes 393224 | tf_op jit(solution)/shard_map/ppermute | solution.py:657
  4.5 0.0 collective-permute-done.sw
  4.5 3.5 %collective-permute-start.3 = (f32[7,16,256]{2,1,0:T(8,128)S(1)}, f32[7,16,256]{2,1,0:T(8,128)S(1)}, u32[]{:S(2)}, u32[]{:S(2)}) collective-permute-start(f32[7,16,256]{2,1,0:T(8,128)S(1)} %pad_maximum_fusion), channel_id=1, source_target_pairs={{0,14},{2,0},{4,2},{6,4},{8,6},{10,8},{12,10},{14,12},{1,15},{3,1}... | collective-permute-start | bytes 344072 | tf_op jit(solution)/shard_map/ppermute | solution.py:658
  8.1 4.3 %inner.1 = (f32[53,24,256]{2,1,0:T(8,128)S(1)}, f32[8,128]{1,0:T(8,128)S(1)}, f32[3,16,16,256]{3,2,1,0:T(8,128)}, f32[3,16,16,256]{3,2,1,0:T(8,128)}) custom-call(f32[3,16,16,256]{3,2,1,0:T(8,128)S(1)} %copy-done, s32[16,16,256]{2,1,0:T(8,128)S(1)} %copy-done.1, f32[16,8,256]{2,1,0:T(8,128)S(1)} %collective-permute-done.sw), custom_call_target="tpu_custom_call" | custom-call | flops 10000000 | bytes 2000000 | tf_op jit(solution)/shard_map/inner/pallas_call | solution.py:660
  12.4 0.0 copy-start.2
  12.4 0.0 copy-start.6
  12.5 0.1 collective-permute-start.2
  12.6 1.2 %collective-permute-done.2.sw = f32[8,8,256]{2,1,0:T(8,128)S(1)} collective-permute-done((f32[8,8,256]{2,1,0:T(8,128)S(1)}, f32[8,8,256]{2,1,0:T(8,128)S(1)}, u32[]{:S(2)}, u32[]{:S(2)}) %collective-permute-start.2) | collective-permute-done | bytes 65568 | tf_op jit(solution)/shard_map/ppermute | solution.py:678
  13.8 0.3 collective-permute-done.3.dn
  14.1 1.3 %rim.1 = (f32[16,8,384]{2,1,0:T(8,128)}, f32[2,24,128]{2,1,0:T(8,128)}, f32[2,24,128]{2,1,0:T(8,128)}, f32[27,24,256]{2,1,0:T(8,128)S(1)}) custom-call(f32[53,24,256]{2,1,0:T(8,128)S(1)} %get-tuple-element.22.kept, f32[8,16,256]{2,1,0:T(8,128)S(1)} %collective-permute-done.1.up, f32[8,8,256]{2,1,0:T(8,128)S(1)} %collective-permute-done.2.sw, ...), custom_call_target="tpu_custom_call" | custom-call | flops 10000000 | bytes 2000000 | tf_op jit(solution)/shard_map/rim/pallas_call | solution.py:679
  15.4 10.0 %all-to-all-start = ((f32[16,8,384]{2,1,0:T(8,128)}), f32[16,8,384]{2,1,0:T(8,128)S(1)}, u32[]{:S(2)}, u32[]{:S(2)}) async-start(f32[16,8,384]{2,1,0:T(8,128)} %get-tuple-element.37), calls=%async_computation | async-start | bytes 393216 | tf_op jit(solution)/shard_map/all_to_all | solution.py:694
  25.4 1.5 %collective-permute-start.4 = (f32[2,24,128]{2,1,0:T(8,128)}, f32[2,24,128]{2,1,0:T(8,128)S(1)}, u32[]{:S(2)}, u32[]{:S(2)}) collective-permute-start(f32[2,24,128]{2,1,0:T(8,128)} %get-tuple-element.33), channel_id=1, source_target_pairs={{0,16},{16,32},{32,48},{48,64},{64,80},{80,96},{96,112},{112,128},... | collective-permute-start | bytes 73736 | tf_op jit(solution)/shard_map/ppermute | solution.py:695
  26.8 2.7 %collective-permute-start.5 = (f32[2,24,128]{2,1,0:T(8,128)}, f32[2,24,128]{2,1,0:T(8,128)S(1)}, u32[]{:S(2)}, u32[]{:S(2)}) collective-permute-start(f32[2,24,128]{2,1,0:T(8,128)} %get-tuple-element.34), channel_id=1, source_target_pairs={{0,240},{16,0},{32,16},{48,32},{64,48},{80,64},{96,80},{112,96},{1... | collective-permute-start | bytes 73736 | tf_op jit(solution)/shard_map/ppermute | solution.py:696
  29.5 1.1 %copy-done.3 = f32[3,16,16,256]{3,2,1,0:T(8,128)S(1)} copy-done((f32[3,16,16,256]{3,2,1,0:T(8,128)S(1)}, f32[3,16,16,256]{3,2,1,0:T(8,128)}, u32[]{:S(2)}) %copy-start.3) | copy-done | bytes 786456
  30.7 0.9 %edge.1 = (f32[3,16,16,256]{3,2,1,0:T(8,128)S(1)}, f32[3,16,16,256]{3,2,1,0:T(8,128)S(1)}, f32[2,16,256]{2,1,0:T(8,128)S(1)}) custom-call(s32[16]{0:T(128)S(1)} %copy-done.6, f32[53,24,256]{2,1,0:T(8,128)S(1)} %get-tuple-element.22.kept, f32[27,24,256]{2,1,0:T(8,128)S(1)} %get-tuple-element.28.rim, f32[3,16,16,256]{3,2,1,0:T(8,128)S(1)} %copy-done.2, ...), custom_call_target="tpu_custom_call" | custom-call | flops 10000000 | bytes 2000000 | tf_op jit(solution)/shard_map/edge/pallas_call | solution.py:697
  31.6 0.0 copy-start.4
  31.6 0.0 copy-start.5
  31.6 1.2 %collective-permute-done.4.from_left = f32[2,24,128]{2,1,0:T(8,128)S(1)} collective-permute-done((f32[2,24,128]{2,1,0:T(8,128)}, f32[2,24,128]{2,1,0:T(8,128)S(1)}, u32[]{:S(2)}, u32[]{:S(2)}) %collective-permute-start.4) | collective-permute-done | bytes 24608 | tf_op jit(solution)/shard_map/ppermute | solution.py:695
  32.8 0.0 collective-permute-done.5.from_right
  32.8 1.6 %seams.1 = (f32[3,16,16,256]{3,2,1,0:T(8,128)}, f32[3,16,16,256]{3,2,1,0:T(8,128)}) custom-call(f32[27,24,256]{2,1,0:T(8,128)S(1)} %get-tuple-element.28.rim, f32[3,16,16,256]{3,2,1,0:T(8,128)S(1)} %get-tuple-element.31.sol_in, f32[3,16,16,256]{3,2,1,0:T(8,128)S(1)} %get-tuple-element.32.res_in, f32[2,24,128]{2,1,0:T(8,128)S(1)} %collective-permute-done.4.from_left, ...), custom_call_target="tpu_custom_call" | custom-call | flops 4000000 | bytes 4000000 | tf_op jit(solution)/shard_map/seams/pallas_call | solution.py:578
  34.4 0.0 all-to-all-done.block
  34.4 1.1 %harmonics.1 = f32[2,1,8,256]{3,2,1,0:T(8,128)} custom-call(f32[16,8,384]{2,1,0:T(8,128)S(1)} %all-to-all-done.block, bf16[256,512]{1,0:T(8,128)(2,1)S(1)} %copy-done.5, bf16[256,512]{1,0:T(8,128)(2,1)S(1)} %copy-done.4, f32[2,16,256]{2,1,0:T(8,128)S(1)} %get-tuple-element.38.table), custom_call_target="tpu_custom_call" | custom-call | flops 100000000 | bytes 1000000 | tf_op jit(solution)/shard_map/harmonics/pallas_call | solution.py:635
  (13 shorter events, 0.1 us)
Async XLA Ops:
  0.6 7.4 %copy-start.1 = (s32[16,16,256]{2,1,0:T(8,128)S(1)}, s32[16,16,256]{2,1,0:T(8,128)}, u32[]{:S(2)}) copy-start(s32[16,16,256]{2,1,0:T(8,128)} %reg.3) | copy-start | bytes 786436
  0.6 7.4 %copy-start = (f32[3,16,16,256]{3,2,1,0:T(8,128)S(1)}, f32[3,16,16,256]{3,2,1,0:T(8,128)}, u32[]{:S(2)}) copy-start(f32[3,16,16,256]{3,2,1,0:T(8,128)} %src.3) | copy-start | bytes 2359300
  2.0 2.5 %collective-permute-start = (f32[16,8,256]{2,1,0:T(8,128)S(1)}, f32[16,8,256]{2,1,0:T(8,128)S(1)}, u32[]{:S(2)}, u32[]{:S(2)}) collective-permute-start(f32[16,8,256]{2,1,0:T(8,128)S(1)} %get-tuple-element.21), channel_id=1, source_target_pairs={{0,1},{1,0},{2,3},{3,2},{4,5},{5,4},{6,7},{7,6},{8,9},{9,8},{10,11... | collective-permute-start | bytes 393224 | tf_op jit(solution)/shard_map/ppermute | solution.py:656
  2.1 10.3 %collective-permute-start.1 = (f32[8,16,256]{2,1,0:T(8,128)S(1)}, f32[8,16,256]{2,1,0:T(8,128)S(1)}, u32[]{:S(2)}, u32[]{:S(2)}) collective-permute-start(f32[8,16,256]{2,1,0:T(8,128)S(1)} %get-tuple-element.23), channel_id=1, source_target_pairs={{0,2},{2,4},{4,6},{6,8},{8,10},{10,12},{12,14},{14,0},{1,3},{3,5},... | collective-permute-start | bytes 393224 | tf_op jit(solution)/shard_map/ppermute | solution.py:657
  4.5 9.6 %collective-permute-start.3 = (f32[7,16,256]{2,1,0:T(8,128)S(1)}, f32[7,16,256]{2,1,0:T(8,128)S(1)}, u32[]{:S(2)}, u32[]{:S(2)}) collective-permute-start(f32[7,16,256]{2,1,0:T(8,128)S(1)} %pad_maximum_fusion), channel_id=1, source_target_pairs={{0,14},{2,0},{4,2},{6,4},{8,6},{10,8},{12,10},{14,12},{1,15},{3,1}... | collective-permute-start | bytes 344072 | tf_op jit(solution)/shard_map/ppermute | solution.py:658
  12.4 17.1 %copy-start.2 = (f32[3,16,16,256]{3,2,1,0:T(8,128)S(1)}, f32[3,16,16,256]{3,2,1,0:T(8,128)}, u32[]{:S(2)}) copy-start(f32[3,16,16,256]{3,2,1,0:T(8,128)} %get-tuple-element.29.sol_in) | copy-start | bytes 2359300
  12.4 17.1 %copy-start.6 = (s32[16]{0:T(128)S(1)}, s32[16]{0:T(128)}, u32[]{:S(2)}) copy-start(s32[16]{0:T(128)} %skew.1) | copy-start | bytes 196
  12.5 1.3 %collective-permute-start.2 = (f32[8,8,256]{2,1,0:T(8,128)S(1)}, f32[8,8,256]{2,1,0:T(8,128)S(1)}, u32[]{:S(2)}, u32[]{:S(2)}) collective-permute-start(f32[8,8,256]{2,1,0:T(8,128)S(1)} %constant_dynamic-slice_fusion), channel_id=1, source_target_pairs={{0,1},{1,0},{2,3},{3,2},{4,5},{5,4},{6,7},{7,6},{8,9},{9,8},{10,11... | collective-permute-start | bytes 196616 | tf_op jit(solution)/shard_map/ppermute | solution.py:678
  15.4 19.0 %all-to-all-start = ((f32[16,8,384]{2,1,0:T(8,128)}), f32[16,8,384]{2,1,0:T(8,128)S(1)}, u32[]{:S(2)}, u32[]{:S(2)}) async-start(f32[16,8,384]{2,1,0:T(8,128)} %get-tuple-element.37), calls=%async_computation | async-start | bytes 393216 | tf_op jit(solution)/shard_map/all_to_all | solution.py:694
  25.4 7.4 %collective-permute-start.4 = (f32[2,24,128]{2,1,0:T(8,128)}, f32[2,24,128]{2,1,0:T(8,128)S(1)}, u32[]{:S(2)}, u32[]{:S(2)}) collective-permute-start(f32[2,24,128]{2,1,0:T(8,128)} %get-tuple-element.33), channel_id=1, source_target_pairs={{0,16},{16,32},{32,48},{48,64},{64,80},{80,96},{96,112},{112,128},... | collective-permute-start | bytes 73736 | tf_op jit(solution)/shard_map/ppermute | solution.py:695
  26.8 5.9 %collective-permute-start.5 = (f32[2,24,128]{2,1,0:T(8,128)}, f32[2,24,128]{2,1,0:T(8,128)S(1)}, u32[]{:S(2)}, u32[]{:S(2)}) collective-permute-start(f32[2,24,128]{2,1,0:T(8,128)} %get-tuple-element.34), channel_id=1, source_target_pairs={{0,240},{16,0},{32,16},{48,32},{64,48},{80,64},{96,80},{112,96},{1... | collective-permute-start | bytes 73736 | tf_op jit(solution)/shard_map/ppermute | solution.py:696
  29.5 1.1 %copy-start.3 = (f32[3,16,16,256]{3,2,1,0:T(8,128)S(1)}, f32[3,16,16,256]{3,2,1,0:T(8,128)}, u32[]{:S(2)}) copy-start(f32[3,16,16,256]{3,2,1,0:T(8,128)} %get-tuple-element.30.res_in) | copy-start | bytes 2359300
  31.6 2.8 %copy-start.4 = (bf16[256,512]{1,0:T(8,128)(2,1)S(1)}, bf16[256,512]{1,0:T(8,128)(2,1)}, u32[]{:S(2)}) copy-start(bf16[256,512]{1,0:T(8,128)(2,1)} %constant.17.clone.basis_lo) | copy-start | bytes 786436
  31.6 2.8 %copy-start.5 = (bf16[256,512]{1,0:T(8,128)(2,1)S(1)}, bf16[256,512]{1,0:T(8,128)(2,1)}, u32[]{:S(2)}) copy-start(bf16[256,512]{1,0:T(8,128)(2,1)} %constant.16.clone.basis_hi) | copy-start | bytes 786436

commit v6 on v5

--- a/solution.py
+++ b/solution.py
@@ -327,7 +327,7 @@
         copy.wait()
 
 
-def rim_kernel(kept, up, sw, dn, _, hbm, az_up, az_dn, rim, w, out, up_msg, dn_msg, sem):
+def rim_kernel(kept, up, sw, dn, _, hbm, up_msg, dn_msg, rim, w, out, sem):
     core, ax = lax.axis_index("rad"), lax.axis_index("ax")
     lo = jnp.where(ax > 0, 1.0, 0.0)
     hi = jnp.where(ax < lax.axis_size("ax") - 1, 1.0, 0.0)
@@ -407,10 +407,6 @@
             k < 2, roll(x[2], -2, 1), jnp.where(k < 4, x[0], roll(x[1], 2, 1))
         )
         msg[1] = x[3]
-    copies.append(pltpu.make_async_copy(up_msg, az_up, sem.at[1]))
-    copies.append(pltpu.make_async_copy(dn_msg, az_dn, sem.at[2]))
-    copies[1].start()
-    copies[2].start()
 
     f = SECOND_A
 
@@ -476,8 +472,8 @@
         for n in range(5):
             extra = jnp.where(part == n, parts[n], extra)
         out[z, :, 256:384] = extra
-    copies.append(pltpu.make_async_copy(out.at[:, :, last], hbm.at[:, :, last], sem.at[3]))
-    copies[3].start()
+    copies.append(pltpu.make_async_copy(out.at[:, :, last], hbm.at[:, :, last], sem.at[1]))
+    copies[1].start()
     for copy in copies:
         copy.wait()
 
@@ -596,12 +592,12 @@
     seam = block[:, :, 256:384]
     right = jnp.concatenate([seam[1:], seam[:1]], axis=0).reshape(128, 128)
     first = 6 * (lax.axis_index("az") + 2)
-    right = pltpu.roll(right, lax.rem(256 - first - 18, 128), 1)
-    seam = pltpu.roll(seam.reshape(128, 128), lax.rem(256 - first, 128), 1)
+    right = pltpu.roll(right, lax.rem(254 - first - 18, 128), 1)
+    seam = pltpu.roll(seam.reshape(128, 128), lax.rem(254 - first, 128), 1)
     product = seam * right
     flux = seam + right + roll(product, -6, 1) + roll(product, -12, 1)
     square = 0.5 * (flux * flux)
-    fixed = roll(square - roll(square, -3, 1), -2, 1).reshape(16, 8, 128)
+    fixed = (square - roll(square, -3, 1)).reshape(16, 8, 128)
     moved = jnp.concatenate([fixed[15:], fixed[:15]], axis=0)
     low = jnp.where(lane == 0, moved, block[:, :, 0:128])
     high = jnp.where(lane >= 126, fixed, block[:, :, 128:256])
@@ -683,13 +679,11 @@
         [
             (4, 8, 24, 256),
             (16, 8, 384),
-            (2, 24, 128),
-            (2, 24, 128),
-            pltpu.SemaphoreType.DMA((4,)),
+            pltpu.SemaphoreType.DMA((2,)),
         ],
         8,
         [VMEM] * 4 + [pl.BlockSpec(memory_space=pl.ANY)],
-        [HBM, HBM, HBM, VMEM],
+        [HBM, VMEM, VMEM, VMEM],
     )(kept, up, sw_up, dn, flag)
     circle = lax.all_to_all(stress, "az", split_axis=0, concat_axis=0, tiled=True)
     from_left = ring("az", n_az, 1)(az_up)

time: 35.8 us -> 35.7 us (level)
  no operation moved by 1% of the time
where the time goes in v6:
time: 35.7 us; the launch traced here: 35.4 us
  starting transfers between devices  20.2 us (57%)
  Pallas kernels  10.6 us (30%)
  waiting for transfers between devices  2.67 us (7%)
  local copies, waits for them, and re-layouts  1.19 us (3%)
  between operations  0.78 us (2%)
    all_to_all x1, starting transfers between devices, on_device(): lax.all_to_all(stress, 'az', split_axis=0, concat_axis=0, tiled=True)  9.96 us
    pallas_call x1, Pallas kernels, on_device(): call(inner_kernel, 'inner', [(Kept.planes, 24, 256), (8, 128), block, blo...  4.34 us
    ppermute x1, starting transfers between devices, on_device(): ring('ax', n_ax, -1)  3.53 us
    ppermute x1, starting transfers between devices, on_device(): from_right = ring('az', n_az, -1)(az_dn)  2.67 us
    ppermute x1, starting transfers between devices, on_device(): up = ring('ax', n_ax, 1)(up)  2.37 us
    pallas_call x1, Pallas kernels, seam_call(): pl.pallas_call(seam_kernel, out_shape=[out, out], in_specs=[VMEM] * len(a...  1.6 us
    ppermute x1, starting transfers between devices, on_device(): from_left = ring('az', n_az, 1)(az_up)  1.46 us
    pallas_call x1, Pallas kernels, send_call(): pl.pallas_call(send_kernel, out_shape=[jax.ShapeDtypeStruct(shape, F32) f...  1.37 us
  transfers between devices with their start and end apart: 7, of which 3 were waited for; matrix products, arithmetic and copies ran while one was open for 0% of the time, Pallas kernels for 19%

profile of v6, /device:TPU:8, one launch (start us, length us, event | category | flops | bytes accessed | tf_op | source)
XLA Modules:
  0.0 35.4 jit_solution(3725704544008787507)
XLA Ops:
  0.6 1.4 %send.1 = (f32[8,16,256]{2,1,0:T(8,128)S(1)}, f32[6,16,256]{2,1,0:T(8,128)S(1)}, f32[16,8,256]{2,1,0:T(8,128)S(1)}) custom-call(f32[3,16,16,256]{3,2,1,0:T(8,128)} %src.3, s32[16,16,256]{2,1,0:T(8,128)} %reg.3), custom_call_target="tpu_custom_call" | custom-call | tf_op jit(solution)/shard_map/send/pallas_call | solution.py:197
  2.0 0.1 collective-permute-start
  2.1 2.4 %collective-permute-start.1 = (f32[8,16,256]{2,1,0:T(8,128)S(1)}, f32[8,16,256]{2,1,0:T(8,128)S(1)}, u32[]{:S(2)}, u32[]{:S(2)}) collective-permute-start(f32[8,16,256]{2,1,0:T(8,128)S(1)} %get-tuple-element.23), channel_id=1, source_target_pairs={{0,2},{2,4},{4,6},{6,8},{8,10},{10,12},{12,14},{14,0},{1,3},{3,5},... | collective-permute-start | bytes 393224 | tf_op jit(solution)/shard_map/ppermute | solution.py:653
  4.5 0.0 collective-permute-done.sw
  4.5 3.5 %collective-permute-start.3 = (f32[7,16,256]{2,1,0:T(8,128)S(1)}, f32[7,16,256]{2,1,0:T(8,128)S(1)}, u32[]{:S(2)}, u32[]{:S(2)}) collective-permute-start(f32[7,16,256]{2,1,0:T(8,128)S(1)} %pad_maximum_fusion), channel_id=1, source_target_pairs={{0,14},{2,0},{4,2},{6,4},{8,6},{10,8},{12,10},{14,12},{1,15},{3,1}... | collective-permute-start | bytes 344072 | tf_op jit(solution)/shard_map/ppermute | solution.py:654
  8.1 4.3 %inner.1 = (f32[53,24,256]{2,1,0:T(8,128)S(1)}, f32[8,128]{1,0:T(8,128)S(1)}, f32[3,16,16,256]{3,2,1,0:T(8,128)}, f32[3,16,16,256]{3,2,1,0:T(8,128)}) custom-call(f32[3,16,16,256]{3,2,1,0:T(8,128)S(1)} %copy-done, s32[16,16,256]{2,1,0:T(8,128)S(1)} %copy-done.1, f32[16,8,256]{2,1,0:T(8,128)S(1)} %collective-permute-done.sw), custom_call_target="tpu_custom_call" | custom-call | flops 10000000 | bytes 2000000 | tf_op jit(solution)/shard_map/inner/pallas_call | solution.py:656
  12.4 0.0 copy-start.2
  12.4 0.0 copy-start.6
  12.5 0.1 collective-permute-start.2
  12.6 1.2 %collective-permute-done.2.sw = f32[8,8,256]{2,1,0:T(8,128)S(1)} collective-permute-done((f32[8,8,256]{2,1,0:T(8,128)S(1)}, f32[8,8,256]{2,1,0:T(8,128)S(1)}, u32[]{:S(2)}, u32[]{:S(2)}) %collective-permute-start.2) | collective-permute-done | bytes 65568 | tf_op jit(solution)/shard_map/ppermute | solution.py:674
  13.8 0.3 collective-permute-done.3.dn
  14.1 1.3 %rim.1 = (f32[16,8,384]{2,1,0:T(8,128)}, f32[2,24,128]{2,1,0:T(8,128)S(1)}, f32[2,24,128]{2,1,0:T(8,128)S(1)}, f32[27,24,256]{2,1,0:T(8,128)S(1)}) custom-call(f32[53,24,256]{2,1,0:T(8,128)S(1)} %get-tuple-element.22.kept, f32[8,16,256]{2,1,0:T(8,128)S(1)} %collective-permute-done.1.up, f32[8,8,256]{2,1,0:T(8,128)S(1)} %collective-permute-done.2.sw, ...), custom_call_target="tpu_custom_call" | custom-call | flops 10000000 | bytes 2000000 | tf_op jit(solution)/shard_map/rim/pallas_call | solution.py:675
  15.4 10.0 %all-to-all-start = ((f32[16,8,384]{2,1,0:T(8,128)}), f32[16,8,384]{2,1,0:T(8,128)S(1)}, u32[]{:S(2)}, u32[]{:S(2)}) async-start(f32[16,8,384]{2,1,0:T(8,128)} %get-tuple-element.37), calls=%async_computation | async-start | bytes 393216 | tf_op jit(solution)/shard_map/all_to_all | solution.py:688
  25.4 1.5 %collective-permute-start.4 = (f32[2,24,128]{2,1,0:T(8,128)S(1)}, f32[2,24,128]{2,1,0:T(8,128)S(1)}, u32[]{:S(2)}, u32[]{:S(2)}) collective-permute-start(f32[2,24,128]{2,1,0:T(8,128)S(1)} %get-tuple-element.33), channel_id=1, source_target_pairs={{0,16},{16,32},{32,48},{48,64},{64,80},{80,96},{96,112},{112,128},... | collective-permute-start | bytes 73736 | tf_op jit(solution)/shard_map/ppermute | solution.py:689
  26.8 2.7 %collective-permute-start.5 = (f32[2,24,128]{2,1,0:T(8,128)S(1)}, f32[2,24,128]{2,1,0:T(8,128)S(1)}, u32[]{:S(2)}, u32[]{:S(2)}) collective-permute-start(f32[2,24,128]{2,1,0:T(8,128)S(1)} %get-tuple-element.34), channel_id=1, source_target_pairs={{0,240},{16,0},{32,16},{48,32},{64,48},{80,64},{96,80},{112,96},{1... | collective-permute-start | bytes 73736 | tf_op jit(solution)/shard_map/ppermute | solution.py:690
  29.5 1.1 %copy-done.3 = f32[3,16,16,256]{3,2,1,0:T(8,128)S(1)} copy-done((f32[3,16,16,256]{3,2,1,0:T(8,128)S(1)}, f32[3,16,16,256]{3,2,1,0:T(8,128)}, u32[]{:S(2)}) %copy-start.3) | copy-done | bytes 786456
  30.6 0.9 %edge.1 = (f32[3,16,16,256]{3,2,1,0:T(8,128)S(1)}, f32[3,16,16,256]{3,2,1,0:T(8,128)S(1)}, f32[2,16,256]{2,1,0:T(8,128)S(1)}) custom-call(s32[16]{0:T(128)S(1)} %copy-done.6, f32[53,24,256]{2,1,0:T(8,128)S(1)} %get-tuple-element.22.kept, f32[27,24,256]{2,1,0:T(8,128)S(1)} %get-tuple-element.28.rim, f32[3,16,16,256]{3,2,1,0:T(8,128)S(1)} %copy-done.2, ...), custom_call_target="tpu_custom_call" | custom-call | flops 10000000 | bytes 2000000 | tf_op jit(solution)/shard_map/edge/pallas_call | solution.py:691
  31.6 0.0 copy-start.4
  31.6 0.0 copy-start.5
  31.6 1.1 %collective-permute-done.4.from_left = f32[2,24,128]{2,1,0:T(8,128)S(1)} collective-permute-done((f32[2,24,128]{2,1,0:T(8,128)S(1)}, f32[2,24,128]{2,1,0:T(8,128)S(1)}, u32[]{:S(2)}, u32[]{:S(2)}) %collective-permute-start.4) | collective-permute-done | bytes 24608 | tf_op jit(solution)/shard_map/ppermute | solution.py:689
  32.7 0.0 collective-permute-done.5.from_right
  32.7 1.6 %seams.1 = (f32[3,16,16,256]{3,2,1,0:T(8,128)}, f32[3,16,16,256]{3,2,1,0:T(8,128)}) custom-call(f32[27,24,256]{2,1,0:T(8,128)S(1)} %get-tuple-element.28.rim, f32[3,16,16,256]{3,2,1,0:T(8,128)S(1)} %get-tuple-element.31.sol_in, f32[3,16,16,256]{3,2,1,0:T(8,128)S(1)} %get-tuple-element.32.res_in, f32[2,24,128]{2,1,0:T(8,128)S(1)} %collective-permute-done.4.from_left, ...), custom_call_target="tpu_custom_call" | custom-call | flops 4000000 | bytes 4000000 | tf_op jit(solution)/shard_map/seams/pallas_call | solution.py:574
  34.3 0.0 all-to-all-done.block
  34.3 1.1 %harmonics.1 = f32[2,1,8,256]{3,2,1,0:T(8,128)} custom-call(f32[16,8,384]{2,1,0:T(8,128)S(1)} %all-to-all-done.block, bf16[256,512]{1,0:T(8,128)(2,1)S(1)} %copy-done.5, bf16[256,512]{1,0:T(8,128)(2,1)S(1)} %copy-done.4, f32[2,16,256]{2,1,0:T(8,128)S(1)} %get-tuple-element.38.table), custom_call_target="tpu_custom_call" | custom-call | flops 100000000 | bytes 1000000 | tf_op jit(solution)/shard_map/harmonics/pallas_call | solution.py:631
  (13 shorter events, 0.1 us)
Async XLA Ops:
  0.6 7.4 %copy-start.1 = (s32[16,16,256]{2,1,0:T(8,128)S(1)}, s32[16,16,256]{2,1,0:T(8,128)}, u32[]{:S(2)}) copy-start(s32[16,16,256]{2,1,0:T(8,128)} %reg.3) | copy-start | bytes 786436
  0.6 7.4 %copy-start = (f32[3,16,16,256]{3,2,1,0:T(8,128)S(1)}, f32[3,16,16,256]{3,2,1,0:T(8,128)}, u32[]{:S(2)}) copy-start(f32[3,16,16,256]{3,2,1,0:T(8,128)} %src.3) | copy-start | bytes 2359300
  2.0 2.5 %collective-permute-start = (f32[16,8,256]{2,1,0:T(8,128)S(1)}, f32[16,8,256]{2,1,0:T(8,128)S(1)}, u32[]{:S(2)}, u32[]{:S(2)}) collective-permute-start(f32[16,8,256]{2,1,0:T(8,128)S(1)} %get-tuple-element.21), channel_id=1, source_target_pairs={{0,1},{1,0},{2,3},{3,2},{4,5},{5,4},{6,7},{7,6},{8,9},{9,8},{10,11... | collective-permute-start | bytes 393224 | tf_op jit(solution)/shard_map/ppermute | solution.py:652
  2.1 10.3 %collective-permute-start.1 = (f32[8,16,256]{2,1,0:T(8,128)S(1)}, f32[8,16,256]{2,1,0:T(8,128)S(1)}, u32[]{:S(2)}, u32[]{:S(2)}) collective-permute-start(f32[8,16,256]{2,1,0:T(8,128)S(1)} %get-tuple-element.23), channel_id=1, source_target_pairs={{0,2},{2,4},{4,6},{6,8},{8,10},{10,12},{12,14},{14,0},{1,3},{3,5},... | collective-permute-start | bytes 393224 | tf_op jit(solution)/shard_map/ppermute | solution.py:653
  4.5 9.6 %collective-permute-start.3 = (f32[7,16,256]{2,1,0:T(8,128)S(1)}, f32[7,16,256]{2,1,0:T(8,128)S(1)}, u32[]{:S(2)}, u32[]{:S(2)}) collective-permute-start(f32[7,16,256]{2,1,0:T(8,128)S(1)} %pad_maximum_fusion), channel_id=1, source_target_pairs={{0,14},{2,0},{4,2},{6,4},{8,6},{10,8},{12,10},{14,12},{1,15},{3,1}... | collective-permute-start | bytes 344072 | tf_op jit(solution)/shard_map/ppermute | solution.py:654
  12.4 17.1 %copy-start.2 = (f32[3,16,16,256]{3,2,1,0:T(8,128)S(1)}, f32[3,16,16,256]{3,2,1,0:T(8,128)}, u32[]{:S(2)}) copy-start(f32[3,16,16,256]{3,2,1,0:T(8,128)} %get-tuple-element.29.sol_in) | copy-start | bytes 2359300
  12.4 17.1 %copy-start.6 = (s32[16]{0:T(128)S(1)}, s32[16]{0:T(128)}, u32[]{:S(2)}) copy-start(s32[16]{0:T(128)} %skew.1) | copy-start | bytes 196
  12.5 1.3 %collective-permute-start.2 = (f32[8,8,256]{2,1,0:T(8,128)S(1)}, f32[8,8,256]{2,1,0:T(8,128)S(1)}, u32[]{:S(2)}, u32[]{:S(2)}) collective-permute-start(f32[8,8,256]{2,1,0:T(8,128)S(1)} %constant_dynamic-slice_fusion), channel_id=1, source_target_pairs={{0,1},{1,0},{2,3},{3,2},{4,5},{5,4},{6,7},{7,6},{8,9},{9,8},{10,11... | collective-permute-start | bytes 196616 | tf_op jit(solution)/shard_map/ppermute | solution.py:674
  15.4 18.9 %all-to-all-start = ((f32[16,8,384]{2,1,0:T(8,128)}), f32[16,8,384]{2,1,0:T(8,128)S(1)}, u32[]{:S(2)}, u32[]{:S(2)}) async-start(f32[16,8,384]{2,1,0:T(8,128)} %get-tuple-element.37), calls=%async_computation | async-start | bytes 393216 | tf_op jit(solution)/shard_map/all_to_all | solution.py:688
  25.4 7.3 %collective-permute-start.4 = (f32[2,24,128]{2,1,0:T(8,128)S(1)}, f32[2,24,128]{2,1,0:T(8,128)S(1)}, u32[]{:S(2)}, u32[]{:S(2)}) collective-permute-start(f32[2,24,128]{2,1,0:T(8,128)S(1)} %get-tuple-element.33), channel_id=1, source_target_pairs={{0,16},{16,32},{32,48},{48,64},{64,80},{80,96},{96,112},{112,128},... | collective-permute-start | bytes 73736 | tf_op jit(solution)/shard_map/ppermute | solution.py:689
  26.8 5.9 %collective-permute-start.5 = (f32[2,24,128]{2,1,0:T(8,128)S(1)}, f32[2,24,128]{2,1,0:T(8,128)S(1)}, u32[]{:S(2)}, u32[]{:S(2)}) collective-permute-start(f32[2,24,128]{2,1,0:T(8,128)S(1)} %get-tuple-element.34), channel_id=1, source_target_pairs={{0,240},{16,0},{32,16},{48,32},{64,48},{80,64},{96,80},{112,96},{1... | collective-permute-start | bytes 73736 | tf_op jit(solution)/shard_map/ppermute | solution.py:690
  29.5 1.1 %copy-start.3 = (f32[3,16,16,256]{3,2,1,0:T(8,128)S(1)}, f32[3,16,16,256]{3,2,1,0:T(8,128)}, u32[]{:S(2)}) copy-start(f32[3,16,16,256]{3,2,1,0:T(8,128)} %get-tuple-element.30.res_in) | copy-start | bytes 2359300
  31.6 2.8 %copy-start.4 = (bf16[256,512]{1,0:T(8,128)(2,1)S(1)}, bf16[256,512]{1,0:T(8,128)(2,1)}, u32[]{:S(2)}) copy-start(bf16[256,512]{1,0:T(8,128)(2,1)} %constant.17.clone.basis_lo) | copy-start | bytes 786436
  31.6 2.8 %copy-start.5 = (bf16[256,512]{1,0:T(8,128)(2,1)S(1)}, bf16[256,512]{1,0:T(8,128)(2,1)}, u32[]{:S(2)}) copy-start(bf16[256,512]{1,0:T(8,128)(2,1)} %constant.16.clone.basis_hi) | copy-start | bytes 786436

commit v7 on v5

--- a/solution.py
+++ b/solution.py
@@ -596,12 +596,12 @@
     seam = block[:, :, 256:384]
     right = jnp.concatenate([seam[1:], seam[:1]], axis=0).reshape(128, 128)
     first = 6 * (lax.axis_index("az") + 2)
-    right = pltpu.roll(right, lax.rem(256 - first - 18, 128), 1)
-    seam = pltpu.roll(seam.reshape(128, 128), lax.rem(256 - first, 128), 1)
+    right = pltpu.roll(right, lax.rem(254 - first - 18, 128), 1)
+    seam = pltpu.roll(seam.reshape(128, 128), lax.rem(254 - first, 128), 1)
     product = seam * right
     flux = seam + right + roll(product, -6, 1) + roll(product, -12, 1)
     square = 0.5 * (flux * flux)
-    fixed = roll(square - roll(square, -3, 1), -2, 1).reshape(16, 8, 128)
+    fixed = (square - roll(square, -3, 1)).reshape(16, 8, 128)
     moved = jnp.concatenate([fixed[15:], fixed[:15]], axis=0)
     low = jnp.where(lane == 0, moved, block[:, :, 0:128])
     high = jnp.where(lane >= 126, fixed, block[:, :, 128:256])

time: 35.8 us -> 35.7 us (level)
  no operation moved by 1% of the time
where the time goes in v7:
time: 35.7 us; the launch traced here: 35.5 us
  starting transfers between devices  20.2 us (57%)
  Pallas kernels  10.6 us (30%)
  waiting for transfers between devices  2.74 us (8%)
  local copies, waits for them, and re-layouts  1.19 us (3%)
  between operations  0.78 us (2%)
    all_to_all x1, starting transfers between devices, on_device(): lax.all_to_all(stress, 'az', split_axis=0, concat_axis=0, tiled=True)  9.96 us
    pallas_call x1, Pallas kernels, on_device(): call(inner_kernel, 'inner', [(Kept.planes, 24, 256), (8, 128), block, blo...  4.34 us
    ppermute x1, starting transfers between devices, on_device(): ring('ax', n_ax, -1)  3.53 us
    ppermute x1, starting transfers between devices, on_device(): from_right = ring('az', n_az, -1)(az_dn)  2.67 us
    ppermute x1, starting transfers between devices, on_device(): up = ring('ax', n_ax, 1)(up)  2.37 us
    pallas_call x1, Pallas kernels, seam_call(): pl.pallas_call(seam_kernel, out_shape=[out, out], in_specs=[VMEM] * len(a...  1.6 us
    ppermute x1, starting transfers between devices, on_device(): from_left = ring('az', n_az, 1)(az_up)  1.46 us
    pallas_call x1, Pallas kernels, send_call(): pl.pallas_call(send_kernel, out_shape=[jax.ShapeDtypeStruct(shape, F32) f...  1.37 us
  transfers between devices with their start and end apart: 7, of which 3 were waited for; matrix products, arithmetic and copies ran while one was open for 0% of the time, Pallas kernels for 19%

profile of v7, /device:TPU:8, one launch (start us, length us, event | category | flops | bytes accessed | tf_op | source)
XLA Modules:
  0.0 35.5 jit_solution(8982734575951968634)
XLA Ops:
  0.6 1.4 %send.1 = (f32[8,16,256]{2,1,0:T(8,128)S(1)}, f32[6,16,256]{2,1,0:T(8,128)S(1)}, f32[16,8,256]{2,1,0:T(8,128)S(1)}) custom-call(f32[3,16,16,256]{3,2,1,0:T(8,128)} %src.3, s32[16,16,256]{2,1,0:T(8,128)} %reg.3), custom_call_target="tpu_custom_call" | custom-call | tf_op jit(solution)/shard_map/send/pallas_call | solution.py:197
  2.0 0.1 collective-permute-start
  2.1 2.4 %collective-permute-start.1 = (f32[8,16,256]{2,1,0:T(8,128)S(1)}, f32[8,16,256]{2,1,0:T(8,128)S(1)}, u32[]{:S(2)}, u32[]{:S(2)}) collective-permute-start(f32[8,16,256]{2,1,0:T(8,128)S(1)} %get-tuple-element.23), channel_id=1, source_target_pairs={{0,2},{2,4},{4,6},{6,8},{8,10},{10,12},{12,14},{14,0},{1,3},{3,5},... | collective-permute-start | bytes 393224 | tf_op jit(solution)/shard_map/ppermute | solution.py:657
  4.5 0.0 collective-permute-done.sw
  4.5 3.5 %collective-permute-start.3 = (f32[7,16,256]{2,1,0:T(8,128)S(1)}, f32[7,16,256]{2,1,0:T(8,128)S(1)}, u32[]{:S(2)}, u32[]{:S(2)}) collective-permute-start(f32[7,16,256]{2,1,0:T(8,128)S(1)} %pad_maximum_fusion), channel_id=1, source_target_pairs={{0,14},{2,0},{4,2},{6,4},{8,6},{10,8},{12,10},{14,12},{1,15},{3,1}... | collective-permute-start | bytes 344072 | tf_op jit(solution)/shard_map/ppermute | solution.py:658
  8.1 4.3 %inner.1 = (f32[53,24,256]{2,1,0:T(8,128)S(1)}, f32[8,128]{1,0:T(8,128)S(1)}, f32[3,16,16,256]{3,2,1,0:T(8,128)}, f32[3,16,16,256]{3,2,1,0:T(8,128)}) custom-call(f32[3,16,16,256]{3,2,1,0:T(8,128)S(1)} %copy-done, s32[16,16,256]{2,1,0:T(8,128)S(1)} %copy-done.1, f32[16,8,256]{2,1,0:T(8,128)S(1)} %collective-permute-done.sw), custom_call_target="tpu_custom_call" | custom-call | flops 10000000 | bytes 2000000 | tf_op jit(solution)/shard_map/inner/pallas_call | solution.py:660
  12.4 0.0 copy-start.2
  12.4 0.0 copy-start.6
  12.5 0.1 collective-permute-start.2
  12.6 1.2 %collective-permute-done.2.sw = f32[8,8,256]{2,1,0:T(8,128)S(1)} collective-permute-done((f32[8,8,256]{2,1,0:T(8,128)S(1)}, f32[8,8,256]{2,1,0:T(8,128)S(1)}, u32[]{:S(2)}, u32[]{:S(2)}) %collective-permute-start.2) | collective-permute-done | bytes 65568 | tf_op jit(solution)/shard_map/ppermute | solution.py:678
  13.8 0.3 collective-permute-done.3.dn
  14.1 1.3 %rim.1 = (f32[16,8,384]{2,1,0:T(8,128)}, f32[2,24,128]{2,1,0:T(8,128)}, f32[2,24,128]{2,1,0:T(8,128)}, f32[27,24,256]{2,1,0:T(8,128)S(1)}) custom-call(f32[53,24,256]{2,1,0:T(8,128)S(1)} %get-tuple-element.22.kept, f32[8,16,256]{2,1,0:T(8,128)S(1)} %collective-permute-done.1.up, f32[8,8,256]{2,1,0:T(8,128)S(1)} %collective-permute-done.2.sw, ...), custom_call_target="tpu_custom_call" | custom-call | flops 10000000 | bytes 2000000 | tf_op jit(solution)/shard_map/rim/pallas_call | solution.py:679
  15.4 10.0 %all-to-all-start = ((f32[16,8,384]{2,1,0:T(8,128)}), f32[16,8,384]{2,1,0:T(8,128)S(1)}, u32[]{:S(2)}, u32[]{:S(2)}) async-start(f32[16,8,384]{2,1,0:T(8,128)} %get-tuple-element.37), calls=%async_computation | async-start | bytes 393216 | tf_op jit(solution)/shard_map/all_to_all | solution.py:694
  25.4 1.5 %collective-permute-start.4 = (f32[2,24,128]{2,1,0:T(8,128)}, f32[2,24,128]{2,1,0:T(8,128)S(1)}, u32[]{:S(2)}, u32[]{:S(2)}) collective-permute-start(f32[2,24,128]{2,1,0:T(8,128)} %get-tuple-element.33), channel_id=1, source_target_pairs={{0,16},{16,32},{32,48},{48,64},{64,80},{80,96},{96,112},{112,128},... | collective-permute-start | bytes 73736 | tf_op jit(solution)/shard_map/ppermute | solution.py:695
  26.8 2.7 %collective-permute-start.5 = (f32[2,24,128]{2,1,0:T(8,128)}, f32[2,24,128]{2,1,0:T(8,128)S(1)}, u32[]{:S(2)}, u32[]{:S(2)}) collective-permute-start(f32[2,24,128]{2,1,0:T(8,128)} %get-tuple-element.34), channel_id=1, source_target_pairs={{0,240},{16,0},{32,16},{48,32},{64,48},{80,64},{96,80},{112,96},{1... | collective-permute-start | bytes 73736 | tf_op jit(solution)/shard_map/ppermute | solution.py:696
  29.5 1.1 %copy-done.3 = f32[3,16,16,256]{3,2,1,0:T(8,128)S(1)} copy-done((f32[3,16,16,256]{3,2,1,0:T(8,128)S(1)}, f32[3,16,16,256]{3,2,1,0:T(8,128)}, u32[]{:S(2)}) %copy-start.3) | copy-done | bytes 786456
  30.7 0.9 %edge.1 = (f32[3,16,16,256]{3,2,1,0:T(8,128)S(1)}, f32[3,16,16,256]{3,2,1,0:T(8,128)S(1)}, f32[2,16,256]{2,1,0:T(8,128)S(1)}) custom-call(s32[16]{0:T(128)S(1)} %copy-done.6, f32[53,24,256]{2,1,0:T(8,128)S(1)} %get-tuple-element.22.kept, f32[27,24,256]{2,1,0:T(8,128)S(1)} %get-tuple-element.28.rim, f32[3,16,16,256]{3,2,1,0:T(8,128)S(1)} %copy-done.2, ...), custom_call_target="tpu_custom_call" | custom-call | flops 10000000 | bytes 2000000 | tf_op jit(solution)/shard_map/edge/pallas_call | solution.py:697
  31.6 0.0 copy-start.4
  31.6 0.0 copy-start.5
  31.6 1.2 %collective-permute-done.4.from_left = f32[2,24,128]{2,1,0:T(8,128)S(1)} collective-permute-done((f32[2,24,128]{2,1,0:T(8,128)}, f32[2,24,128]{2,1,0:T(8,128)S(1)}, u32[]{:S(2)}, u32[]{:S(2)}) %collective-permute-start.4) | collective-permute-done | bytes 24608 | tf_op jit(solution)/shard_map/ppermute | solution.py:695
  32.8 0.0 collective-permute-done.5.from_right
  32.8 1.6 %seams.1 = (f32[3,16,16,256]{3,2,1,0:T(8,128)}, f32[3,16,16,256]{3,2,1,0:T(8,128)}) custom-call(f32[27,24,256]{2,1,0:T(8,128)S(1)} %get-tuple-element.28.rim, f32[3,16,16,256]{3,2,1,0:T(8,128)S(1)} %get-tuple-element.31.sol_in, f32[3,16,16,256]{3,2,1,0:T(8,128)S(1)} %get-tuple-element.32.res_in, f32[2,24,128]{2,1,0:T(8,128)S(1)} %collective-permute-done.4.from_left, ...), custom_call_target="tpu_custom_call" | custom-call | flops 4000000 | bytes 4000000 | tf_op jit(solution)/shard_map/seams/pallas_call | solution.py:578
  34.4 0.0 all-to-all-done.block
  34.4 1.1 %harmonics.1 = f32[2,1,8,256]{3,2,1,0:T(8,128)} custom-call(f32[16,8,384]{2,1,0:T(8,128)S(1)} %all-to-all-done.block, bf16[256,512]{1,0:T(8,128)(2,1)S(1)} %copy-done.5, bf16[256,512]{1,0:T(8,128)(2,1)S(1)} %copy-done.4, f32[2,16,256]{2,1,0:T(8,128)S(1)} %get-tuple-element.38.table), custom_call_target="tpu_custom_call" | custom-call | flops 100000000 | bytes 1000000 | tf_op jit(solution)/shard_map/harmonics/pallas_call | solution.py:635
  (13 shorter events, 0.1 us)
Async XLA Ops:
  0.6 7.4 %copy-start.1 = (s32[16,16,256]{2,1,0:T(8,128)S(1)}, s32[16,16,256]{2,1,0:T(8,128)}, u32[]{:S(2)}) copy-start(s32[16,16,256]{2,1,0:T(8,128)} %reg.3) | copy-start | bytes 786436
  0.6 7.4 %copy-start = (f32[3,16,16,256]{3,2,1,0:T(8,128)S(1)}, f32[3,16,16,256]{3,2,1,0:T(8,128)}, u32[]{:S(2)}) copy-start(f32[3,16,16,256]{3,2,1,0:T(8,128)} %src.3) | copy-start | bytes 2359300
  2.0 2.5 %collective-permute-start = (f32[16,8,256]{2,1,0:T(8,128)S(1)}, f32[16,8,256]{2,1,0:T(8,128)S(1)}, u32[]{:S(2)}, u32[]{:S(2)}) collective-permute-start(f32[16,8,256]{2,1,0:T(8,128)S(1)} %get-tuple-element.21), channel_id=1, source_target_pairs={{0,1},{1,0},{2,3},{3,2},{4,5},{5,4},{6,7},{7,6},{8,9},{9,8},{10,11... | collective-permute-start | bytes 393224 | tf_op jit(solution)/shard_map/ppermute | solution.py:656
  2.1 10.3 %collective-permute-start.1 = (f32[8,16,256]{2,1,0:T(8,128)S(1)}, f32[8,16,256]{2,1,0:T(8,128)S(1)}, u32[]{:S(2)}, u32[]{:S(2)}) collective-permute-start(f32[8,16,256]{2,1,0:T(8,128)S(1)} %get-tuple-element.23), channel_id=1, source_target_pairs={{0,2},{2,4},{4,6},{6,8},{8,10},{10,12},{12,14},{14,0},{1,3},{3,5},... | collective-permute-start | bytes 393224 | tf_op jit(solution)/shard_map/ppermute | solution.py:657
  4.5 9.6 %collective-permute-start.3 = (f32[7,16,256]{2,1,0:T(8,128)S(1)}, f32[7,16,256]{2,1,0:T(8,128)S(1)}, u32[]{:S(2)}, u32[]{:S(2)}) collective-permute-start(f32[7,16,256]{2,1,0:T(8,128)S(1)} %pad_maximum_fusion), channel_id=1, source_target_pairs={{0,14},{2,0},{4,2},{6,4},{8,6},{10,8},{12,10},{14,12},{1,15},{3,1}... | collective-permute-start | bytes 344072 | tf_op jit(solution)/shard_map/ppermute | solution.py:658
  12.4 17.1 %copy-start.2 = (f32[3,16,16,256]{3,2,1,0:T(8,128)S(1)}, f32[3,16,16,256]{3,2,1,0:T(8,128)}, u32[]{:S(2)}) copy-start(f32[3,16,16,256]{3,2,1,0:T(8,128)} %get-tuple-element.29.sol_in) | copy-start | bytes 2359300
  12.4 17.1 %copy-start.6 = (s32[16]{0:T(128)S(1)}, s32[16]{0:T(128)}, u32[]{:S(2)}) copy-start(s32[16]{0:T(128)} %skew.1) | copy-start | bytes 196
  12.5 1.3 %collective-permute-start.2 = (f32[8,8,256]{2,1,0:T(8,128)S(1)}, f32[8,8,256]{2,1,0:T(8,128)S(1)}, u32[]{:S(2)}, u32[]{:S(2)}) collective-permute-start(f32[8,8,256]{2,1,0:T(8,128)S(1)} %constant_dynamic-slice_fusion), channel_id=1, source_target_pairs={{0,1},{1,0},{2,3},{3,2},{4,5},{5,4},{6,7},{7,6},{8,9},{9,8},{10,11... | collective-permute-start | bytes 196616 | tf_op jit(solution)/shard_map/ppermute | solution.py:678
  15.4 19.0 %all-to-all-start = ((f32[16,8,384]{2,1,0:T(8,128)}), f32[16,8,384]{2,1,0:T(8,128)S(1)}, u32[]{:S(2)}, u32[]{:S(2)}) async-start(f32[16,8,384]{2,1,0:T(8,128)} %get-tuple-element.37), calls=%async_computation | async-start | bytes 393216 | tf_op jit(solution)/shard_map/all_to_all | solution.py:694
  25.4 7.4 %collective-permute-start.4 = (f32[2,24,128]{2,1,0:T(8,128)}, f32[2,24,128]{2,1,0:T(8,128)S(1)}, u32[]{:S(2)}, u32[]{:S(2)}) collective-permute-start(f32[2,24,128]{2,1,0:T(8,128)} %get-tuple-element.33), channel_id=1, source_target_pairs={{0,16},{16,32},{32,48},{48,64},{64,80},{80,96},{96,112},{112,128},... | collective-permute-start | bytes 73736 | tf_op jit(solution)/shard_map/ppermute | solution.py:695
  26.8 5.9 %collective-permute-start.5 = (f32[2,24,128]{2,1,0:T(8,128)}, f32[2,24,128]{2,1,0:T(8,128)S(1)}, u32[]{:S(2)}, u32[]{:S(2)}) collective-permute-start(f32[2,24,128]{2,1,0:T(8,128)} %get-tuple-element.34), channel_id=1, source_target_pairs={{0,240},{16,0},{32,16},{48,32},{64,48},{80,64},{96,80},{112,96},{1... | collective-permute-start | bytes 73736 | tf_op jit(solution)/shard_map/ppermute | solution.py:696
  29.5 1.1 %copy-start.3 = (f32[3,16,16,256]{3,2,1,0:T(8,128)S(1)}, f32[3,16,16,256]{3,2,1,0:T(8,128)}, u32[]{:S(2)}) copy-start(f32[3,16,16,256]{3,2,1,0:T(8,128)} %get-tuple-element.30.res_in) | copy-start | bytes 2359300
  31.6 2.8 %copy-start.4 = (bf16[256,512]{1,0:T(8,128)(2,1)S(1)}, bf16[256,512]{1,0:T(8,128)(2,1)}, u32[]{:S(2)}) copy-start(bf16[256,512]{1,0:T(8,128)(2,1)} %constant.17.clone.basis_lo) | copy-start | bytes 786436
  31.6 2.8 %copy-start.5 = (bf16[256,512]{1,0:T(8,128)(2,1)S(1)}, bf16[256,512]{1,0:T(8,128)(2,1)}, u32[]{:S(2)}) copy-start(bf16[256,512]{1,0:T(8,128)(2,1)} %constant.16.clone.basis_hi) | copy-start | bytes 786436
